TPU v7x, 256 devices: a whole 4x4x8 slice. The times are simulated.
256 devices in a mesh: clip: 8 (over x_lo, y), group: 32 (over x_hi, z, core).
Axes of the slice: x: 4 (x_hi: 2, x_lo: 2; x = x_hi * 2 + x_lo), y: 4, z: 8, core: 2. Of those that a mesh axis runs over, the one named last changes fastest.
Arguments:
- latents: bfloat16 [512, 640, 640], P(('clip', 'group')), may hold values from -8 to 8
- timestep: int32 [1], replicated, may hold values from 0 to 999
- context_frame: int32 [256], P(('clip', 'group')), may hold values from 0 to 1
- gain_pre: float32 [640], replicated, may hold values from 0.5 to 1.5
- w_temporal: bfloat16 [3, 640, 640], replicated, may hold values from -0.125 to 0.125
- w_time: float32 [640, 640], replicated, may hold values from -0.25 to 0.25
- gain_mid: float32 [640], replicated, may hold values from 0.5 to 1.5
- w_query: bfloat16 [640, 640], replicated, may hold values from -2 to 2
- w_key: bfloat16 [640, 640], replicated, may hold values from -2 to 2
- w_value: bfloat16 [640, 640], replicated, may hold values from -0.25 to 0.25
- w_out: bfloat16 [640, 640], replicated, may hold values from -1 to 1
Outputs:
- block_out: bfloat16 [512, 640, 640], P(('clip', 'group'))
All inputs are finite; a program needn't handle non-finite values.
Results may differ from a plain program's by a relative error of at most 0.035.
Values may be sent and summed in bfloat16 or wider, within the bound.
No kernel may reach another device: no remote copies, remote signals or barrier semaphores. Data moves between devices by JAX's collectives and lax.ppermute only.
A program may use at most 128 MiB of HBM per device.

v0:
```python
import math

import jax
import jax.numpy as jnp
from jax import lax
from jax.sharding import PartitionSpec as P

HEAD_DIM = 64
PH = 32
PW = 20


def padded_2(shard, sides, width):
    for axis, dim in sides:
        size, length = (lax.axis_size(axis), shard.shape[dim])
        up = [(i, (i + 1) % size) for i in range(size)]
        down = [(j, i) for i, j in up]
        last = lax.slice_in_dim(shard, length - width, length, axis=dim)
        first = lax.slice_in_dim(shard, 0, width, axis=dim)
        before = lax.ppermute(last, axis, up)
        after = lax.ppermute(first, axis, down)
        shard = jnp.concatenate([before, shard, after], axis=dim)
    return shard


def normalize(values, gain):
    return values * lax.rsqrt(jnp.mean(values * values, -1, keepdims=True) + 1e-06) * gain


def time_bias(timestep, w_time):
    half = w_time.shape[0] // 2
    freqs = jnp.exp(-math.log(10000.0) * jnp.arange(half, dtype=jnp.float32) / half)
    angle = timestep.astype(jnp.float32)[0] * freqs
    embed = jnp.concatenate([jnp.cos(angle), jnp.sin(angle)])
    return jnp.dot(
        jax.nn.silu(embed)[None, :],
        w_time,
        precision=lax.Precision.HIGHEST,
        preferred_element_type=jnp.float32,
    )[0]


def shards(
    latents,
    timestep,
    context_frame,
    gain_pre,
    w_temporal,
    w_time,
    gain_mid,
    w_query,
    w_key,
    w_value,
    w_out,
):
    frames, pixels, width = latents.shape
    heads = width // HEAD_DIM
    source = latents.astype(jnp.float32)
    norm1 = normalize(source, gain_pre).astype(jnp.bfloat16)
    padded = padded_2(norm1, ((("clip", "group"), 0),), 1)
    conv = jnp.zeros((frames * pixels, width), jnp.float32)
    for offset in range(3):
        window = padded[offset : offset + frames].reshape(frames * pixels, width)
        conv = conv + jnp.dot(window, w_temporal[offset], preferred_element_type=jnp.float32)
    temb = time_bias(timestep, w_time)
    hidden = (source + conv.reshape(frames, pixels, width) + temb).astype(jnp.bfloat16)
    norm2 = normalize(hidden.astype(jnp.float32), gain_mid).astype(jnp.bfloat16)
    chosen = lax.dynamic_index_in_dim(norm2, context_frame[0], 0, keepdims=False)
    regions = chosen.astype(jnp.float32).reshape(2, PH // 2, 2, PW // 2, width)
    pooled = jnp.mean(regions, axis=(1, 3)).reshape(4, width)
    ctx = normalize(pooled, 1.0).astype(jnp.bfloat16)
    keys = jnp.dot(ctx, w_key, preferred_element_type=jnp.float32).astype(jnp.bfloat16)
    values = jnp.dot(ctx, w_value, preferred_element_type=jnp.float32).astype(jnp.bfloat16)
    all_keys, all_values = (
        lax.all_gather(keys, ("clip", "group"), axis=0, tiled=True),
        lax.all_gather(values, ("clip", "group"), axis=0, tiled=True),
    )
    key_heads = all_keys.reshape(-1, heads, HEAD_DIM)
    value_heads = all_values.reshape(-1, heads, HEAD_DIM)

    def one_frame(pair):
        frame_hidden, frame_norm = pair
        queries = jnp.dot(frame_norm, w_query, preferred_element_type=jnp.float32).astype(
            jnp.bfloat16
        )
        query_heads = queries.reshape(pixels, heads, HEAD_DIM)
        scores = (
            jnp.einsum("qhd,rhd->qhr", query_heads, key_heads, preferred_element_type=jnp.float32)
            * 0.125
        )
        peak = jnp.max(scores, -1, keepdims=True)
        weights = jnp.exp(scores - peak)
        total = jnp.sum(weights, -1)
        summed = jnp.einsum(
            "qhr,rhd->qhd",
            weights.astype(jnp.bfloat16),
            value_heads,
            preferred_element_type=jnp.float32,
        )
        attended = (summed / total[..., None]).reshape(pixels, width).astype(jnp.bfloat16)
        mixed = frame_hidden.astype(jnp.float32) + jnp.dot(
            attended, w_out, preferred_element_type=jnp.float32
        )
        return mixed.astype(jnp.bfloat16)

    return lax.map(one_frame, (hidden, norm2))


def solution(mesh):
    return jax.shard_map(
        shards,
        mesh=mesh,
        in_specs=(
            P(("clip", "group"), None, None),
            P(),
            P(("clip", "group")),
            P(),
            P(),
            P(),
            P(),
            P(),
            P(),
            P(),
            P(),
        ),
        out_specs=P(("clip", "group"), None, None),
        check_vma=False,
    )
```

profile of v0, /device:TPU:1, one launch (start us, length us, event | category | flops | bytes accessed | tf_op | source)
XLA Modules:
  0.0 938.9 jit_solution(3607186713353595645)
XLA Ops:
  6.5 2.0 fusion.19
  9.1 1.4 fusion.37
  10.7 3.0 collective-permute-start
  15.5 0.9 convolution_reduce_fusion
  16.9 2.7 fusion.28
  19.7 3.7 collective-permute-done
  23.4 2.8 collective-permute-done.1
  26.2 1.7 pad_maximum_fusion.1
  27.9 1.6 fusion.26
  29.5 1.6 fusion.15
  33.0 1.2 copy-done.7
  34.3 1.7 reshape.87
  35.9 2.0 reduce_sum.49
  38.2 0.9 fusion.25
  40.2 404.3 %all-gather.7.cloned.1.call-done = bf16[256,4,640]{2,1,0:T(4,128)(2,1)} async-done(((bf16[1,4,640]{2,1,0:T(4,128)(2,1)}), bf16[256,4,640]{2,1,0:T(4,128)(2,1)}) %all-gather.7.cloned.1.call-update) | async-done | bytes 1310736 | tf_op jit(solution)/shard_map/all_gather | solution.py:76
  444.6 5.9 reshape.85
  450.5 5.1 copy.19
  455.5 391.3 %all-gather.5.cloned.1.call-done = bf16[256,4,640]{2,1,0:T(4,128)(2,1)} async-done(((bf16[1,4,640]{2,1,0:T(4,128)(2,1)}), bf16[256,4,640]{2,1,0:T(4,128)(2,1)}) %all-gather.5.cloned.1.call-update) | async-done | bytes 1310736 | tf_op jit(solution)/shard_map/all_gather | solution.py:75
  846.8 5.9 reshape.84
  852.8 4.3 copy.18
  857.1 73.6 %while.10 = (s32[]{:T(128)}, bf16[2,640,640]{2,1,0:T(8,128)(2,1)}, bf16[2,640,640]{2,1,0:T(8,128)(2,1)S(1)}, bf16[2,640,640]{2,1,0:T(8,128)(2,1)}, bf16[640,640]...) while((s32[]{:T(128)}, bf16[2,640,640]{2,1,0:T(8,128)(2,1)}, ...), condition=%wide.region_7.8_spmd, body=%wide.region_4.7_spmd.sunk | while | flops 2781171200 | bytes 97286296 | solution.py:106
  857.1 2.3 convolution_convert_fusion.4
  859.4 10.6 %bitcast_reduce_fusion.2 = (f32[640,10]{0,1:T(8,128)S(1)}, f32[10,640,1024]{2,1,0:T(8,128)}) fusion(bf16[640,10,64]{0,2,1:T(8,128)(2,1)S(1)} %bitcast.93, bf16[1024,10,64]{0,2,1:T(8,128)(2,1)S(1)} %get-tuple-element.182), kind=kOutput, calls=%fused_computation.1.clone.1 | convolution fusion | flops 851961600 | bytes 28369920 | tf_op jit(solution)/shard_map/while/body/eval_jaxpr/qhd,rhd->qhr/dot_general | solution.py:88
  870.0 11.0 %fusion.70 = f32[640,10]{0,1:T(8,128)S(1)} fusion(f32[10,640,1024]{2,1,0:T(8,128)} %get-tuple-element.157, f32[640,10]{0,1:T(8,128)S(1)} %get-tuple-element.158), kind=kLoop, calls=%fused_computation.3.clone.1 | loop fusion | flops 19654400 | bytes 26265600 | tf_op jit(solution)/shard_map/while/body/eval_jaxpr/reduce_sum | solution.py:93
  881.0 11.0 %fusion.71 = bf16[640,10,64]{0,2,1:T(8,128)(2,1)S(1)} fusion(bf16[1024,10,64]{0,2,1:T(8,128)(2,1)S(1)} %copy-done.8, f32[10,640,1024]{2,1,0:T(8,128)} %get-tuple-element.157, f32[640,10]{0,1:T(8,128)S(1)} %get-tuple-element.158, f32[640,10]{0,1:T(8,128)S(1)} %fusion.70), kind=kOutput, calls=%fused_computation.9.clone.1 | convolution fusion | flops 859340800 | bytes 28395520 | tf_op jit(solution)/shard_map/while/body/eval_jaxpr/qhr,rhd->qhd/dot_general | solution.py:94
  892.1 1.8 fusion.72
  893.9 2.3 convolution_convert_fusion.4
  896.2 10.6 %bitcast_reduce_fusion.2 = (f32[640,10]{0,1:T(8,128)S(1)}, f32[10,640,1024]{2,1,0:T(8,128)}) fusion(bf16[640,10,64]{0,2,1:T(8,128)(2,1)S(1)} %bitcast.93, bf16[1024,10,64]{0,2,1:T(8,128)(2,1)S(1)} %get-tuple-element.182), kind=kOutput, calls=%fused_computation.1.clone.1 | convolution fusion | flops 851961600 | bytes 28369920 | tf_op jit(solution)/shard_map/while/body/eval_jaxpr/qhd,rhd->qhr/dot_general | solution.py:88
  906.8 11.0 %fusion.70 = f32[640,10]{0,1:T(8,128)S(1)} fusion(f32[10,640,1024]{2,1,0:T(8,128)} %get-tuple-element.157, f32[640,10]{0,1:T(8,128)S(1)} %get-tuple-element.158), kind=kLoop, calls=%fused_computation.3.clone.1 | loop fusion | flops 19654400 | bytes 26265600 | tf_op jit(solution)/shard_map/while/body/eval_jaxpr/reduce_sum | solution.py:93
  917.8 11.0 %fusion.71 = bf16[640,10,64]{0,2,1:T(8,128)(2,1)S(1)} fusion(bf16[1024,10,64]{0,2,1:T(8,128)(2,1)S(1)} %copy-done.8, f32[10,640,1024]{2,1,0:T(8,128)} %get-tuple-element.157, f32[640,10]{0,1:T(8,128)S(1)} %get-tuple-element.158, f32[640,10]{0,1:T(8,128)S(1)} %fusion.70), kind=kOutput, calls=%fused_computation.9.clone.1 | convolution fusion | flops 859340800 | bytes 28395520 | tf_op jit(solution)/shard_map/while/body/eval_jaxpr/qhr,rhd->qhd/dot_general | solution.py:94
  928.9 1.8 fusion.72
  930.7 1.4 copy-done.1
  (52 shorter events, 5.0 us)
Async XLA Ops:
  6.5 8.9 copy-start
  6.5 2.0 copy-start.2
  6.5 2.0 copy-start.12
  6.5 438.0 %all-gather.7.cloned.1.call-start = ((), (), s32[]{:S(2)}) async-start(), calls=%async_computation.1 | async-start | bytes 1315840 | tf_op jit(solution)/shard_map/all_gather | solution.py:76
  9.0 1.7 copy-start.3
  10.7 12.6 %collective-permute-start = (bf16[1,640,640]{2,1,0:T(8,128)(2,1)}, bf16[1,640,640]{2,1,0:T(8,128)(2,1)}, u32[]{:S(2)}, u32[]{:S(2)}) collective-permute-start(bf16[1,640,640]{2,1,0:T(8,128)(2,1)} %get-tuple-element.102), channel_id=1, source_target_pairs={{0,1},{1,2},{2,3},{3,4},{4,5},{5,6},{6,7},{7,8},{8,9},{9,10},{10,1... | collective-permute-start | bytes 2457608 | tf_op jit(solution)/shard_map/ppermute | solution.py:20
  13.8 12.4 %collective-permute-start.1 = (bf16[1,640,640]{2,1,0:T(8,128)(2,1)}, bf16[1,640,640]{2,1,0:T(8,128)(2,1)}, u32[]{:S(2)}, u32[]{:S(2)}) collective-permute-start(bf16[1,640,640]{2,1,0:T(8,128)(2,1)} %get-tuple-element.103), channel_id=1, source_target_pairs={{1,0},{2,1},{3,2},{4,3},{5,4},{6,5},{7,6},{8,7},{9,8},{10,9},{11,1... | collective-permute-start | bytes 2457608 | tf_op jit(solution)/shard_map/ppermute | solution.py:21
  15.5 1.4 copy-start.4
  19.6 8.2 copy-start.11
  31.1 0.7 copy-start.13
  31.8 1.2 copy-start.5
  33.0 1.2 copy-start.7
  35.9 2.3 copy-start.9
  35.9 3.4 copy-start.10
  39.1 807.8 %all-gather.5.cloned.1.call-start = ((), (), s32[]{:S(2)}) async-start(), calls=%async_computation | async-start | bytes 1315840 | tf_op jit(solution)/shard_map/all_gather | solution.py:75
  852.7 4.3 copy-start.6
  870.0 11.0 %copy-start.8 = (bf16[1024,10,64]{0,2,1:T(8,128)(2,1)S(1)}, bf16[1024,10,64]{0,2,1:T(8,128)(2,1)}, u32[]{:S(2)}) copy-start(bf16[1024,10,64]{0,2,1:T(8,128)(2,1)} %get-tuple-element.183) | copy-start | bytes 3932164 | tf_op jit(solution)/shard_map/while
  881.0 11.0 %copy-start.14 = (bf16[640,640]{1,0:T(8,128)(2,1)S(1)}, bf16[640,640]{1,0:T(8,128)(2,1)}, u32[]{:S(2)}) copy-start(bf16[640,640]{1,0:T(8,128)(2,1)} %get-tuple-element.184) | copy-start | bytes 2457604 | tf_op jit(solution)/shard_map/while
  906.8 11.0 %copy-start.8 = (bf16[1024,10,64]{0,2,1:T(8,128)(2,1)S(1)}, bf16[1024,10,64]{0,2,1:T(8,128)(2,1)}, u32[]{:S(2)}) copy-start(bf16[1024,10,64]{0,2,1:T(8,128)(2,1)} %get-tuple-element.183) | copy-start | bytes 3932164 | tf_op jit(solution)/shard_map/while
  917.8 11.0 %copy-start.14 = (bf16[640,640]{1,0:T(8,128)(2,1)S(1)}, bf16[640,640]{1,0:T(8,128)(2,1)}, u32[]{:S(2)}) copy-start(bf16[640,640]{1,0:T(8,128)(2,1)} %get-tuple-element.184) | copy-start | bytes 2457604 | tf_op jit(solution)/shard_map/while
  930.7 1.4 copy-start.1
Sparse Core Ops, SparseCore 0:
  39.2 405.3 all-gather.6
  446.4 400.3 all-gather.4
where the time goes:
time: 940 us; the launch traced here: 939 us
  waiting for transfers between devices  802 us (85%)
  matrix products  60 us (6%)
  other arithmetic  29.7 us (3%)
  local copies, waits for them, and re-layouts  28.6 us (3%)
  between operations  14.9 us (2%)
    all_gather x1, waiting for transfers between devices, shards(): lax.all_gather(values, ('clip', 'group'), axis=0, tiled=True)  404 us
    all_gather x1, waiting for transfers between devices, shards(): lax.all_gather(keys, ('clip', 'group'), axis=0, tiled=True)  391 us
    dot_general x2, matrix products, one_frame(): jnp.einsum('qhr,rhd->qhd', weights.astype(jnp.bfloat16), value_heads, pre...  22 us
    reduce_sum x2, other arithmetic, one_frame(): total = jnp.sum(weights, -1)  22 us
    dot_general x2, matrix products, one_frame(): jnp.einsum('qhd,rhd->qhr', query_heads, key_heads, preferred_element_type...  21.2 us
  transfers between devices with their start and end apart: 4, of which 4 were waited for; matrix products, arithmetic and copies ran while one was open for 2% of the time, Pallas kernels for 0%

commit v1 on v0

--- a/solution.py
+++ b/solution.py
@@ -21,6 +21,38 @@
         after = lax.ppermute(first, axis, down)
         shard = jnp.concatenate([before, shard, after], axis=dim)
     return shard
+
+
+AXES = ("clip", "group")
+
+
+def place(device):
+    clip, group = divmod(device, 32)
+    x_low, y = divmod(clip, 4)
+    x_high, rest = divmod(group, 16)
+    z, core = divmod(rest, 2)
+    return x_high * 2 + x_low, y, z, core
+
+
+def groups_by(key):
+    found = {}
+    for device in range(256):
+        found.setdefault(key(*place(device)), []).append(device)
+    return list(found.values())
+
+
+def spread(rows, groups):
+    count = len(groups[0])
+    copies = jnp.broadcast_to(rows[None], (count,) + rows.shape)
+    got = lax.all_to_all(copies, AXES, 0, 0, axis_index_groups=groups, tiled=False)
+    return got.reshape(count * rows.shape[0], rows.shape[1])
+
+
+def gather_rows(rows):
+    rows = spread(rows, groups_by(lambda x, y, z, core: (x, y, core)))
+    rows = spread(rows, groups_by(lambda x, y, z, core: (z, core)))
+    other = lax.ppermute(rows, AXES, [(i, i ^ 1) for i in range(256)])
+    return jnp.concatenate([rows, other], axis=0)
 
 
 def normalize(values, gain):
@@ -69,12 +101,9 @@
     regions = chosen.astype(jnp.float32).reshape(2, PH // 2, 2, PW // 2, width)
     pooled = jnp.mean(regions, axis=(1, 3)).reshape(4, width)
     ctx = normalize(pooled, 1.0).astype(jnp.bfloat16)
-    keys = jnp.dot(ctx, w_key, preferred_element_type=jnp.float32).astype(jnp.bfloat16)
-    values = jnp.dot(ctx, w_value, preferred_element_type=jnp.float32).astype(jnp.bfloat16)
-    all_keys, all_values = (
-        lax.all_gather(keys, ("clip", "group"), axis=0, tiled=True),
-        lax.all_gather(values, ("clip", "group"), axis=0, tiled=True),
-    )
+    all_ctx = gather_rows(ctx)
+    all_keys = jnp.dot(all_ctx, w_key, preferred_element_type=jnp.float32).astype(jnp.bfloat16)
+    all_values = jnp.dot(all_ctx, w_value, preferred_element_type=jnp.float32).astype(jnp.bfloat16)
     key_heads = all_keys.reshape(-1, heads, HEAD_DIM)
     value_heads = all_values.reshape(-1, heads, HEAD_DIM)
 

time: 940 us -> 152 us (0.16)
  waiting for transfers between devices: 802 us -> 8.21 us
  blocking collectives: 0 us -> 35.4 us
  local copies, waits for them, and re-layouts: 28.6 us -> 8.31 us
  between operations: 14.9 us -> 1.51 us
    all_gather x2 -> x0, waiting for transfers between devices: 796 us -> none  [the longest x1 404 us: shards(): lax.all_gather(values, ('clip', 'group'), axis=0, tiled=True)]
    all_to_all x0 -> x2, blocking collectives: none -> 35.4 us  [spread(): lax.all_to_all(copies, AXES, 0, 0, axis_index_groups=groups, tiled=False)]
    reshape x2 -> x0, local copies, waits for them, and re-layouts: 11.8 us -> none  [the longest x1 5.9 us: shards(): value_heads = all_values.reshape(-1, heads, HEAD_DIM)]
  transfers between devices with their start and end apart: 4 -> 3, of which waited for: 4 -> 3; matrix products, arithmetic and copies ran while one was open for 2% -> 3% of each run, Pallas kernels for 0% -> 0%
where the time goes in v1:
time: 152 us; the launch traced here: 151 us
  matrix products  63.4 us (42%)
  blocking collectives  35.4 us (23%)
  other arithmetic  29.6 us (19%)
  local copies, waits for them, and re-layouts  8.31 us (5%)
  waiting for transfers between devices  8.21 us (5%)
  starting transfers between devices  4.59 us (3%)
    all_to_all x2, blocking collectives, spread(): lax.all_to_all(copies, AXES, 0, 0, axis_index_groups=groups, tiled=False)  35.4 us
    dot_general x2, matrix products, one_frame(): jnp.einsum('qhr,rhd->qhd', weights.astype(jnp.bfloat16), value_heads, pre...  22 us
    reduce_sum x2, other arithmetic, one_frame(): total = jnp.sum(weights, -1)  22 us
    dot_general x2, matrix products, one_frame(): jnp.einsum('qhd,rhd->qhr', query_heads, key_heads, preferred_element_type...  21.1 us
    dot_general x3, matrix products, shards(): jnp.dot(window, w_temporal[offset], preferred_element_type=jnp.float32)  6.17 us
    unnamed x30, local copies, waits for them, and re-layouts  5.01 us
    dot_general x2, matrix products, one_frame(): jnp.dot(frame_norm, w_query, preferred_element_type=jnp.float32)  4.67 us
    ppermute x1, waiting for transfers between devices, padded_2(): before = lax.ppermute(last, axis, up)  3.72 us
  transfers between devices with their start and end apart: 3, of which 3 were waited for; matrix products, arithmetic and copies ran while one was open for 3% of the time, Pallas kernels for 0%

profile of v1, /device:TPU:1, one launch (start us, length us, event | category | flops | bytes accessed | tf_op | source)
XLA Modules:
  0.0 151.1 jit_solution(7360042732160444357)
XLA Ops:
  0.0 2.0 %fusion.19 = f32[2,640]{1,0:T(2,128)S(1)} fusion(bf16[2,640,640]{2,1,0:T(8,128)(2,1)} %param.13), kind=kLoop, calls=%fused_computation.27 | loop fusion | flops 2456320 | bytes 1643520 | tf_op jit(solution)/shard_map/reduce_sum | solution.py:59
  2.5 1.4 fusion.37
  4.2 3.0 %collective-permute-start = (bf16[1,640,640]{2,1,0:T(8,128)(2,1)}, bf16[1,640,640]{2,1,0:T(8,128)(2,1)}, u32[]{:S(2)}, u32[]{:S(2)}) collective-permute-start(bf16[1,640,640]{2,1,0:T(8,128)(2,1)} %get-tuple-element.70), channel_id=1, source_target_pairs={{0,1},{1,2},{2,3},{3,4},{4,5},{5,6},{6,7},{7,8},{8,9},{9,10},{10,1... | collective-permute-start | bytes 2457608 | tf_op jit(solution)/shard_map/ppermute | solution.py:20
  8.9 0.9 convolution_reduce_fusion
  10.4 2.7 %fusion.26 = f32[1280,640]{1,0:T(8,128)S(1)} fusion(bf16[1280,640]{1,0:T(8,128)(2,1)S(1)} %bitcast.94, bf16[3,640,640]{2,1,0:T(8,128)(2,1)} %param.17), kind=kOutput, calls=%fused_computation.40 | convolution fusion | flops 1048576000 | bytes 5734400 | tf_op jit(solution)/shard_map/dot_general | solution.py:96
  13.1 3.7 %collective-permute-done = bf16[1,640,640]{2,1,0:T(8,128)(2,1)} collective-permute-done((bf16[1,640,640]{2,1,0:T(8,128)(2,1)}, bf16[1,640,640]{2,1,0:T(8,128)(2,1)}, u32[]{:S(2)}, u32[]{:S(2)}) %collective-permute-start) | collective-permute-done | bytes 819232 | tf_op jit(solution)/shard_map/ppermute | solution.py:20
  16.8 2.8 %collective-permute-done.1 = bf16[1,640,640]{2,1,0:T(8,128)(2,1)} collective-permute-done((bf16[1,640,640]{2,1,0:T(8,128)(2,1)}, bf16[1,640,640]{2,1,0:T(8,128)(2,1)}, u32[]{:S(2)}, u32[]{:S(2)}) %collective-permute-start.1) | collective-permute-done | bytes 819232 | tf_op jit(solution)/shard_map/ppermute | solution.py:21
  19.6 1.7 %pad_maximum_fusion.1 = (bf16[2,640,640]{2,1,0:T(8,128)(2,1)S(1)}, bf16[2,640,640]{2,1,0:T(8,128)(2,1)S(1)}) fusion(bf16[2,640,640]{2,1,0:T(8,128)(2,1)S(1)} %copy-done.4, bf16[1,640,640]{2,1,0:T(8,128)(2,1)} %collective-permute-done, bf16[1,640,640]{2,1,0:T(8,128)(2,1)} %collective-permute-done.1), kind=kLoop, calls=%fused_computation.33 | loop fusion | flops 1638400 | bytes 6553600 | tf_op jit(solution)/shard_map/concatenate | solution.py:22
  21.4 1.6 %fusion.24 = f32[1280,640]{1,0:T(8,128)S(1)} fusion(bf16[1280,640]{1,0:T(8,128)(2,1)S(1)} %bitcast.97, bf16[3,640,640]{2,1,0:T(8,128)(2,1)S(1)} %copy-done.9), kind=kOutput, calls=%fused_computation.38 | convolution fusion | flops 1048576000 | bytes 5734400 | tf_op jit(solution)/shard_map/dot_general | solution.py:96
  23.0 1.8 %fusion.15 = f32[1280,640]{1,0:T(8,128)S(1)} fusion(f32[1280,640]{1,0:T(8,128)S(1)} %fusion.24, f32[1280,640]{1,0:T(8,128)S(1)} %fusion.26, bf16[1280,640]{1,0:T(8,128)(2,1)S(1)} %bitcast.96, bf16[3,640,640]{2,1,0:T(8,128)(2,1)S(1)} %copy-done.9), kind=kOutput, calls=%fused_computation.23 | convolution fusion | flops 1050214400 | bytes 12288000 | tf_op jit(solution)/shard_map/dot_general | solution.py:96
  26.7 1.2 copy-done.7
  28.0 1.6 %reshape.110 = f32[2,16,2,10,640]{4,3,2,1,0:T(8,128)} reshape(f32[1,640,640]{2,1,0:T(8,128)S(1)} %dynamic-slice_convert_fusion) | data formatting | bytes 3276800 | tf_op jit(solution)/shard_map/convert_element_type | solution.py:101
  29.6 1.9 %reduce_sum.49 = f32[2,2,640]{2,1,0:T(2,128)S(1)} reduce(f32[2,16,2,10,640]{4,3,2,1,0:T(8,128)} %reshape.110, f32[]{:T(128)} %constant.40.clone.1), dimensions={1,3}, to_apply=%region_2.3 | reduce | flops 407040 | bytes 1648644 | tf_op jit(solution)/shard_map/reduce_sum | solution.py:102
  31.9 14.9 %all_to_all.10 = bf16[8,4,640]{2,1,0:T(4,128)(2,1)S(1)} all-to-all(bf16[8,4,640]{2,1,0:T(4,128)(2,1)S(1)} %broadcast_in_dim.12), channel_id=1, replica_groups={{0,2,4,6,8,10,12,14},{1,3,5,7,9,11,13,15},{16,18,20,22,24,26,28,30},{17..., dimensions={0} | all-to-all | bytes 81920 | tf_op jit(solution)/shard_map/all_to_all | solution.py:47
  46.8 20.5 %all_to_all.11 = bf16[16,32,640]{2,1,0:T(8,128)(2,1)S(1)} all-to-all(bf16[16,32,640]{2,1,0:T(8,128)(2,1)S(1)} %broadcast_in_dim.14), channel_id=1, replica_groups={{0,16,32,48,64,80,96,112,128,144,160,176,192,208,224,240},{1,17,33,49,6..., dimensions={0} | all-to-all | bytes 1310720 | tf_op jit(solution)/shard_map/all_to_all | solution.py:47
  67.3 1.3 collective-permute-start.2
  68.6 1.7 %collective-permute-done.2 = bf16[512,640]{1,0:T(8,128)(2,1)S(1)} collective-permute-done((bf16[512,640]{1,0:T(8,128)(2,1)S(1)}, bf16[512,640]{1,0:T(8,128)(2,1)S(1)}, u32[]{:S(2)}, u32[]{:S(2)}) %collective-permute-start.2) | collective-permute-done | bytes 655392 | tf_op jit(solution)/shard_map/ppermute | solution.py:54
  70.4 0.8 copy-done.15
  71.2 2.3 %convolution_convert_fusion.1 = bf16[1024,640]{0,1:T(8,128)(2,1)} fusion(bf16[640,640]{1,0:T(8,128)(2,1)S(1)} %copy-done.12, bf16[512,640]{1,0:T(8,128)(2,1)S(1)} %collective-permute-done.2, bf16[512,640]{1,0:T(8,128)(2,1)S(1)} %bitcast.99), kind=kOutput, calls=%fused_computation.34 | convolution fusion | flops 842137600 | bytes 3440640 | tf_op jit(solution)/shard_map/dot_general | solution.py:106
  73.5 2.7 %convolution_convert_fusion.2 = bf16[1024,640]{0,1:T(8,128)(2,1)S(1)} fusion(bf16[640,640]{1,0:T(8,128)(2,1)S(1)} %copy-done.13, bf16[512,640]{1,0:T(8,128)(2,1)} %copy-done.15, bf16[512,640]{1,0:T(8,128)(2,1)} %bitcast.100), kind=kOutput, calls=%fused_computation.35 | convolution fusion | flops 842137600 | bytes 3440640 | tf_op jit(solution)/shard_map/dot_general | solution.py:105
  76.2 73.5 %while.10 = (s32[]{:T(128)}, bf16[2,640,640]{2,1,0:T(8,128)(2,1)}, bf16[2,640,640]{2,1,0:T(8,128)(2,1)S(1)}, bf16[2,640,640]{2,1,0:T(8,128)(2,1)}, bf16[640,640]...) while((s32[]{:T(128)}, bf16[2,640,640]{2,1,0:T(8,128)(2,1)}, ...), condition=%wide.region_7.8_spmd, body=%wide.region_4.7_spmd.sunk | while | flops 2781171200 | bytes 97286296 | solution.py:135
  76.2 2.3 %convolution_convert_fusion.4 = bf16[640,640]{0,1:T(8,128)(2,1)S(1)} fusion(bf16[640,640]{1,0:T(8,128)(2,1)} %get-tuple-element.149, bf16[2,640,640]{2,1,0:T(8,128)(2,1)} %get-tuple-element.148, s32[]{:T(128)} %get-tuple-element.136), kind=kOutput, calls=%fused_computation.10.clone.1 | convolution fusion | flops 524697600 | bytes 2458112 | tf_op jit(solution)/shard_map/while/body/eval_jaxpr/dot_general | solution.py:112
  78.5 10.6 %bitcast_reduce_fusion.2 = (f32[640,10]{0,1:T(8,128)S(1)}, f32[10,640,1024]{2,1,0:T(8,128)}) fusion(bf16[640,10,64]{0,2,1:T(8,128)(2,1)S(1)} %bitcast.93, bf16[1024,10,64]{0,2,1:T(8,128)(2,1)S(1)} %get-tuple-element.150), kind=kOutput, calls=%fused_computation.1.clone.1 | convolution fusion | flops 851961600 | bytes 28369920 | tf_op jit(solution)/shard_map/while/body/eval_jaxpr/qhd,rhd->qhr/dot_general | solution.py:117
  89.1 11.0 %fusion.70 = f32[640,10]{0,1:T(8,128)S(1)} fusion(f32[10,640,1024]{2,1,0:T(8,128)} %get-tuple-element.125, f32[640,10]{0,1:T(8,128)S(1)} %get-tuple-element.126), kind=kLoop, calls=%fused_computation.3.clone.1 | loop fusion | flops 19654400 | bytes 26265600 | tf_op jit(solution)/shard_map/while/body/eval_jaxpr/reduce_sum | solution.py:122
  100.1 11.0 %fusion.71 = bf16[640,10,64]{0,2,1:T(8,128)(2,1)S(1)} fusion(bf16[1024,10,64]{0,2,1:T(8,128)(2,1)S(1)} %copy-done.16, f32[10,640,1024]{2,1,0:T(8,128)} %get-tuple-element.125, f32[640,10]{0,1:T(8,128)S(1)} %get-tuple-element.126, f32[640,10]{0,1:T(8,128)S(1)} %fusion.70), kind=kOutput, calls=%fused_computation.9.clone.1 | convolution fusion | flops 859340800 | bytes 28395520 | tf_op jit(solution)/shard_map/while/body/eval_jaxpr/qhr,rhd->qhd/dot_general | solution.py:123
  111.1 1.8 %fusion.72 = bf16[2,640,640]{2,1,0:T(8,128)(2,1)} fusion(bf16[2,640,640]{2,1,0:T(8,128)(2,1)} %get-tuple-element.137, s32[]{:T(128)} %get-tuple-element.136, bf16[640,640]{0,1:T(8,128)(2,1)S(1)} %bitcast.102, bf16[640,640]{1,0:T(8,128)(2,1)S(1)} %copy-done.14, bf16[2,640,640]{2,1,0:T(8,128)(2,1)S(1)} %get-tuple-element.147), kind=kOutput, calls=%fused_computation.12.clone.1 | convolution fusion | flops 525516800 | bytes 3277312 | tf_op jit(solution)/shard_map/while/body/eval_jaxpr/dot_general | solution.py:130
  112.9 2.3 %convolution_convert_fusion.4 = bf16[640,640]{0,1:T(8,128)(2,1)S(1)} fusion(bf16[640,640]{1,0:T(8,128)(2,1)} %get-tuple-element.149, bf16[2,640,640]{2,1,0:T(8,128)(2,1)} %get-tuple-element.148, s32[]{:T(128)} %get-tuple-element.136), kind=kOutput, calls=%fused_computation.10.clone.1 | convolution fusion | flops 524697600 | bytes 2458112 | tf_op jit(solution)/shard_map/while/body/eval_jaxpr/dot_general | solution.py:112
  115.3 10.6 %bitcast_reduce_fusion.2 = (f32[640,10]{0,1:T(8,128)S(1)}, f32[10,640,1024]{2,1,0:T(8,128)}) fusion(bf16[640,10,64]{0,2,1:T(8,128)(2,1)S(1)} %bitcast.93, bf16[1024,10,64]{0,2,1:T(8,128)(2,1)S(1)} %get-tuple-element.150), kind=kOutput, calls=%fused_computation.1.clone.1 | convolution fusion | flops 851961600 | bytes 28369920 | tf_op jit(solution)/shard_map/while/body/eval_jaxpr/qhd,rhd->qhr/dot_general | solution.py:117
  125.9 11.0 %fusion.70 = f32[640,10]{0,1:T(8,128)S(1)} fusion(f32[10,640,1024]{2,1,0:T(8,128)} %get-tuple-element.125, f32[640,10]{0,1:T(8,128)S(1)} %get-tuple-element.126), kind=kLoop, calls=%fused_computation.3.clone.1 | loop fusion | flops 19654400 | bytes 26265600 | tf_op jit(solution)/shard_map/while/body/eval_jaxpr/reduce_sum | solution.py:122
  136.9 11.0 %fusion.71 = bf16[640,10,64]{0,2,1:T(8,128)(2,1)S(1)} fusion(bf16[1024,10,64]{0,2,1:T(8,128)(2,1)S(1)} %copy-done.16, f32[10,640,1024]{2,1,0:T(8,128)} %get-tuple-element.125, f32[640,10]{0,1:T(8,128)S(1)} %get-tuple-element.126, f32[640,10]{0,1:T(8,128)S(1)} %fusion.70), kind=kOutput, calls=%fused_computation.9.clone.1 | convolution fusion | flops 859340800 | bytes 28395520 | tf_op jit(solution)/shard_map/while/body/eval_jaxpr/qhr,rhd->qhd/dot_general | solution.py:123
  147.9 1.8 %fusion.72 = bf16[2,640,640]{2,1,0:T(8,128)(2,1)} fusion(bf16[2,640,640]{2,1,0:T(8,128)(2,1)} %get-tuple-element.137, s32[]{:T(128)} %get-tuple-element.136, bf16[640,640]{0,1:T(8,128)(2,1)S(1)} %bitcast.102, bf16[640,640]{1,0:T(8,128)(2,1)S(1)} %copy-done.14, bf16[2,640,640]{2,1,0:T(8,128)(2,1)S(1)} %get-tuple-element.147), kind=kOutput, calls=%fused_computation.12.clone.1 | convolution fusion | flops 525516800 | bytes 3277312 | tf_op jit(solution)/shard_map/while/body/eval_jaxpr/dot_general | solution.py:130
  149.7 1.4 copy-done.1
  (54 shorter events, 4.0 us)
Async XLA Ops:
  0.0 8.9 %copy-start = (f32[640,640]{1,0:T(8,128)S(1)}, f32[640,640]{1,0:T(8,128)}, u32[]{:S(2)}) copy-start(f32[640,640]{1,0:T(8,128)} %param.18) | copy-start | bytes 4915204
  0.0 2.0 %copy-start.2 = (bf16[2,640,640]{2,1,0:T(8,128)(2,1)S(1)}, bf16[2,640,640]{2,1,0:T(8,128)(2,1)}, u32[]{:S(2)}) copy-start(bf16[2,640,640]{2,1,0:T(8,128)(2,1)} %param.13) | copy-start | bytes 4915204
  0.0 2.0 %copy-start.10 = (f32[640]{0:T(1024)S(1)}, f32[640]{0:T(1024)}, u32[]{:S(2)}) copy-start(f32[640]{0:T(1024)} %param.16) | copy-start | bytes 7684
  2.5 1.7 %copy-start.3 = (bf16[2,640,640]{2,1,0:T(8,128)(2,1)}, bf16[2,640,640]{2,1,0:T(8,128)(2,1)S(1)}, u32[]{:S(2)}) copy-start(bf16[2,640,640]{2,1,0:T(8,128)(2,1)S(1)} %fusion.21) | copy-start | bytes 4915204
  4.2 12.6 %collective-permute-start = (bf16[1,640,640]{2,1,0:T(8,128)(2,1)}, bf16[1,640,640]{2,1,0:T(8,128)(2,1)}, u32[]{:S(2)}, u32[]{:S(2)}) collective-permute-start(bf16[1,640,640]{2,1,0:T(8,128)(2,1)} %get-tuple-element.70), channel_id=1, source_target_pairs={{0,1},{1,2},{2,3},{3,4},{4,5},{5,6},{6,7},{7,8},{8,9},{9,10},{10,1... | collective-permute-start | bytes 2457608 | tf_op jit(solution)/shard_map/ppermute | solution.py:20
  7.2 12.4 %collective-permute-start.1 = (bf16[1,640,640]{2,1,0:T(8,128)(2,1)}, bf16[1,640,640]{2,1,0:T(8,128)(2,1)}, u32[]{:S(2)}, u32[]{:S(2)}) collective-permute-start(bf16[1,640,640]{2,1,0:T(8,128)(2,1)} %get-tuple-element.71), channel_id=1, source_target_pairs={{1,0},{2,1},{3,2},{4,3},{5,4},{6,5},{7,6},{8,7},{9,8},{10,9},{11,1... | collective-permute-start | bytes 2457608 | tf_op jit(solution)/shard_map/ppermute | solution.py:21
  8.9 1.4 copy-start.4
  13.1 8.2 %copy-start.9 = (bf16[3,640,640]{2,1,0:T(8,128)(2,1)S(1)}, bf16[3,640,640]{2,1,0:T(8,128)(2,1)}, u32[]{:S(2)}) copy-start(bf16[3,640,640]{2,1,0:T(8,128)(2,1)} %param.17) | copy-start | bytes 7372804
  24.8 0.7 copy-start.11
  25.5 1.2 copy-start.5
  26.7 1.2 copy-start.7
  31.5 39.7 %copy-start.12 = (bf16[640,640]{1,0:T(8,128)(2,1)S(1)}, bf16[640,640]{1,0:T(8,128)(2,1)}, u32[]{:S(2)}) copy-start(bf16[640,640]{1,0:T(8,128)(2,1)} %param.22) | copy-start | bytes 2457604
  67.3 3.1 %copy-start.8 = (bf16[16,32,640]{2,1,0:T(8,128)(2,1)}, bf16[16,32,640]{2,1,0:T(8,128)(2,1)S(1)}, u32[]{:S(2)}) copy-start(bf16[16,32,640]{2,1,0:T(8,128)(2,1)S(1)} %all_to_all.11) | copy-start | bytes 1966084
  67.3 3.1 %collective-permute-start.2 = (bf16[512,640]{1,0:T(8,128)(2,1)S(1)}, bf16[512,640]{1,0:T(8,128)(2,1)S(1)}, u32[]{:S(2)}, u32[]{:S(2)}) collective-permute-start(bf16[512,640]{1,0:T(8,128)(2,1)S(1)} %bitcast.98), channel_id=1, source_target_pairs={{0,1},{1,0},{2,3},{3,2},{4,5},{5,4},{6,7},{7,6},{8,9},{9,8},{10,11... | collective-permute-start | bytes 1966088 | tf_op jit(solution)/shard_map/ppermute | solution.py:54
  68.6 4.9 %copy-start.13 = (bf16[640,640]{1,0:T(8,128)(2,1)S(1)}, bf16[640,640]{1,0:T(8,128)(2,1)}, u32[]{:S(2)}) copy-start(bf16[640,640]{1,0:T(8,128)(2,1)} %param.21) | copy-start | bytes 2457604
  70.4 0.8 copy-start.15
  73.5 2.7 %copy-start.6 = (bf16[2,640,640]{2,1,0:T(8,128)(2,1)S(1)}, bf16[2,640,640]{2,1,0:T(8,128)(2,1)}, u32[]{:S(2)}) copy-start(bf16[2,640,640]{2,1,0:T(8,128)(2,1)} %copy-done.5) | copy-start | bytes 4915204
  89.1 11.0 %copy-start.16 = (bf16[1024,10,64]{0,2,1:T(8,128)(2,1)S(1)}, bf16[1024,10,64]{0,2,1:T(8,128)(2,1)}, u32[]{:S(2)}) copy-start(bf16[1024,10,64]{0,2,1:T(8,128)(2,1)} %get-tuple-element.151) | copy-start | bytes 3932164 | tf_op jit(solution)/shard_map/while
  100.1 11.0 %copy-start.14 = (bf16[640,640]{1,0:T(8,128)(2,1)S(1)}, bf16[640,640]{1,0:T(8,128)(2,1)}, u32[]{:S(2)}) copy-start(bf16[640,640]{1,0:T(8,128)(2,1)} %get-tuple-element.152) | copy-start | bytes 2457604 | tf_op jit(solution)/shard_map/while
  125.9 11.0 %copy-start.16 = (bf16[1024,10,64]{0,2,1:T(8,128)(2,1)S(1)}, bf16[1024,10,64]{0,2,1:T(8,128)(2,1)}, u32[]{:S(2)}) copy-start(bf16[1024,10,64]{0,2,1:T(8,128)(2,1)} %get-tuple-element.151) | copy-start | bytes 3932164 | tf_op jit(solution)/shard_map/while
  136.9 11.0 %copy-start.14 = (bf16[640,640]{1,0:T(8,128)(2,1)S(1)}, bf16[640,640]{1,0:T(8,128)(2,1)}, u32[]{:S(2)}) copy-start(bf16[640,640]{1,0:T(8,128)(2,1)} %get-tuple-element.152) | copy-start | bytes 2457604 | tf_op jit(solution)/shard_map/while
  149.7 1.4 copy-start.1

commit v2 on v1

v2 whole, which is shorter than its diff:
```python
import math

import jax
import jax.numpy as jnp
import numpy as np
from jax import lax
from jax.experimental import pallas as pl
from jax.experimental.pallas import tpu as pltpu
from jax.sharding import PartitionSpec as P

HEAD_DIM = 64
PH = 32
PW = 20
PIX = PH * PW
C = 640
PAIRS = C // (2 * HEAD_DIM)
ROWS = 1024
CHUNK = 256
AXES = ("clip", "group")
VMEM = 56 * 2**20
SCALE = math.log2(math.e) / math.sqrt(HEAD_DIM)
LOW, HIGH = 2.0**-100, 2.0**110


def place(device):
    clip, group = divmod(device, 32)
    x_low, y = divmod(clip, 4)
    x_high, rest = divmod(group, 16)
    z, core = divmod(rest, 2)
    return x_high * 2 + x_low, y, z, core


def groups_by(key):
    found = {}
    for device in range(256):
        found.setdefault(key(*place(device)), []).append(device)
    return list(found.values())


def exchange(copies, groups):
    return lax.all_to_all(copies, AXES, 0, 0, axis_index_groups=groups, tiled=False)


def dot(a, b):
    return jnp.dot(a, b, preferred_element_type=jnp.float32)


def normalize(values, gain):
    return values * lax.rsqrt(jnp.mean(values * values, -1, keepdims=True) + 1e-06) * gain


def time_bias(timestep, w_time):
    half = w_time.shape[0] // 2
    freqs = jnp.exp(-math.log(10000.0) * jnp.arange(half, dtype=jnp.float32) / half)
    angle = timestep.astype(jnp.float32)[0] * freqs
    embed = jnp.concatenate([jnp.cos(angle), jnp.sin(angle)])
    return jnp.dot(
        jax.nn.silu(embed)[None, :],
        w_time,
        precision=lax.Precision.HIGHEST,
        preferred_element_type=jnp.float32,
    )


def whole(shape, **kwargs):
    return pl.BlockSpec(shape, lambda *_: (0,) * len(shape), **kwargs)


def call(kernel, name, out_shape, in_specs, out_specs, flops, moved, **kwargs):
    if in_specs is not None:
        kwargs.update(in_specs=in_specs, out_specs=out_specs)
    return pl.pallas_call(
        kernel,
        out_shape=out_shape,
        name=name,
        compiler_params=pltpu.CompilerParams(vmem_limit_bytes=VMEM),
        cost_estimate=pl.CostEstimate(flops=flops, bytes_accessed=moved, transcendentals=0),
        **kwargs,
    )


def own_taps(latents_ref, gain_ref, taps_ref, temb_ref, acc_ref):
    gain = gain_ref[...]
    source = [latents_ref[f].astype(jnp.float32) for f in range(2)]
    norm = [normalize(s, gain).astype(jnp.bfloat16) for s in source]
    temb = temb_ref[...]
    acc_ref[0] = source[0] + temb + dot(norm[0], taps_ref[1]) + dot(norm[1], taps_ref[2])
    acc_ref[1] = source[1] + temb + dot(norm[0], taps_ref[0]) + dot(norm[1], taps_ref[1])


def finish(halo_ref, acc, tap, gain_pre, gain_mid):
    norm = normalize(halo_ref[0].astype(jnp.float32), gain_pre).astype(jnp.bfloat16)
    hidden = (acc + dot(norm, tap)).astype(jnp.bfloat16)
    return hidden, normalize(hidden.astype(jnp.float32), gain_mid).astype(jnp.bfloat16)


def chosen_frame(
    pick_ref, before_ref, after_ref, acc_ref, taps_ref, gain_pre_ref, gain_mid_ref, region_ref,
    hidden_ref, norm_ref, ctx_ref,
):
    def run(halo_ref, frame, tap):
        hidden, norm = finish(
            halo_ref, acc_ref[frame], taps_ref[tap], gain_pre_ref[...], gain_mid_ref[...]
        )
        hidden_ref[...] = hidden
        norm_ref[...] = norm
        pooled = dot(region_ref[...], norm) * (4.0 / PIX)
        rows = normalize(pooled, 1.0).astype(jnp.bfloat16)[:4]
        for copy in range(ctx_ref.shape[0]):
            ctx_ref[copy] = rows

    pl.when(pick_ref[0] == 0)(lambda: run(before_ref, 0, 0))
    pl.when(pick_ref[0] != 0)(lambda: run(after_ref, 1, 2))


def other_frame(
    pick_ref, before_ref, after_ref, acc_ref, taps_ref, gain_pre_ref, gain_mid_ref, w_query_ref,
    hidden_in_ref, norm_in_ref, hidden_ref, query_ref,
):
    def queries(norm):
        return (dot(norm, w_query_ref[...]) * SCALE).astype(jnp.bfloat16)

    def run(halo_ref, frame, tap):
        hidden, norm = finish(
            halo_ref, acc_ref[frame], taps_ref[tap], gain_pre_ref[...], gain_mid_ref[...]
        )
        hidden_ref[1] = hidden
        query_ref[1] = queries(norm)

    pl.when(pick_ref[0] == 0)(lambda: run(after_ref, 1, 2))
    pl.when(pick_ref[0] != 0)(lambda: run(before_ref, 0, 0))
    hidden_ref[0] = hidden_in_ref[...]
    query_ref[0] = queries(norm_in_ref[...])


def attention(
    pick_ref, ctx_ref, w_key_ref, w_value_ref, w_out_ref, query_ref, hidden_ref, out_ref,
    key_ref, value_ref, mixed_ref,
):
    @pl.when(pl.program_id(0) == 0)
    def _():
        left = lax.broadcasted_iota(jnp.int32, (ROWS, 128), 1) < HEAD_DIM
        zero = jnp.zeros((HEAD_DIM, ROWS), jnp.bfloat16)
        for pair in range(PAIRS):
            lanes = slice(128 * pair, 128 * pair + 128)
            keys = dot(ctx_ref[...], w_key_ref[:, lanes]).T.astype(jnp.bfloat16)
            key_ref[2 * pair, :HEAD_DIM] = keys[:HEAD_DIM]
            key_ref[2 * pair, HEAD_DIM:] = zero
            key_ref[2 * pair + 1, :HEAD_DIM] = zero
            key_ref[2 * pair + 1, HEAD_DIM:] = keys[HEAD_DIM:]
            values = dot(ctx_ref[...], w_value_ref[:, lanes])
            value_ref[2 * pair, :, :128] = jnp.where(left, values, 0.0).astype(jnp.bfloat16)
            value_ref[2 * pair, :, 128:] = jnp.where(left, 1.0, 0.0).astype(jnp.bfloat16)
            value_ref[2 * pair + 1, :, :128] = jnp.where(left, 0.0, values).astype(jnp.bfloat16)
            value_ref[2 * pair + 1, :, 128:] = jnp.where(left, 0.0, 1.0).astype(jnp.bfloat16)

    inside = None
    for pair in range(PAIRS):
        lanes = slice(128 * pair, 128 * pair + 128)
        query = query_ref[0, :, lanes]
        total = None
        for side in range(2):
            for start in range(0, ROWS, CHUNK):
                rows = slice(start, start + CHUNK)
                weights = jnp.exp2(dot(query, key_ref[2 * pair + side, :, rows]))
                part = dot(weights.astype(jnp.bfloat16), value_ref[2 * pair + side, rows])
                total = part if total is None else total + part
        sums = total[:, 128:]
        good = jnp.where((sums >= LOW) & (sums <= HIGH), 1.0, 0.0)
        inside = good if inside is None else jnp.minimum(inside, good)
        mixed_ref[:, lanes] = (total[:, :128] / sums).astype(jnp.bfloat16)

    @pl.when(jnp.min(inside) < 0.5)
    def _():
        def some_rows(step, carry):
            rows = pl.ds(pl.multiple_of(step * 128, 128), 128)
            for pair in range(PAIRS):
                lanes = slice(128 * pair, 128 * pair + 128)
                query = query_ref[0, rows, lanes]
                total = jnp.zeros((128, 256), jnp.float32)
                for side in range(2):
                    scores = dot(query, key_ref[2 * pair + side])
                    weights = jnp.exp2(scores - jnp.max(scores, -1, keepdims=True))
                    total += dot(weights.astype(jnp.bfloat16), value_ref[2 * pair + side])
                mixed_ref[rows, lanes] = (total[:, :128] / total[:, 128:]).astype(jnp.bfloat16)
            return carry

        lax.fori_loop(0, PIX // 128, some_rows, 0)

    projected = dot(mixed_ref[...], w_out_ref[...])
    out_ref[0] = (hidden_ref[0].astype(jnp.float32) + projected).astype(jnp.bfloat16)


def shards(
    latents,
    timestep,
    context_frame,
    gain_pre,
    w_temporal,
    w_time,
    gain_mid,
    w_query,
    w_key,
    w_value,
    w_out,
):
    up = [(i, (i + 1) % 256) for i in range(256)]
    down = [(j, i) for i, j in up]
    before = lax.ppermute(latents[1:], AXES, up)
    after = lax.ppermute(latents[:1], AXES, down)

    gain_pre = gain_pre.reshape(1, C)
    gain_mid = gain_mid.reshape(1, C)
    frame, pair = (PIX, C), (2, PIX, C)
    half, single = jnp.bfloat16, jnp.float32
    mac = 2 * PIX * C * C
    temb = time_bias(timestep, w_time)
    acc = call(
        own_taps,
        "own_taps",
        jax.ShapeDtypeStruct(pair, single),
        [whole(pair), whole((1, C)), whole((3, C, C)), whole((1, C))],
        whole(pair),
        4 * mac,
        8 * 10**6,
    )(latents, gain_pre, w_temporal, temb)

    region = np.zeros((16, PIX), np.float32)
    pixel = np.arange(PIX)
    region[(pixel // PW) // (PH // 2) * 2 + (pixel % PW) // (PW // 2), pixel] = 1.0
    scalar = pl.BlockSpec(memory_space=pltpu.SMEM)
    shared = [
        scalar,
        whole((1,) + frame),
        whole((1,) + frame),
        whole(pair),
        whole((3, C, C)),
        whole((1, C)),
        whole((1, C)),
    ]
    hidden, norm, ctx = call(
        chosen_frame,
        "chosen_frame",
        (
            jax.ShapeDtypeStruct(frame, half),
            jax.ShapeDtypeStruct(frame, half),
            jax.ShapeDtypeStruct((8, 4, C), half),
        ),
        shared + [whole((16, PIX))],
        (whole(frame), whole(frame), whole((8, 4, C))),
        mac,
        8 * 10**6,
    )(context_frame, before, after, acc, w_temporal, gain_pre, gain_mid, jnp.asarray(region, half))

    line = exchange(ctx, groups_by(lambda x, y, z, core: (x, y, core))).reshape(32, C)
    plane = exchange(
        jnp.broadcast_to(line[None], (16, 32, C)), groups_by(lambda x, y, z, core: (z, core))
    ).reshape(512, C)
    swapped = lax.ppermute(plane, AXES, [(i, i ^ 1) for i in range(256)])

    hidden, query = call(
        other_frame,
        "other_frame",
        (jax.ShapeDtypeStruct(pair, half), jax.ShapeDtypeStruct(pair, half)),
        shared + [whole((C, C)), whole(frame), whole(frame)],
        (whole(pair), whole(pair)),
        3 * mac,
        12 * 10**6,
    )(context_frame, before, after, acc, w_temporal, gain_pre, gain_mid, w_query, hidden, norm)

    by_frame = pl.BlockSpec((1,) + frame, lambda i, *_: (i, 0, 0))
    return call(
        attention,
        "attention",
        jax.ShapeDtypeStruct(pair, half),
        None,
        None,
        2 * 10**10,
        10 * 10**6,
        grid_spec=pltpu.PrefetchScalarGridSpec(
            num_scalar_prefetch=1,
            grid=(2,),
            in_specs=[whole((ROWS, C))] + [whole((C, C))] * 3 + [by_frame] * 2,
            out_specs=pl.BlockSpec((1,) + frame, lambda i, pick: (jnp.where(pick[0] == 0, i, 1 - i), 0, 0)),
            scratch_shapes=[
                pltpu.VMEM((2 * PAIRS, 128, ROWS), half),
                pltpu.VMEM((2 * PAIRS, ROWS, 256), half),
                pltpu.VMEM(frame, half),
            ],
        ),
    )(context_frame, jnp.concatenate([plane, swapped]), w_key, w_value, w_out, query, hidden)


def solution(mesh):
    return jax.shard_map(
        shards,
        mesh=mesh,
        in_specs=(
            P(("clip", "group"), None, None),
            P(),
            P(("clip", "group")),
            P(),
            P(),
            P(),
            P(),
            P(),
            P(),
            P(),
            P(),
        ),
        out_specs=P(("clip", "group"), None, None),
        check_vma=False,
    )
```

time: 152 us -> 120 us (0.79)
  Pallas kernels: 0 us -> 68.1 us
  matrix products: 63.4 us -> 1.49 us
  other arithmetic: 29.6 us -> 1.33 us
  waiting for transfers between devices: 8.21 us -> 0.01 us
  local copies, waits for them, and re-layouts: 8.31 us -> 4.72 us
  starting transfers between devices: 4.59 us -> 6.83 us
    pallas_call x0 -> x4, Pallas kernels: none -> 68.1 us  [the longest x1 46.3 us: shards(): call(attention, 'attention', jax.ShapeDtypeStruct(pair, half), None, None...]
    dot_general x13 -> x0, matrix products: 62.5 us -> none  [the longest x2 22 us: one_frame(): jnp.einsum('qhr,rhd->qhd', weights.astype(jnp.bfloat16), value_heads, pre...]
    reduce_sum x6 -> x0, other arithmetic: 26.7 us -> none  [the longest x2 22 us: one_frame(): total = jnp.sum(weights, -1)]
    ppermute x3, waiting for transfers between devices: 8.21 us -> 0.01 us  [the longest x1 0.01 us: shards(): after = lax.ppermute(latents[:1], AXES, down)]
    unnamed x30 -> x10, local copies, waits for them, and re-layouts: 5.01 us -> 1.79 us
    ppermute x3, starting transfers between devices: 4.59 us -> 6.83 us  [the longest x1 3.51 us: shards(): swapped = lax.ppermute(plane, AXES, [(i, i ^ 1) for i in range(256)])]
    convert_element_type x1 -> x0, local copies, waits for them, and re-layouts: 1.65 us -> none  [shards(): regions = chosen.astype(jnp.float32).reshape(2, PH // 2, 2, PW // 2, width)]
  transfers between devices with their start and end apart: 3 -> 3, of which waited for: 3 -> 0; matrix products, arithmetic and copies ran while one was open for 3% -> 2% of each run, Pallas kernels for 0% -> 13%
where the time goes in v2:
time: 120 us; the launch traced here: 119 us
  Pallas kernels  68.1 us (57%)
  blocking collectives  35.5 us (30%)
  starting transfers between devices  6.83 us (6%)
  local copies, waits for them, and re-layouts  4.72 us (4%)
  matrix products  1.49 us (1%)
  between operations  1.35 us (1%)
  other arithmetic  1.33 us (1%)
    pallas_call x1, Pallas kernels, shards(): call(attention, 'attention', jax.ShapeDtypeStruct(pair, half), None, None...  46.3 us
    all_to_all x2, blocking collectives, exchange(): lax.all_to_all(copies, AXES, 0, 0, axis_index_groups=groups, tiled=False)  35.5 us
    pallas_call x1, Pallas kernels, shards(): call(other_frame, 'other_frame', (jax.ShapeDtypeStruct(pair, half), jax.S...  8.63 us
    pallas_call x1, Pallas kernels, shards(): call(own_taps, 'own_taps', jax.ShapeDtypeStruct(pair, single), [whole(pai...  7.06 us
    pallas_call x1, Pallas kernels, shards(): call(chosen_frame, 'chosen_frame', (jax.ShapeDtypeStruct(frame, half), ja...  6.14 us
    ppermute x1, starting transfers between devices, shards(): swapped = lax.ppermute(plane, AXES, [(i, i ^ 1) for i in range(256)])  3.51 us
    ppermute x1, starting transfers between devices, shards(): after = lax.ppermute(latents[:1], AXES, down)  3.31 us
  transfers between devices with their start and end apart: 3, of which 0 were waited for; matrix products, arithmetic and copies ran while one was open for 2% of the time, Pallas kernels for 13%

profile of v2, /device:TPU:1, one launch (start us, length us, event | category | flops | bytes accessed | tf_op | source)
XLA Modules:
  0.0 119.3 jit_solution(11125325963045954353)
XLA Ops:
  0.0 0.0 copy-start
  0.0 0.0 copy-start.3
  0.0 0.0 copy-start.4
  0.0 1.7 %fusion.2 = (bf16[1,640,640]{2,1,0:T(8,128)(2,1)S(1)}, bf16[1,640,640]{2,1,0:T(8,128)(2,1)S(1)}) fusion(bf16[2,640,640]{2,1,0:T(8,128)(2,1)} %latents_ref.1), kind=kLoop, calls=%fused_computation.6 | loop fusion | bytes 3276800 | tf_op jit(solution)/shard_map/slice | solution.py:210
  1.7 3.3 %collective-permute-start.1 = (bf16[1,640,640]{2,1,0:T(8,128)(2,1)S(1)}, bf16[1,640,640]{2,1,0:T(8,128)(2,1)S(1)}, u32[]{:S(2)}, u32[]{:S(2)}) collective-permute-start(bf16[1,640,640]{2,1,0:T(8,128)(2,1)S(1)} %get-tuple-element.15), channel_id=1, source_target_pairs={{1,0},{2,1},{3,2},{4,3},{5,4},{6,5},{7,6},{8,7},{9,8},{10,9},{11,1... | collective-permute-start | bytes 2457608 | tf_op jit(solution)/shard_map/ppermute | solution.py:210
  5.0 0.0 collective-permute-start
  6.3 0.0 copy-done.3
  6.3 0.6 reshape.18.gain_ref.gain_pre_ref
  6.9 0.0 copy-done.4
  6.9 0.6 reshape.19.gain_mid_ref
  7.5 0.1 divide_multiply_fusion
  7.6 0.0 copy-done
  7.6 1.5 %fusion.3.temb_ref = f32[1,640]{1,0:T(1,128)} fusion(f32[640,1]{0,1:T(1,128)S(1)} %reshape.21, f32[640,640]{1,0:T(8,128)S(1)} %copy-done), kind=kOutput, calls=%fused_computation.7 | convolution fusion | flops 4915200 | bytes 1643520 | tf_op jit(solution)/shard_map/dot_general | solution.py:57
  9.1 7.1 %own_taps.1.acc_ref = f32[2,640,640]{2,1,0:T(8,128)} custom-call(bf16[2,640,640]{2,1,0:T(8,128)(2,1)} %latents_ref.1, f32[1,640]{1,0:T(1,128)} %reshape.18.gain_ref.gain_pre_ref, bf16[3,640,640]{2,1,0:T(8,128)(2,1)} %taps_ref.5, f32[1,640]{1,0:T(1,128)} %fusion.3.temb_ref), custom_call_target="tpu_custom_call" | custom-call | flops 2097152000 | bytes 8000000 | tf_op jit(solution)/shard_map/own_taps/pallas_call | solution.py:218
  16.2 0.0 collective-permute-done.1.after_ref
  16.2 0.0 copy-start.1
  16.2 0.0 collective-permute-done.before_ref
  16.2 0.9 copy-done.1
  17.1 0.0 copy-start.2
  17.1 0.9 copy-done.2
  18.0 6.1 %chosen_frame.1 = (bf16[640,640]{1,0:T(8,128)(2,1)}, bf16[640,640]{1,0:T(8,128)(2,1)}, bf16[8,4,640]{2,1,0:T(4,128)(2,1)}) custom-call(s32[1]{0:T(128)S(6)} %copy.14.pick_ref, bf16[1,640,640]{2,1,0:T(8,128)(2,1)} %copy-done.2, bf16[1,640,640]{2,1,0:T(8,128)(2,1)} %copy-done.1, f32[2,640,640]{2,1,0:T(8,128)} %own_taps.1.acc_ref, ...), custom_call_target="tpu_custom_call" | custom-call | flops 524288000 | bytes 8000000 | tf_op jit(solution)/shard_map/chosen_frame/pallas_call | solution.py:241
  24.1 16.8 %all_to_all.10 = bf16[8,4,640]{2,1,0:T(4,128)(2,1)S(1)} all-to-all(bf16[8,4,640]{2,1,0:T(4,128)(2,1)} %get-tuple-element.10), channel_id=1, replica_groups={{0,2,4,6,8,10,12,14},{1,3,5,7,9,11,13,15},{16,18,20,22,24,26,28,30},{17..., dimensions={0} | all-to-all | bytes 81920 | tf_op jit(solution)/shard_map/all_to_all | solution.py:41
  40.9 0.1 broadcast_in_dim.9
  41.0 18.8 %all_to_all.11 = bf16[16,32,640]{2,1,0:T(8,128)(2,1)S(1)} all-to-all(bf16[16,32,640]{2,1,0:T(8,128)(2,1)S(1)} %broadcast_in_dim.9), channel_id=1, replica_groups={{0,16,32,48,64,80,96,112,128,144,160,176,192,208,224,240},{1,17,33,49,6..., dimensions={0} | all-to-all | bytes 1310720 | tf_op jit(solution)/shard_map/all_to_all | solution.py:41
  59.7 3.5 %collective-permute-start.2 = (bf16[512,640]{1,0:T(8,128)(2,1)S(1)}, bf16[512,640]{1,0:T(8,128)(2,1)S(1)}, u32[]{:S(2)}, u32[]{:S(2)}) collective-permute-start(bf16[512,640]{1,0:T(8,128)(2,1)S(1)} %bitcast.4), channel_id=1, source_target_pairs={{0,1},{1,0},{2,3},{3,2},{4,5},{5,4},{6,7},{7,6},{8,9},{9,8},{10,11... | collective-permute-start | bytes 1966088 | tf_op jit(solution)/shard_map/ppermute | solution.py:259
  63.2 8.6 %other_frame.1 = (bf16[2,640,640]{2,1,0:T(8,128)(2,1)}, bf16[2,640,640]{2,1,0:T(8,128)(2,1)}) custom-call(s32[1]{0:T(128)S(6)} %copy.14.pick_ref, bf16[1,640,640]{2,1,0:T(8,128)(2,1)} %copy-done.2, bf16[1,640,640]{2,1,0:T(8,128)(2,1)} %copy-done.1, f32[2,640,640]{2,1,0:T(8,128)} %own_taps.1.acc_ref, bf16[3,640,640]{2,1,0:T(8,128)(2,1)} %taps_ref.5, ...), custom_call_target="tpu_custom_call" | custom-call | flops 1572864000 | bytes 12000000 | tf_op jit(solution)/shard_map/other_frame/pallas_call | solution.py:261
  71.9 0.0 collective-permute-done.2
  71.9 1.2 %pad_maximum_fusion.ctx_ref = bf16[1024,640]{1,0:T(8,128)(2,1)} fusion(bf16[512,640]{1,0:T(8,128)(2,1)S(1)} %collective-permute-done.2, bf16[512,640]{1,0:T(8,128)(2,1)S(1)} %bitcast.5), kind=kLoop, calls=%fused_computation | loop fusion | flops 2621440 | bytes 2621440 | tf_op jit(solution)/shard_map/concatenate | solution.py:291
  73.1 46.3 %attention.1 = bf16[2,640,640]{2,1,0:T(8,128)(2,1)} custom-call(s32[1]{0:T(128)S(6)} %copy.14.pick_ref, bf16[1024,640]{1,0:T(8,128)(2,1)} %pad_maximum_fusion.ctx_ref, bf16[640,640]{1,0:T(8,128)(2,1)} %w_key_ref.1, bf16[640,640]{1,0:T(8,128)(2,1)} %w_value_ref.1, bf16[640,640]{1,0:T(8,128)(2,1)} %w_out_ref.1, ...), custom_call_target="tpu_custom_call" | custom-call | flops 20000000000 | bytes 10000000 | tf_op jit(solution)/shard_map/attention/pallas_call | solution.py:272
  (3 shorter events, 0.1 us)
Async XLA Ops:
  0.0 7.6 %copy-start = (f32[640,640]{1,0:T(8,128)S(1)}, f32[640,640]{1,0:T(8,128)}, u32[]{:S(2)}) copy-start(f32[640,640]{1,0:T(8,128)} %param.17) | copy-start | bytes 4915204
  0.0 6.3 %copy-start.3 = (f32[640]{0:T(1024)S(1)}, f32[640]{0:T(1024)}, u32[]{:S(2)}) copy-start(f32[640]{0:T(1024)} %param.15) | copy-start | bytes 7684
  0.0 6.9 %copy-start.4 = (f32[640]{0:T(1024)S(1)}, f32[640]{0:T(1024)}, u32[]{:S(2)}) copy-start(f32[640]{0:T(1024)} %param.18) | copy-start | bytes 7684
  1.7 14.5 %collective-permute-start.1 = (bf16[1,640,640]{2,1,0:T(8,128)(2,1)S(1)}, bf16[1,640,640]{2,1,0:T(8,128)(2,1)S(1)}, u32[]{:S(2)}, u32[]{:S(2)}) collective-permute-start(bf16[1,640,640]{2,1,0:T(8,128)(2,1)S(1)} %get-tuple-element.15), channel_id=1, source_target_pairs={{1,0},{2,1},{3,2},{4,3},{5,4},{6,5},{7,6},{8,7},{9,8},{10,9},{11,1... | collective-permute-start | bytes 2457608 | tf_op jit(solution)/shard_map/ppermute | solution.py:210
  5.0 11.2 %collective-permute-start = (bf16[1,640,640]{2,1,0:T(8,128)(2,1)S(1)}, bf16[1,640,640]{2,1,0:T(8,128)(2,1)S(1)}, u32[]{:S(2)}, u32[]{:S(2)}) collective-permute-start(bf16[1,640,640]{2,1,0:T(8,128)(2,1)S(1)} %get-tuple-element.16), channel_id=1, source_target_pairs={{0,1},{1,2},{2,3},{3,4},{4,5},{5,6},{6,7},{7,8},{8,9},{9,10},{10,1... | collective-permute-start | bytes 2457608 | tf_op jit(solution)/shard_map/ppermute | solution.py:209
  16.2 0.9 copy-start.1
  17.1 0.9 copy-start.2
  59.7 12.1 %collective-permute-start.2 = (bf16[512,640]{1,0:T(8,128)(2,1)S(1)}, bf16[512,640]{1,0:T(8,128)(2,1)S(1)}, u32[]{:S(2)}, u32[]{:S(2)}) collective-permute-start(bf16[512,640]{1,0:T(8,128)(2,1)S(1)} %bitcast.4), channel_id=1, source_target_pairs={{0,1},{1,0},{2,3},{3,2},{4,5},{5,4},{6,7},{7,6},{8,9},{9,8},{10,11... | collective-permute-start | bytes 1966088 | tf_op jit(solution)/shard_map/ppermute | solution.py:259

commit v3 on v2

v3 whole, which is shorter than its diff:
```python
import math

import jax
import jax.numpy as jnp
import numpy as np
from jax import lax
from jax.experimental import pallas as pl
from jax.experimental.pallas import tpu as pltpu
from jax.sharding import PartitionSpec as P

HEAD_DIM = 64
PH = 32
PW = 20
PIX = PH * PW
C = 640
PAIRS = C // (2 * HEAD_DIM)
ROWS = 1024
CHUNK = 256
STRIP = 128
AXES = ("clip", "group")
VMEM = 60 * 2**20
TAPS_VMEM = 56 * 2**20
SCALE = math.log2(math.e) / math.sqrt(HEAD_DIM)
LOW, HIGH = 2.0**-100, 2.0**110


def place(device):
    clip, group = divmod(device, 32)
    x_low, y = divmod(clip, 4)
    x_high, rest = divmod(group, 16)
    z, core = divmod(rest, 2)
    return x_high * 2 + x_low, y, z, core


def groups_by(key):
    found = {}
    for device in range(256):
        found.setdefault(key(*place(device)), []).append(device)
    return list(found.values())


def exchange(copies, groups):
    return lax.all_to_all(copies, AXES, 0, 0, axis_index_groups=groups, tiled=False)


def dot(a, b):
    return jnp.dot(a, b, preferred_element_type=jnp.float32)


def normalize(values, gain):
    return values * lax.rsqrt(jnp.mean(values * values, -1, keepdims=True) + 1e-06) * gain


def time_bias(timestep, w_time):
    half = w_time.shape[0] // 2
    freqs = jnp.exp(-math.log(10000.0) * jnp.arange(half, dtype=jnp.float32) / half)
    angle = timestep.astype(jnp.float32)[0] * freqs
    embed = jnp.concatenate([jnp.cos(angle), jnp.sin(angle)])
    return jnp.dot(
        jax.nn.silu(embed)[None, :],
        w_time,
        precision=lax.Precision.HIGHEST,
        preferred_element_type=jnp.float32,
    )


def whole(shape, **kwargs):
    return pl.BlockSpec(shape, lambda *_: (0,) * len(shape), **kwargs)


def call(kernel, name, out_shape, in_specs, out_specs, flops, moved, vmem=VMEM, **kwargs):
    if in_specs is not None:
        kwargs.update(in_specs=in_specs, out_specs=out_specs)
    return pl.pallas_call(
        kernel,
        out_shape=out_shape,
        name=name,
        compiler_params=pltpu.CompilerParams(vmem_limit_bytes=vmem),
        cost_estimate=pl.CostEstimate(flops=flops, bytes_accessed=moved, transcendentals=0),
        **kwargs,
    )


def copy_all(pairs, sems):
    copies = [pltpu.make_async_copy(a, b, sems.at[i]) for i, (a, b) in enumerate(pairs)]
    for copy in copies:
        copy.start()
    return copies


def strips():
    return [slice(start, start + STRIP) for start in range(0, PIX, STRIP)]


def own_taps(latents_ref, gain_ref, temb_ref, taps_ref, acc_ref, big_ref, part_ref, sems, out_sems):
    order = ((1, 0), (2, 1))
    places = [
        (taps_ref.at[order[i][j]], big_ref.at[pl.ds(C * i, C), pl.ds(C * j, C)])
        for i in range(2)
        for j in range(2)
    ]
    copies = copy_all(places, sems)
    gain, temb = gain_ref[...], temb_ref[...]
    writes = []
    for number, rows in enumerate(strips()):
        source = [latents_ref[f, rows].astype(jnp.float32) for f in range(2)]
        norm = jnp.concatenate([normalize(s, gain).astype(jnp.bfloat16) for s in source], axis=1)
        if number == 0:
            for copy in copies:
                copy.wait()
        both = dot(norm, big_ref[...])
        for f in range(2):
            part_ref[f, rows] = source[f] + temb + both[:, C * f : C * f + C]
            copy = pltpu.make_async_copy(
                part_ref.at[f, rows], acc_ref.at[f, rows], out_sems.at[2 * number + f]
            )
            copy.start()
            writes.append(copy)
    for copy in writes:
        copy.wait()


def chosen_frame(
    pick_ref, before_ref, after_ref, gain_pre_ref, gain_mid_ref, region_ref, acc_ref, taps_ref,
    hidden_out, ctx_ref, hidden_ref, part_ref, tap_ref, sems, out_sems,
):
    first = pick_ref[0] == 0
    frame = jnp.where(first, 0, 1)
    tap_copy, part_copy = copy_all(
        [(taps_ref.at[2 * frame], tap_ref), (acc_ref.at[frame], part_ref)], sems
    )
    gain_pre, gain_mid = gain_pre_ref[...], gain_mid_ref[...]
    pooled = None
    writes = []
    for number, rows in enumerate(strips()):
        halo = jnp.where(first, before_ref[0, rows], after_ref[0, rows]).astype(jnp.float32)
        norm = normalize(halo, gain_pre).astype(jnp.bfloat16)
        if number == 0:
            tap_copy.wait()
            part_copy.wait()
        hidden = (part_ref[rows] + dot(norm, tap_ref[...])).astype(jnp.bfloat16)
        hidden_ref[rows] = hidden
        writes += copy_all([(hidden_ref.at[rows], hidden_out.at[rows])], out_sems.at[pl.ds(number, 1)])
        norm = normalize(hidden.astype(jnp.float32), gain_mid).astype(jnp.bfloat16)
        sums = dot(region_ref[:, rows], norm)
        pooled = sums if pooled is None else pooled + sums
    rows = normalize(pooled * (4.0 / PIX), 1.0).astype(jnp.bfloat16)[:4]
    for copy in range(ctx_ref.shape[0]):
        ctx_ref[copy] = rows
    for copy in writes:
        copy.wait()


def other_frame(
    pick_ref, before_ref, after_ref, gain_pre_ref, gain_mid_ref, chosen_hbm, acc_ref, taps_ref,
    w_query_hbm, hidden_out, query_out, hidden_ref, query_ref, part_ref, tap_ref, chosen_ref,
    w_query_ref, sems, out_sems,
):
    first = pick_ref[0] == 0
    frame = jnp.where(first, 1, 0)
    copies = copy_all(
        [
            (chosen_hbm, chosen_ref),
            (w_query_hbm, w_query_ref),
            (taps_ref.at[2 * frame], tap_ref),
            (acc_ref.at[frame], part_ref),
        ],
        sems,
    )
    gain_pre, gain_mid = gain_pre_ref[...], gain_mid_ref[...]
    for copy in copies[:2]:
        copy.wait()

    def queries(slot, rows, hidden):
        norm = normalize(hidden.astype(jnp.float32), gain_mid).astype(jnp.bfloat16)
        query_ref[slot, rows] = (dot(norm, w_query_ref[...]) * SCALE).astype(jnp.bfloat16)

    for rows in strips():
        queries(0, rows, chosen_ref[rows])
    writes = copy_all([(query_ref.at[0], query_out.at[0])], out_sems.at[pl.ds(0, 1)])
    for copy in copies[2:]:
        copy.wait()
    for rows in strips():
        halo = jnp.where(first, after_ref[0, rows], before_ref[0, rows]).astype(jnp.float32)
        norm = normalize(halo, gain_pre).astype(jnp.bfloat16)
        hidden = (part_ref[rows] + dot(norm, tap_ref[...])).astype(jnp.bfloat16)
        hidden_ref[rows] = hidden
        queries(1, rows, hidden)
    writes += copy_all(
        [(query_ref.at[1], query_out.at[1]), (hidden_ref, hidden_out)], out_sems.at[pl.ds(1, 2)]
    )
    for copy in writes:
        copy.wait()


def attention(
    pick_ref, near_ref, far_ref, w_key_hbm, w_value_hbm, w_out_hbm, query_hbm, chosen_hbm, other_hbm,
    out_ref, key_ref, value_ref, mixed_ref, w_key_ref, w_value_ref, w_out_ref, query_ref, hidden_ref,
    sems,
):
    step = pl.program_id(0)
    moves = [
        pltpu.make_async_copy(a, b, sems.at[i])
        for i, (a, b) in enumerate(
            [
                (w_key_hbm, w_key_ref),
                (w_value_hbm, w_value_ref),
                (query_hbm, query_ref),
                (w_out_hbm, w_out_ref),
                (chosen_hbm, hidden_ref.at[0]),
                (other_hbm, hidden_ref.at[1]),
            ]
        )
    ]

    @pl.when(step == 0)
    def _():
        for move in moves:
            move.start()
        half = ROWS // 2
        left = lax.broadcasted_iota(jnp.int32, (half, 128), 1) < HEAD_DIM
        zero = jnp.zeros((HEAD_DIM, half), jnp.bfloat16)
        moves[0].wait()
        for number, ctx_ref in enumerate((near_ref, far_ref)):
            rows = slice(half * number, half * number + half)
            for pair in range(PAIRS):
                lanes = slice(128 * pair, 128 * pair + 128)
                keys = dot(ctx_ref[...], w_key_ref[:, lanes]).T.astype(jnp.bfloat16)
                key_ref[2 * pair, :HEAD_DIM, rows] = keys[:HEAD_DIM]
                key_ref[2 * pair, HEAD_DIM:, rows] = zero
                key_ref[2 * pair + 1, :HEAD_DIM, rows] = zero
                key_ref[2 * pair + 1, HEAD_DIM:, rows] = keys[HEAD_DIM:]
        moves[1].wait()
        for number, ctx_ref in enumerate((near_ref, far_ref)):
            rows = slice(half * number, half * number + half)
            for pair in range(PAIRS):
                lanes = slice(128 * pair, 128 * pair + 128)
                values = dot(ctx_ref[...], w_value_ref[:, lanes])
                for side in range(2):
                    mine = left if side == 0 else ~left
                    value_ref[2 * pair + side, rows, :128] = jnp.where(mine, values, 0.0).astype(
                        jnp.bfloat16
                    )
                    value_ref[2 * pair + side, rows, 128:] = jnp.where(mine, 1.0, 0.0).astype(
                        jnp.bfloat16
                    )
        for move in moves[2:]:
            move.wait()

    inside = None
    for pair in range(PAIRS):
        lanes = slice(128 * pair, 128 * pair + 128)
        query = query_ref[step, :, lanes]
        total = None
        for side in range(2):
            for start in range(0, ROWS, CHUNK):
                rows = slice(start, start + CHUNK)
                weights = jnp.exp2(dot(query, key_ref[2 * pair + side, :, rows]))
                part = dot(weights.astype(jnp.bfloat16), value_ref[2 * pair + side, rows])
                total = part if total is None else total + part
        sums = total[:, 128:]
        good = jnp.where((sums >= LOW) & (sums <= HIGH), 1.0, 0.0)
        inside = good if inside is None else jnp.minimum(inside, good)
        mixed_ref[:, lanes] = (total[:, :128] / sums).astype(jnp.bfloat16)

    @pl.when(jnp.min(inside) < 0.5)
    def _():
        def some_rows(strip, carry):
            rows = pl.ds(pl.multiple_of(strip * 128, 128), 128)
            for pair in range(PAIRS):
                lanes = slice(128 * pair, 128 * pair + 128)
                query = query_ref[step, rows, lanes]
                total = jnp.zeros((128, 256), jnp.float32)
                for side in range(2):
                    scores = dot(query, key_ref[2 * pair + side])
                    weights = jnp.exp2(scores - jnp.max(scores, -1, keepdims=True))
                    total += dot(weights.astype(jnp.bfloat16), value_ref[2 * pair + side])
                mixed_ref[rows, lanes] = (total[:, :128] / total[:, 128:]).astype(jnp.bfloat16)
            return carry

        lax.fori_loop(0, PIX // 128, some_rows, 0)

    projected = dot(mixed_ref[...], w_out_ref[...])
    out_ref[0] = (hidden_ref[step].astype(jnp.float32) + projected).astype(jnp.bfloat16)


def shards(
    latents,
    timestep,
    context_frame,
    gain_pre,
    w_temporal,
    w_time,
    gain_mid,
    w_query,
    w_key,
    w_value,
    w_out,
):
    up = [(i, (i + 1) % 256) for i in range(256)]
    down = [(j, i) for i, j in up]
    after = lax.ppermute(latents[:1], AXES, down)
    before = lax.ppermute(latents[1:], AXES, up)

    gain_pre = gain_pre.reshape(1, C)
    gain_mid = gain_mid.reshape(1, C)
    frame, pair, square = (PIX, C), (2, PIX, C), (C, C)
    half, single = jnp.bfloat16, jnp.float32
    mac = 2 * PIX * C * C
    here, there = pl.BlockSpec(memory_space=pltpu.VMEM), pl.BlockSpec(memory_space=pltpu.HBM)
    scalar = pl.BlockSpec(memory_space=pltpu.SMEM)
    temb = time_bias(timestep, w_time)
    acc = call(
        own_taps,
        "own_taps",
        jax.ShapeDtypeStruct(pair, single),
        [here, here, here, there],
        there,
        4 * mac,
        8 * 10**6,
        TAPS_VMEM,
        scratch_shapes=[
            pltpu.VMEM((2 * C, 2 * C), half),
            pltpu.VMEM(pair, single),
            pltpu.SemaphoreType.DMA((4,)),
            pltpu.SemaphoreType.DMA((2 * PIX // STRIP,)),
        ],
    )(latents, gain_pre, temb, w_temporal)

    region = np.zeros((16, PIX), np.float32)
    pixel = np.arange(PIX)
    region[(pixel // PW) // (PH // 2) * 2 + (pixel % PW) // (PW // 2), pixel] = 1.0
    chosen, ctx = call(
        chosen_frame,
        "chosen_frame",
        (jax.ShapeDtypeStruct(frame, half), jax.ShapeDtypeStruct((8, 4, C), half)),
        [scalar, here, here, here, here, here, there, there],
        (there, here),
        mac,
        8 * 10**6,
        scratch_shapes=[
            pltpu.VMEM(frame, half),
            pltpu.VMEM(frame, single),
            pltpu.VMEM(square, half),
            pltpu.SemaphoreType.DMA((2,)),
            pltpu.SemaphoreType.DMA((PIX // STRIP,)),
        ],
    )(context_frame, before, after, gain_pre, gain_mid, jnp.asarray(region, half), acc, w_temporal)

    line = exchange(ctx, groups_by(lambda x, y, z, core: (x, y, core))).reshape(32, C)
    other, query = call(
        other_frame,
        "other_frame",
        (jax.ShapeDtypeStruct(frame, half), jax.ShapeDtypeStruct(pair, half)),
        [scalar, here, here, here, here, there, there, there, there],
        (there, there),
        3 * mac,
        12 * 10**6,
        scratch_shapes=[
            pltpu.VMEM(frame, half),
            pltpu.VMEM(pair, half),
            pltpu.VMEM(frame, single),
            pltpu.VMEM(square, half),
            pltpu.VMEM(frame, half),
            pltpu.VMEM(square, half),
            pltpu.SemaphoreType.DMA((4,)),
            pltpu.SemaphoreType.DMA((3,)),
        ],
    )(context_frame, before, after, gain_pre, gain_mid, chosen, acc, w_temporal, w_query)

    line, other, query = lax.optimization_barrier((line, other, query))
    plane = exchange(
        jnp.broadcast_to(line[None], (16, 32, C)), groups_by(lambda x, y, z, core: (z, core))
    ).reshape(512, C)
    swapped = lax.ppermute(plane, AXES, [(i, i ^ 1) for i in range(256)])

    return call(
        attention,
        "attention",
        jax.ShapeDtypeStruct(pair, half),
        None,
        None,
        2 * 10**10,
        10 * 10**6,
        grid_spec=pltpu.PrefetchScalarGridSpec(
            num_scalar_prefetch=1,
            grid=(2,),
            in_specs=[whole((ROWS // 2, C))] * 2 + [there] * 6,
            out_specs=pl.BlockSpec(
                (1,) + frame, lambda i, pick: (jnp.where(pick[0] == 0, i, 1 - i), 0, 0)
            ),
            scratch_shapes=[
                pltpu.VMEM((2 * PAIRS, 128, ROWS), half),
                pltpu.VMEM((2 * PAIRS, ROWS, 256), half),
                pltpu.VMEM(frame, half),
                pltpu.VMEM(square, half),
                pltpu.VMEM(square, half),
                pltpu.VMEM(square, half),
                pltpu.VMEM(pair, half),
                pltpu.VMEM(pair, half),
                pltpu.SemaphoreType.DMA((6,)),
            ],
        ),
    )(context_frame, plane, swapped, w_key, w_value, w_out, query, chosen, other)


def solution(mesh):
    return jax.shard_map(
        shards,
        mesh=mesh,
        in_specs=(
            P(("clip", "group"), None, None),
            P(),
            P(("clip", "group")),
            P(),
            P(),
            P(),
            P(),
            P(),
            P(),
            P(),
            P(),
        ),
        out_specs=P(("clip", "group"), None, None),
        check_vma=False,
    )
```

time: 120 us -> 111 us (0.925)
  blocking collectives: 35.5 us -> 20.2 us
  starting transfers between devices: 6.83 us -> 13.2 us
  waiting for transfers between devices: 0.01 us -> 2.82 us
  other arithmetic: 1.33 us -> 0.13 us
    all_to_all x2 -> x1, blocking collectives: 35.5 us -> 20.2 us  [exchange(): lax.all_to_all(copies, AXES, 0, 0, axis_index_groups=groups, tiled=False)]
    all_to_all x0 -> x1, starting transfers between devices: none -> 8.11 us  [exchange(): lax.all_to_all(copies, AXES, 0, 0, axis_index_groups=groups, tiled=False)]
    ppermute x1, starting transfers between devices: 0.01 us -> 3.1 us  [shards(): before = lax.ppermute(latents[1:], AXES, up)]
    ppermute x1, starting transfers between devices: 3.31 us -> 0.3 us  [shards(): after = lax.ppermute(latents[:1], AXES, down)]
    ppermute x1, starting transfers between devices: 3.51 us -> 1.69 us  [shards(): swapped = lax.ppermute(plane, AXES, [(i, i ^ 1) for i in range(256)])]
    ppermute x1, waiting for transfers between devices: 0.01 us -> 1.72 us  [shards(): swapped = lax.ppermute(plane, AXES, [(i, i ^ 1) for i in range(256)])]
    pallas_call x2, Pallas kernels: 15.7 us -> 14.4 us  [the longest x1 7.92 us: shards(): call(other_frame, 'other_frame', (jax.ShapeDtypeStruct(frame, half), jax....]
    concatenate x1 -> x0, other arithmetic: 1.2 us -> none  [shards(): jnp.concatenate([plane, swapped])]
  transfers between devices with their start and end apart: 3 -> 4, of which waited for: 0 -> 2; matrix products, arithmetic and copies ran while one was open for 2% -> 3% of each run, Pallas kernels for 13% -> 13%
where the time goes in v3:
time: 111 us
  Pallas kernels  67 us (60%)
  blocking collectives  20.2 us (18%)
  starting transfers between devices  13.2 us (12%)
  local copies, waits for them, and re-layouts  4.69 us (4%)
  waiting for transfers between devices  2.82 us (3%)
  between operations  1.56 us (1%)
  matrix products  1.49 us (1%)
    pallas_call x1, Pallas kernels, shards(): call(attention, 'attention', jax.ShapeDtypeStruct(pair, half), None, None...  46.3 us
    all_to_all x1, blocking collectives, exchange(): lax.all_to_all(copies, AXES, 0, 0, axis_index_groups=groups, tiled=False)  20.2 us
    all_to_all x1, starting transfers between devices, exchange(): lax.all_to_all(copies, AXES, 0, 0, axis_index_groups=groups, tiled=False)  8.11 us
    pallas_call x1, Pallas kernels, shards(): call(other_frame, 'other_frame', (jax.ShapeDtypeStruct(frame, half), jax....  7.92 us
    pallas_call x1, Pallas kernels, shards(): call(own_taps, 'own_taps', jax.ShapeDtypeStruct(pair, single), [here, her...  6.51 us
    pallas_call x1, Pallas kernels, shards(): call(chosen_frame, 'chosen_frame', (jax.ShapeDtypeStruct(frame, half), ja...  6.27 us
    ppermute x1, starting transfers between devices, shards(): before = lax.ppermute(latents[1:], AXES, up)  3.1 us
  transfers between devices with their start and end apart: 4, of which 2 were waited for; matrix products, arithmetic and copies ran while one was open for 3% of the time, Pallas kernels for 13%

profile of v3, /device:TPU:1, one launch (start us, length us, event | category | flops | bytes accessed | tf_op | source)
XLA Modules:
  0.0 111.1 jit_solution(14678496354971400605)
XLA Ops:
  0.0 0.0 copy-start
  0.0 0.0 copy-start.4
  0.0 0.0 copy-start.5
  0.0 1.7 %fusion.2 = (bf16[1,640,640]{2,1,0:T(8,128)(2,1)S(1)}, bf16[1,640,640]{2,1,0:T(8,128)(2,1)S(1)}) fusion(bf16[2,640,640]{2,1,0:T(8,128)(2,1)} %latents_ref.1), kind=kLoop, calls=%fused_computation.5 | loop fusion | bytes 3276800 | tf_op jit(solution)/shard_map/slice | solution.py:302
  1.7 3.1 %collective-permute-start = (bf16[1,640,640]{2,1,0:T(8,128)(2,1)S(1)}, bf16[1,640,640]{2,1,0:T(8,128)(2,1)S(1)}, u32[]{:S(2)}, u32[]{:S(2)}) collective-permute-start(bf16[1,640,640]{2,1,0:T(8,128)(2,1)S(1)} %get-tuple-element.20), channel_id=1, source_target_pairs={{0,1},{1,2},{2,3},{3,4},{4,5},{5,6},{6,7},{7,8},{8,9},{9,10},{10,1... | collective-permute-start | bytes 2457608 | tf_op jit(solution)/shard_map/ppermute | solution.py:303
  4.8 0.3 collective-permute-start.1
  5.7 0.0 copy-done.4
  5.7 0.6 reshape.21.gain_ref.gain_pre_ref
  6.3 0.0 copy-done.5
  6.3 0.6 reshape.22.gain_mid_ref
  7.6 0.1 divide_multiply_fusion
  7.7 0.0 copy-done
  7.7 1.5 %fusion.3.temb_ref = f32[1,640]{1,0:T(1,128)} fusion(f32[640,1]{0,1:T(1,128)S(1)} %reshape.25, f32[640,640]{1,0:T(8,128)S(1)} %copy-done), kind=kOutput, calls=%fused_computation.6 | convolution fusion | flops 4915200 | bytes 1643520 | tf_op jit(solution)/shard_map/dot_general | solution.py:59
  9.2 6.5 %own_taps.1.acc_ref = f32[2,640,640]{2,1,0:T(8,128)} custom-call(bf16[2,640,640]{2,1,0:T(8,128)(2,1)} %latents_ref.1, f32[1,640]{1,0:T(1,128)} %reshape.21.gain_ref.gain_pre_ref, f32[1,640]{1,0:T(1,128)} %fusion.3.temb_ref, bf16[3,640,640]{2,1,0:T(8,128)(2,1)} %taps_ref.5), custom_call_target="tpu_custom_call" | custom-call | flops 2097152000 | bytes 8000000 | tf_op jit(solution)/shard_map/own_taps/pallas_call | solution.py:313
  15.7 0.0 collective-permute-done.before_ref
  15.7 0.0 copy-start.1
  15.7 1.1 collective-permute-done.1.after_ref
  16.8 0.0 copy-done.1
  16.8 0.0 copy-start.2
  16.8 0.9 copy-done.2
  17.7 6.3 %chosen_frame.1 = (bf16[640,640]{1,0:T(8,128)(2,1)}, bf16[8,4,640]{2,1,0:T(4,128)(2,1)}) custom-call(s32[1]{0:T(128)S(6)} %copy.14.pick_ref, bf16[1,640,640]{2,1,0:T(8,128)(2,1)} %copy-done.1, bf16[1,640,640]{2,1,0:T(8,128)(2,1)} %copy-done.2, f32[1,640]{1,0:T(1,128)} %reshape.21.gain_ref.gain_pre_ref, f32[1,640]{1,0:T(1,128)} %reshape.22.gain_mid_ref, ...), custom_call_target="tpu_custom_call" | custom-call | flops 524288000 | bytes 8000000 | tf_op jit(solution)/shard_map/chosen_frame/pallas_call | solution.py:333
  24.0 8.1 %all-to-all-start = ((bf16[8,4,640]{2,1,0:T(4,128)(2,1)}), bf16[8,4,640]{2,1,0:T(4,128)(2,1)S(1)}, u32[]{:S(2)}, u32[]{:S(2)}) async-start(bf16[8,4,640]{2,1,0:T(4,128)(2,1)} %get-tuple-element.12), calls=%async_computation | async-start | bytes 81920 | tf_op jit(solution)/shard_map/all_to_all | solution.py:43
  32.1 7.9 %other_frame.1 = (bf16[640,640]{1,0:T(8,128)(2,1)}, bf16[2,640,640]{2,1,0:T(8,128)(2,1)}) custom-call(s32[1]{0:T(128)S(6)} %copy.14.pick_ref, bf16[1,640,640]{2,1,0:T(8,128)(2,1)} %copy-done.1, bf16[1,640,640]{2,1,0:T(8,128)(2,1)} %copy-done.2, f32[1,640]{1,0:T(1,128)} %reshape.21.gain_ref.gain_pre_ref, f32[1,640]{1,0:T(1,128)} %reshape.22.gain_mid_ref, ...), custom_call_target="tpu_custom_call" | custom-call | flops 1572864000 | bytes 12000000 | tf_op jit(solution)/shard_map/other_frame/pallas_call | solution.py:351
  40.1 0.0 all-to-all-done
  40.1 0.1 broadcast_in_dim.2
  40.1 20.2 %all_to_all.10 = bf16[16,32,640]{2,1,0:T(8,128)(2,1)S(1)} all-to-all(bf16[16,32,640]{2,1,0:T(8,128)(2,1)S(1)} %broadcast_in_dim.2), channel_id=1, replica_groups={{0,16,32,48,64,80,96,112,128,144,160,176,192,208,224,240},{1,17,33,49,6..., dimensions={0} | all-to-all | bytes 1310720 | tf_op jit(solution)/shard_map/all_to_all | solution.py:43
  60.4 0.0 copy-start.3
  60.4 1.7 %collective-permute-start.2 = (bf16[512,640]{1,0:T(8,128)(2,1)S(1)}, bf16[512,640]{1,0:T(8,128)(2,1)S(1)}, u32[]{:S(2)}, u32[]{:S(2)}) collective-permute-start(bf16[512,640]{1,0:T(8,128)(2,1)S(1)} %bitcast.4), channel_id=1, source_target_pairs={{0,1},{1,0},{2,3},{3,2},{4,5},{5,4},{6,7},{7,6},{8,9},{9,8},{10,11... | collective-permute-start | bytes 1966088 | tf_op jit(solution)/shard_map/ppermute | solution.py:375
  62.1 1.7 %collective-permute-done.2.far_ref = bf16[512,640]{1,0:T(8,128)(2,1)S(1)} collective-permute-done((bf16[512,640]{1,0:T(8,128)(2,1)S(1)}, bf16[512,640]{1,0:T(8,128)(2,1)S(1)}, u32[]{:S(2)}, u32[]{:S(2)}) %collective-permute-start.2) | collective-permute-done | bytes 655392 | tf_op jit(solution)/shard_map/ppermute | solution.py:375
  63.8 0.0 copy-done.3
  63.8 0.9 copy-done.6
  64.7 46.3 %attention.1 = bf16[2,640,640]{2,1,0:T(8,128)(2,1)} custom-call(s32[1]{0:T(128)S(6)} %copy.14.pick_ref, bf16[512,640]{1,0:T(8,128)(2,1)} %bitcast.5, bf16[512,640]{1,0:T(8,128)(2,1)} %copy-done.6, bf16[640,640]{1,0:T(8,128)(2,1)} %w_key_hbm.1, bf16[640,640]{1,0:T(8,128)(2,1)} %w_value_hbm.1, bf16[640,640]{1,0:T(8,128)(2,1)} %w_out_hbm.1, ...), custom_call_target="tpu_custom_call" | custom-call | flops 20000000000 | bytes 10000000 | tf_op jit(solution)/shard_map/attention/pallas_call | solution.py:377
  (4 shorter events, 0.1 us)
Async XLA Ops:
  0.0 7.7 %copy-start = (f32[640,640]{1,0:T(8,128)S(1)}, f32[640,640]{1,0:T(8,128)}, u32[]{:S(2)}) copy-start(f32[640,640]{1,0:T(8,128)} %param.17) | copy-start | bytes 4915204
  0.0 5.7 %copy-start.4 = (f32[640]{0:T(1024)S(1)}, f32[640]{0:T(1024)}, u32[]{:S(2)}) copy-start(f32[640]{0:T(1024)} %param.15) | copy-start | bytes 7684
  0.0 6.3 %copy-start.5 = (f32[640]{0:T(1024)S(1)}, f32[640]{0:T(1024)}, u32[]{:S(2)}) copy-start(f32[640]{0:T(1024)} %param.18) | copy-start | bytes 7684
  1.7 14.1 %collective-permute-start = (bf16[1,640,640]{2,1,0:T(8,128)(2,1)S(1)}, bf16[1,640,640]{2,1,0:T(8,128)(2,1)S(1)}, u32[]{:S(2)}, u32[]{:S(2)}) collective-permute-start(bf16[1,640,640]{2,1,0:T(8,128)(2,1)S(1)} %get-tuple-element.20), channel_id=1, source_target_pairs={{0,1},{1,2},{2,3},{3,4},{4,5},{5,6},{6,7},{7,8},{8,9},{9,10},{10,1... | collective-permute-start | bytes 2457608 | tf_op jit(solution)/shard_map/ppermute | solution.py:303
  4.8 12.1 %collective-permute-start.1 = (bf16[1,640,640]{2,1,0:T(8,128)(2,1)S(1)}, bf16[1,640,640]{2,1,0:T(8,128)(2,1)S(1)}, u32[]{:S(2)}, u32[]{:S(2)}) collective-permute-start(bf16[1,640,640]{2,1,0:T(8,128)(2,1)S(1)} %get-tuple-element.19), channel_id=1, source_target_pairs={{1,0},{2,1},{3,2},{4,3},{5,4},{6,5},{7,6},{8,7},{9,8},{10,9},{11,1... | collective-permute-start | bytes 2457608 | tf_op jit(solution)/shard_map/ppermute | solution.py:302
  15.7 1.1 copy-start.1
  16.8 0.9 copy-start.2
  24.0 16.0 %all-to-all-start = ((bf16[8,4,640]{2,1,0:T(4,128)(2,1)}), bf16[8,4,640]{2,1,0:T(4,128)(2,1)S(1)}, u32[]{:S(2)}, u32[]{:S(2)}) async-start(bf16[8,4,640]{2,1,0:T(4,128)(2,1)} %get-tuple-element.12), calls=%async_computation | async-start | bytes 81920 | tf_op jit(solution)/shard_map/all_to_all | solution.py:43
  60.4 3.4 %copy-start.3 = (bf16[16,32,640]{2,1,0:T(8,128)(2,1)}, bf16[16,32,640]{2,1,0:T(8,128)(2,1)S(1)}, u32[]{:S(2)}) copy-start(bf16[16,32,640]{2,1,0:T(8,128)(2,1)S(1)} %all_to_all.10) | copy-start | bytes 1966084
  60.4 3.4 %collective-permute-start.2 = (bf16[512,640]{1,0:T(8,128)(2,1)S(1)}, bf16[512,640]{1,0:T(8,128)(2,1)S(1)}, u32[]{:S(2)}, u32[]{:S(2)}) collective-permute-start(bf16[512,640]{1,0:T(8,128)(2,1)S(1)} %bitcast.4), channel_id=1, source_target_pairs={{0,1},{1,0},{2,3},{3,2},{4,5},{5,4},{6,7},{7,6},{8,9},{9,8},{10,11... | collective-permute-start | bytes 1966088 | tf_op jit(solution)/shard_map/ppermute | solution.py:375
  63.8 0.9 copy-start.6

commit v4 on v3

--- a/solution.py
+++ b/solution.py
@@ -16,10 +16,13 @@
 PAIRS = C // (2 * HEAD_DIM)
 ROWS = 1024
 CHUNK = 256
-STRIP = 128
+STRIP = 320
 AXES = ("clip", "group")
-VMEM = 60 * 2**20
-TAPS_VMEM = 56 * 2**20
+MIB = 2**20
+TAPS_VMEM = 24 * MIB
+CONTEXT_VMEM = 24 * MIB
+HIDDEN_VMEM = 56 * MIB
+ATTENTION_VMEM = 52 * MIB
 SCALE = math.log2(math.e) / math.sqrt(HEAD_DIM)
 LOW, HIGH = 2.0**-100, 2.0**110
 
@@ -68,7 +71,7 @@
     return pl.BlockSpec(shape, lambda *_: (0,) * len(shape), **kwargs)
 
 
-def call(kernel, name, out_shape, in_specs, out_specs, flops, moved, vmem=VMEM, **kwargs):
+def call(kernel, name, out_shape, in_specs, out_specs, flops, moved, vmem, **kwargs):
     if in_specs is not None:
         kwargs.update(in_specs=in_specs, out_specs=out_specs)
     return pl.pallas_call(
@@ -92,109 +95,86 @@
     return [slice(start, start + STRIP) for start in range(0, PIX, STRIP)]
 
 
-def own_taps(latents_ref, gain_ref, temb_ref, taps_ref, acc_ref, big_ref, part_ref, sems, out_sems):
+def own_taps(
+    pick_ref, latents_ref, gain_ref, temb_ref, taps_ref, chosen_ref, other_ref, big_ref, sems
+):
+    first = pick_ref[0] == 0
     order = ((1, 0), (2, 1))
-    places = [
-        (taps_ref.at[order[i][j]], big_ref.at[pl.ds(C * i, C), pl.ds(C * j, C)])
-        for i in range(2)
-        for j in range(2)
-    ]
-    copies = copy_all(places, sems)
+    copies = copy_all(
+        [
+            (taps_ref.at[order[i][j]], big_ref.at[pl.ds(C * i, C), pl.ds(C * j, C)])
+            for i in range(2)
+            for j in range(2)
+        ],
+        sems,
+    )
     gain, temb = gain_ref[...], temb_ref[...]
-    writes = []
-    for number, rows in enumerate(strips()):
+    for copy in copies:
+        copy.wait()
+    for rows in strips():
         source = [latents_ref[f, rows].astype(jnp.float32) for f in range(2)]
         norm = jnp.concatenate([normalize(s, gain).astype(jnp.bfloat16) for s in source], axis=1)
-        if number == 0:
-            for copy in copies:
-                copy.wait()
         both = dot(norm, big_ref[...])
-        for f in range(2):
-            part_ref[f, rows] = source[f] + temb + both[:, C * f : C * f + C]
-            copy = pltpu.make_async_copy(
-                part_ref.at[f, rows], acc_ref.at[f, rows], out_sems.at[2 * number + f]
-            )
-            copy.start()
-            writes.append(copy)
-    for copy in writes:
-        copy.wait()
-
-
-def chosen_frame(
-    pick_ref, before_ref, after_ref, gain_pre_ref, gain_mid_ref, region_ref, acc_ref, taps_ref,
-    hidden_out, ctx_ref, hidden_ref, part_ref, tap_ref, sems, out_sems,
+        parts = [source[f] + temb + both[:, C * f : C * f + C] for f in range(2)]
+        chosen_ref[rows] = jnp.where(first, parts[0], parts[1])
+        other_ref[rows] = jnp.where(first, parts[1], parts[0])
+
+
+def context_rows(
+    pick_ref, before_ref, after_ref, gain_pre_ref, gain_mid_ref, side_ref, part_ref, taps_ref, ctx_ref
 ):
     first = pick_ref[0] == 0
-    frame = jnp.where(first, 0, 1)
-    tap_copy, part_copy = copy_all(
-        [(taps_ref.at[2 * frame], tap_ref), (acc_ref.at[frame], part_ref)], sems
-    )
+    tap = jnp.where(first, 0, 2)
     gain_pre, gain_mid = gain_pre_ref[...], gain_mid_ref[...]
-    pooled = None
-    writes = []
-    for number, rows in enumerate(strips()):
+    tile = side_ref.shape[0]
+    sums = []
+    for half in range(2):
+        rows = slice(half * PIX // 2, (half + 1) * PIX // 2)
         halo = jnp.where(first, before_ref[0, rows], after_ref[0, rows]).astype(jnp.float32)
         norm = normalize(halo, gain_pre).astype(jnp.bfloat16)
-        if number == 0:
-            tap_copy.wait()
-            part_copy.wait()
-        hidden = (part_ref[rows] + dot(norm, tap_ref[...])).astype(jnp.bfloat16)
-        hidden_ref[rows] = hidden
-        writes += copy_all([(hidden_ref.at[rows], hidden_out.at[rows])], out_sems.at[pl.ds(number, 1)])
+        hidden = (part_ref[rows] + dot(norm, taps_ref[tap])).astype(jnp.bfloat16)
         norm = normalize(hidden.astype(jnp.float32), gain_mid).astype(jnp.bfloat16)
-        sums = dot(region_ref[:, rows], norm)
-        pooled = sums if pooled is None else pooled + sums
-    rows = normalize(pooled * (4.0 / PIX), 1.0).astype(jnp.bfloat16)[:4]
+        norm = norm.astype(jnp.float32).reshape(PIX // 2 // tile, tile, C)
+        for side in range(2):
+            here = jnp.sum(norm * side_ref[:, C * side : C * side + C], axis=0)
+            sums.append(jnp.sum(here, axis=0, keepdims=True))
+    pooled = jnp.concatenate(sums, axis=0) * (4.0 / PIX)
+    rows = normalize(pooled, 1.0).astype(jnp.bfloat16)
     for copy in range(ctx_ref.shape[0]):
         ctx_ref[copy] = rows
-    for copy in writes:
-        copy.wait()
-
-
-def other_frame(
-    pick_ref, before_ref, after_ref, gain_pre_ref, gain_mid_ref, chosen_hbm, acc_ref, taps_ref,
-    w_query_hbm, hidden_out, query_out, hidden_ref, query_ref, part_ref, tap_ref, chosen_ref,
-    w_query_ref, sems, out_sems,
+
+
+def hidden_queries(
+    pick_ref, before_ref, after_ref, gain_pre_ref, gain_mid_ref, part_hbm, other_part_hbm, taps_hbm,
+    w_query_hbm, hidden_ref, query_ref, part_ref, taps_ref, w_query_ref, sems,
 ):
     first = pick_ref[0] == 0
-    frame = jnp.where(first, 1, 0)
     copies = copy_all(
         [
-            (chosen_hbm, chosen_ref),
+            (taps_hbm.at[0], taps_ref.at[0]),
+            (taps_hbm.at[2], taps_ref.at[1]),
+            (part_hbm, part_ref.at[0]),
+            (other_part_hbm, part_ref.at[1]),
             (w_query_hbm, w_query_ref),
-            (taps_ref.at[2 * frame], tap_ref),
-            (acc_ref.at[frame], part_ref),
         ],
         sems,
     )
     gain_pre, gain_mid = gain_pre_ref[...], gain_mid_ref[...]
-    for copy in copies[:2]:
+    for copy in copies:
         copy.wait()
-
-    def queries(slot, rows, hidden):
-        norm = normalize(hidden.astype(jnp.float32), gain_mid).astype(jnp.bfloat16)
-        query_ref[slot, rows] = (dot(norm, w_query_ref[...]) * SCALE).astype(jnp.bfloat16)
-
-    for rows in strips():
-        queries(0, rows, chosen_ref[rows])
-    writes = copy_all([(query_ref.at[0], query_out.at[0])], out_sems.at[pl.ds(0, 1)])
-    for copy in copies[2:]:
-        copy.wait()
-    for rows in strips():
-        halo = jnp.where(first, after_ref[0, rows], before_ref[0, rows]).astype(jnp.float32)
-        norm = normalize(halo, gain_pre).astype(jnp.bfloat16)
-        hidden = (part_ref[rows] + dot(norm, tap_ref[...])).astype(jnp.bfloat16)
-        hidden_ref[rows] = hidden
-        queries(1, rows, hidden)
-    writes += copy_all(
-        [(query_ref.at[1], query_out.at[1]), (hidden_ref, hidden_out)], out_sems.at[pl.ds(1, 2)]
-    )
-    for copy in writes:
-        copy.wait()
+    for slot in range(2):
+        tap = jnp.where(first, slot, 1 - slot)
+        for rows in strips():
+            halo = jnp.where(tap == 0, before_ref[0, rows], after_ref[0, rows]).astype(jnp.float32)
+            norm = normalize(halo, gain_pre).astype(jnp.bfloat16)
+            hidden = (part_ref[slot, rows] + dot(norm, taps_ref[tap])).astype(jnp.bfloat16)
+            hidden_ref[slot, rows] = hidden
+            norm = normalize(hidden.astype(jnp.float32), gain_mid).astype(jnp.bfloat16)
+            query_ref[slot, rows] = (dot(norm, w_query_ref[...]) * SCALE).astype(jnp.bfloat16)
 
 
 def attention(
-    pick_ref, near_ref, far_ref, w_key_hbm, w_value_hbm, w_out_hbm, query_hbm, chosen_hbm, other_hbm,
+    pick_ref, near_ref, far_ref, w_key_hbm, w_value_hbm, w_out_hbm, query_hbm, hidden_hbm,
     out_ref, key_ref, value_ref, mixed_ref, w_key_ref, w_value_ref, w_out_ref, query_ref, hidden_ref,
     sems,
 ):
@@ -207,8 +187,7 @@
                 (w_value_hbm, w_value_ref),
                 (query_hbm, query_ref),
                 (w_out_hbm, w_out_ref),
-                (chosen_hbm, hidden_ref.at[0]),
-                (other_hbm, hidden_ref.at[1]),
+                (hidden_hbm, hidden_ref),
             ]
         )
     ]
@@ -310,68 +289,53 @@
     here, there = pl.BlockSpec(memory_space=pltpu.VMEM), pl.BlockSpec(memory_space=pltpu.HBM)
     scalar = pl.BlockSpec(memory_space=pltpu.SMEM)
     temb = time_bias(timestep, w_time)
-    acc = call(
+    part, other_part = call(
         own_taps,
         "own_taps",
-        jax.ShapeDtypeStruct(pair, single),
-        [here, here, here, there],
-        there,
+        (jax.ShapeDtypeStruct(frame, single), jax.ShapeDtypeStruct(frame, single)),
+        [scalar, here, here, here, there],
+        (here, here),
         4 * mac,
         8 * 10**6,
         TAPS_VMEM,
-        scratch_shapes=[
-            pltpu.VMEM((2 * C, 2 * C), half),
-            pltpu.VMEM(pair, single),
-            pltpu.SemaphoreType.DMA((4,)),
-            pltpu.SemaphoreType.DMA((2 * PIX // STRIP,)),
-        ],
-    )(latents, gain_pre, temb, w_temporal)
-
-    region = np.zeros((16, PIX), np.float32)
-    pixel = np.arange(PIX)
-    region[(pixel // PW) // (PH // 2) * 2 + (pixel % PW) // (PW // 2), pixel] = 1.0
-    chosen, ctx = call(
-        chosen_frame,
-        "chosen_frame",
-        (jax.ShapeDtypeStruct(frame, half), jax.ShapeDtypeStruct((8, 4, C), half)),
-        [scalar, here, here, here, here, here, there, there],
-        (there, here),
+        scratch_shapes=[pltpu.VMEM((2 * C, 2 * C), half), pltpu.SemaphoreType.DMA((4,))],
+    )(context_frame, latents, gain_pre, temb, w_temporal)
+
+    row = np.arange(2 * PW)
+    left = np.broadcast_to((row % PW < PW // 2)[:, None], (2 * PW, C))
+    sides = jnp.asarray(np.concatenate([left, ~left], axis=1), single)
+    ctx = call(
+        context_rows,
+        "context_rows",
+        jax.ShapeDtypeStruct((8, 4, C), half),
+        [scalar, here, here, here, here, here, here, here],
+        here,
         mac,
         8 * 10**6,
+        CONTEXT_VMEM,
+    )(context_frame, before, after, gain_pre, gain_mid, sides, part, w_temporal)
+    hidden, query = call(
+        hidden_queries,
+        "hidden_queries",
+        (jax.ShapeDtypeStruct(pair, half), jax.ShapeDtypeStruct(pair, half)),
+        [scalar, here, here, here, here, there, there, there, there],
+        (here, here),
+        4 * mac,
+        12 * 10**6,
+        HIDDEN_VMEM,
         scratch_shapes=[
-            pltpu.VMEM(frame, half),
-            pltpu.VMEM(frame, single),
+            pltpu.VMEM(pair, single),
+            pltpu.VMEM(pair, half),
             pltpu.VMEM(square, half),
-            pltpu.SemaphoreType.DMA((2,)),
-            pltpu.SemaphoreType.DMA((PIX // STRIP,)),
+            pltpu.SemaphoreType.DMA((5,)),
         ],
-    )(context_frame, before, after, gain_pre, gain_mid, jnp.asarray(region, half), acc, w_temporal)
+    )(context_frame, before, after, gain_pre, gain_mid, part, other_part, w_temporal, w_query)
 
     line = exchange(ctx, groups_by(lambda x, y, z, core: (x, y, core))).reshape(32, C)
-    other, query = call(
-        other_frame,
-        "other_frame",
-        (jax.ShapeDtypeStruct(frame, half), jax.ShapeDtypeStruct(pair, half)),
-        [scalar, here, here, here, here, there, there, there, there],
-        (there, there),
-        3 * mac,
-        12 * 10**6,
-        scratch_shapes=[
-            pltpu.VMEM(frame, half),
-            pltpu.VMEM(pair, half),
-            pltpu.VMEM(frame, single),
-            pltpu.VMEM(square, half),
-            pltpu.VMEM(frame, half),
-            pltpu.VMEM(square, half),
-            pltpu.SemaphoreType.DMA((4,)),
-            pltpu.SemaphoreType.DMA((3,)),
-        ],
-    )(context_frame, before, after, gain_pre, gain_mid, chosen, acc, w_temporal, w_query)
-
-    line, other, query = lax.optimization_barrier((line, other, query))
     plane = exchange(
         jnp.broadcast_to(line[None], (16, 32, C)), groups_by(lambda x, y, z, core: (z, core))
     ).reshape(512, C)
+    plane, hidden, query = lax.optimization_barrier((plane, hidden, query))
     swapped = lax.ppermute(plane, AXES, [(i, i ^ 1) for i in range(256)])
 
     return call(
@@ -382,10 +346,11 @@
         None,
         2 * 10**10,
         10 * 10**6,
+        ATTENTION_VMEM,
         grid_spec=pltpu.PrefetchScalarGridSpec(
             num_scalar_prefetch=1,
             grid=(2,),
-            in_specs=[whole((ROWS // 2, C))] * 2 + [there] * 6,
+            in_specs=[whole((ROWS // 2, C))] * 2 + [there] * 5,
             out_specs=pl.BlockSpec(
                 (1,) + frame, lambda i, pick: (jnp.where(pick[0] == 0, i, 1 - i), 0, 0)
             ),
@@ -398,10 +363,10 @@
                 pltpu.VMEM(square, half),
                 pltpu.VMEM(pair, half),
                 pltpu.VMEM(pair, half),
-                pltpu.SemaphoreType.DMA((6,)),
+                pltpu.SemaphoreType.DMA((5,)),
             ],
         ),
-    )(context_frame, plane, swapped, w_key, w_value, w_out, query, chosen, other)
+    )(context_frame, plane, swapped, w_key, w_value, w_out, query, hidden)
 
 
 def solution(mesh):

time: 111 us -> 103 us (0.928)
  Pallas kernels: 67 us -> 59.1 us
  waiting for transfers between devices: 2.82 us -> 10.3 us
  blocking collectives: 20.2 us -> 14.9 us
  local copies, waits for them, and re-layouts: 4.69 us -> 2.68 us
    pallas_call x3, Pallas kernels: 20.7 us -> 14.1 us  [the longest x1 9.57 us: shards(): call(hidden_queries, 'hidden_queries', (jax.ShapeDtypeStruct(pair, half),...]
    all_to_all x1, blocking collectives: 20.2 us -> 14.9 us  [exchange(): lax.all_to_all(copies, AXES, 0, 0, axis_index_groups=groups, tiled=False)]
    ppermute x1, waiting for transfers between devices: 0.01 us -> 3.71 us  [shards(): before = lax.ppermute(latents[1:], AXES, up)]
    all_to_all x1, waiting for transfers between devices: 0.01 us -> 2.09 us  [exchange(): lax.all_to_all(copies, AXES, 0, 0, axis_index_groups=groups, tiled=False)]
    unnamed x14 -> x24, local copies, waits for them, and re-layouts: 1.79 us -> 0.06 us
    ppermute x1, waiting for transfers between devices: 1.09 us -> 2.77 us  [shards(): after = lax.ppermute(latents[:1], AXES, down)]
    pallas_call x1, Pallas kernels: 46.3 us -> 45 us  [shards(): call(attention, 'attention', jax.ShapeDtypeStruct(pair, half), None, None...]
  transfers between devices with their start and end apart: 4 -> 4, of which waited for: 2 -> 4; matrix products, arithmetic and copies ran while one was open for 3% -> 1% of each run, Pallas kernels for 13% -> 12%
where the time goes in v4:
time: 103 us; the launch traced here: 102 us
  Pallas kernels  59.1 us (57%)
  blocking collectives  14.9 us (14%)
  starting transfers between devices  12.8 us (12%)
  waiting for transfers between devices  10.3 us (10%)
  local copies, waits for them, and re-layouts  2.68 us (3%)
  between operations  1.64 us (2%)
    pallas_call x1, Pallas kernels, shards(): call(attention, 'attention', jax.ShapeDtypeStruct(pair, half), None, None...  45 us
    all_to_all x1, blocking collectives, exchange(): lax.all_to_all(copies, AXES, 0, 0, axis_index_groups=groups, tiled=False)  14.9 us
    pallas_call x1, Pallas kernels, shards(): call(hidden_queries, 'hidden_queries', (jax.ShapeDtypeStruct(pair, half),...  9.57 us
    all_to_all x1, starting transfers between devices, exchange(): lax.all_to_all(copies, AXES, 0, 0, axis_index_groups=groups, tiled=False)  8.09 us
    ppermute x1, waiting for transfers between devices, shards(): before = lax.ppermute(latents[1:], AXES, up)  3.71 us
    ppermute x1, starting transfers between devices, shards(): before = lax.ppermute(latents[1:], AXES, up)  3.1 us
    pallas_call x1, Pallas kernels, shards(): call(own_taps, 'own_taps', (jax.ShapeDtypeStruct(frame, single), jax.Shap...  2.82 us
    ppermute x1, waiting for transfers between devices, shards(): after = lax.ppermute(latents[:1], AXES, down)  2.77 us
  transfers between devices with their start and end apart: 4, of which 4 were waited for; matrix products, arithmetic and copies ran while one was open for 1% of the time, Pallas kernels for 12%

profile of v4, /device:TPU:1, one launch (start us, length us, event | category | flops | bytes accessed | tf_op | source)
XLA Modules:
  0.0 102.4 jit_solution(9629373741618456261)
XLA Ops:
  0.0 0.0 copy-start
  0.0 0.0 copy-start.1
  0.0 1.7 %fusion.2 = (bf16[1,640,640]{2,1,0:T(8,128)(2,1)S(1)}, bf16[1,640,640]{2,1,0:T(8,128)(2,1)S(1)}) fusion(bf16[2,640,640]{2,1,0:T(8,128)(2,1)} %latents_ref.1), kind=kLoop, calls=%fused_computation.5 | loop fusion | bytes 3276800 | tf_op jit(solution)/shard_map/slice | solution.py:281
  1.7 0.0 copy-start.5
  1.7 3.1 %collective-permute-start = (bf16[1,640,640]{2,1,0:T(8,128)(2,1)S(1)}, bf16[1,640,640]{2,1,0:T(8,128)(2,1)S(1)}, u32[]{:S(2)}, u32[]{:S(2)}) collective-permute-start(bf16[1,640,640]{2,1,0:T(8,128)(2,1)S(1)} %get-tuple-element.20), channel_id=1, source_target_pairs={{0,1},{1,2},{2,3},{3,4},{4,5},{5,6},{6,7},{7,8},{8,9},{9,10},{10,1... | collective-permute-start | bytes 2457608 | tf_op jit(solution)/shard_map/ppermute | solution.py:282
  4.8 0.3 collective-permute-start.1
  6.5 0.1 divide_multiply_fusion
  6.6 0.0 copy-done.10
  6.6 0.0 copy-done.11
  6.6 0.0 copy-start.8
  6.6 0.0 copy-done
  6.6 0.0 copy-start.9
  6.6 0.9 fusion.3.temb_ref
  7.5 0.0 copy-done.1
  7.5 0.0 copy-done.5
  7.5 0.0 copy-start.7
  7.6 2.8 %own_taps.1 = (f32[640,640]{1,0:T(8,128)S(1)}, f32[640,640]{1,0:T(8,128)S(1)}) custom-call(s32[1]{0:T(128)S(6)} %copy.14.pick_ref, bf16[2,640,640]{2,1,0:T(8,128)(2,1)S(1)} %copy-done.5, f32[1,640]{1,0:T(1,128)S(1)} %reshape.18.gain_ref.gain_pre_ref, f32[1,640]{1,0:T(1,128)S(1)} %fusion.3.temb_ref, bf16[3,640,640]{2,1,0:T(8,128)(2,1)S(1)} %copy-done.1), custom_call_target="tpu_custom_call" | custom-call | flops 2097152000 | bytes 8000000 | tf_op jit(solution)/shard_map/own_taps/pallas_call | solution.py:292
  10.4 0.0 copy-start.2
  10.4 0.0 copy-start.6
  10.4 3.7 %collective-permute-done.before_ref = bf16[1,640,640]{2,1,0:T(8,128)(2,1)S(1)} collective-permute-done((bf16[1,640,640]{2,1,0:T(8,128)(2,1)S(1)}, bf16[1,640,640]{2,1,0:T(8,128)(2,1)S(1)}, u32[]{:S(2)}, u32[]{:S(2)}) %collective-permute-start) | collective-permute-done | bytes 819232 | tf_op jit(solution)/shard_map/ppermute | solution.py:282
  14.1 2.8 %collective-permute-done.1.after_ref = bf16[1,640,640]{2,1,0:T(8,128)(2,1)S(1)} collective-permute-done((bf16[1,640,640]{2,1,0:T(8,128)(2,1)S(1)}, bf16[1,640,640]{2,1,0:T(8,128)(2,1)S(1)}, u32[]{:S(2)}, u32[]{:S(2)}) %collective-permute-start.1) | collective-permute-done | bytes 819232 | tf_op jit(solution)/shard_map/ppermute | solution.py:281
  16.9 0.0 copy-done.8
  16.9 0.0 copy-done.9
  16.9 1.7 %context_rows.1 = bf16[8,4,640]{2,1,0:T(4,128)(2,1)S(1)} custom-call(s32[1]{0:T(128)S(6)} %copy.14.pick_ref, bf16[1,640,640]{2,1,0:T(8,128)(2,1)S(1)} %collective-permute-done.before_ref, bf16[1,640,640]{2,1,0:T(8,128)(2,1)S(1)} %collective-permute-done.1.after_ref, f32[1,640]{1,0:T(1,128)S(1)} %reshape.18.gain_ref.gain_pre_ref, ...), custom_call_target="tpu_custom_call" | custom-call | flops 524288000 | bytes 8000000 | tf_op jit(solution)/shard_map/context_rows/pallas_call | solution.py:307
  18.7 14.9 %all_to_all.10 = bf16[8,4,640]{2,1,0:T(4,128)(2,1)S(1)} all-to-all(bf16[8,4,640]{2,1,0:T(4,128)(2,1)S(1)} %context_rows.1), channel_id=1, replica_groups={{0,2,4,6,8,10,12,14},{1,3,5,7,9,11,13,15},{16,18,20,22,24,26,28,30},{17..., dimensions={0} | all-to-all | bytes 81920 | tf_op jit(solution)/shard_map/all_to_all | solution.py:46
  33.6 0.9 broadcast_in_dim.9
  34.5 8.1 %all-to-all-start.1 = ((bf16[16,32,640]{2,1,0:T(8,128)(2,1)}), bf16[16,32,640]{2,1,0:T(8,128)(2,1)S(1)}, u32[]{:S(2)}, u32[]{:S(2)}) async-start(bf16[16,32,640]{2,1,0:T(8,128)(2,1)} %broadcast_in_dim.9), calls=%async_computation.1 | async-start | bytes 1310720 | tf_op jit(solution)/shard_map/all_to_all | solution.py:46
  42.6 9.6 %hidden_queries.1 = (bf16[2,640,640]{2,1,0:T(8,128)(2,1)}, bf16[2,640,640]{2,1,0:T(8,128)(2,1)}) custom-call(s32[1]{0:T(128)S(6)} %copy.14.pick_ref, bf16[1,640,640]{2,1,0:T(8,128)(2,1)} %copy-done.3, bf16[1,640,640]{2,1,0:T(8,128)(2,1)} %copy-done.4, f32[1,640]{1,0:T(1,128)} %copy-done.8, f32[1,640]{1,0:T(1,128)} %copy-done.9, f32[640,640]{1,0:T(8,128)} %copy-done.2, ...), custom_call_target="tpu_custom_call" | custom-call | flops 2097152000 | bytes 12000000 | tf_op jit(solution)/shard_map/hidden_queries/pallas_call | solution.py:317
  52.1 2.1 %all-to-all-done.1 = bf16[16,32,640]{2,1,0:T(8,128)(2,1)S(1)} async-done(((bf16[16,32,640]{2,1,0:T(8,128)(2,1)}), bf16[16,32,640]{2,1,0:T(8,128)(2,1)S(1)}, u32[]{:S(2)}, u32[]{:S(2)}) %all-to-all-start.1) | async-done | bytes 655392 | tf_op jit(solution)/shard_map/all_to_all | solution.py:46
  54.2 1.3 %collective-permute-start.2 = (bf16[512,640]{1,0:T(8,128)(2,1)S(1)}, bf16[512,640]{1,0:T(8,128)(2,1)S(1)}, u32[]{:S(2)}, u32[]{:S(2)}) collective-permute-start(bf16[512,640]{1,0:T(8,128)(2,1)S(1)} %bitcast.4), channel_id=1, source_target_pairs={{0,1},{1,0},{2,3},{3,2},{4,5},{5,4},{6,7},{7,6},{8,9},{9,8},{10,11... | collective-permute-start | bytes 1966088 | tf_op jit(solution)/shard_map/ppermute | solution.py:339
  55.5 1.7 %collective-permute-done.2.far_ref = bf16[512,640]{1,0:T(8,128)(2,1)S(1)} collective-permute-done((bf16[512,640]{1,0:T(8,128)(2,1)S(1)}, bf16[512,640]{1,0:T(8,128)(2,1)S(1)}, u32[]{:S(2)}, u32[]{:S(2)}) %collective-permute-start.2) | collective-permute-done | bytes 655392 | tf_op jit(solution)/shard_map/ppermute | solution.py:339
  57.2 45.0 %attention.1 = bf16[2,640,640]{2,1,0:T(8,128)(2,1)} custom-call(s32[1]{0:T(128)S(6)} %copy.14.pick_ref, bf16[512,640]{1,0:T(8,128)(2,1)S(1)} %bitcast.5, bf16[512,640]{1,0:T(8,128)(2,1)S(1)} %collective-permute-done.2.far_ref, bf16[640,640]{1,0:T(8,128)(2,1)} %w_key_hbm.1, bf16[640,640]{1,0:T(8,128)(2,1)} %w_value_hbm.1, bf16[640,640]{1,0:T(8,128)(2,1)} %w_out_hbm.1, ...), custom_call_target="tpu_custom_call" | custom-call | flops 20000000000 | bytes 10000000 | tf_op jit(solution)/shard_map/attention/pallas_call | solution.py:341
  (14 shorter events, 0.1 us)
Async XLA Ops:
  0.0 6.6 %copy-start = (f32[640,640]{1,0:T(8,128)S(1)}, f32[640,640]{1,0:T(8,128)}, u32[]{:S(2)}) copy-start(f32[640,640]{1,0:T(8,128)} %param.17) | copy-start | bytes 4915204
  0.0 6.6 %copy-start.10 = (f32[640]{0:T(1024)S(1)}, f32[640]{0:T(1024)}, u32[]{:S(2)}) copy-start(f32[640]{0:T(1024)} %param.15) | copy-start | bytes 7684
  0.0 6.6 %copy-start.11 = (f32[640]{0:T(1024)S(1)}, f32[640]{0:T(1024)}, u32[]{:S(2)}) copy-start(f32[640]{0:T(1024)} %param.18) | copy-start | bytes 7684
  0.0 7.5 %copy-start.1 = (bf16[3,640,640]{2,1,0:T(8,128)(2,1)S(1)}, bf16[3,640,640]{2,1,0:T(8,128)(2,1)}, u32[]{:S(2)}) copy-start(bf16[3,640,640]{2,1,0:T(8,128)(2,1)} %taps_hbm.1) | copy-start | bytes 7372804
  1.7 5.8 %copy-start.5 = (bf16[2,640,640]{2,1,0:T(8,128)(2,1)S(1)}, bf16[2,640,640]{2,1,0:T(8,128)(2,1)}, u32[]{:S(2)}) copy-start(bf16[2,640,640]{2,1,0:T(8,128)(2,1)} %latents_ref.1) | copy-start | bytes 4915204
  1.7 12.4 %collective-permute-start = (bf16[1,640,640]{2,1,0:T(8,128)(2,1)S(1)}, bf16[1,640,640]{2,1,0:T(8,128)(2,1)S(1)}, u32[]{:S(2)}, u32[]{:S(2)}) collective-permute-start(bf16[1,640,640]{2,1,0:T(8,128)(2,1)S(1)} %get-tuple-element.20), channel_id=1, source_target_pairs={{0,1},{1,2},{2,3},{3,4},{4,5},{5,6},{6,7},{7,8},{8,9},{9,10},{10,1... | collective-permute-start | bytes 2457608 | tf_op jit(solution)/shard_map/ppermute | solution.py:282
  4.8 12.1 %collective-permute-start.1 = (bf16[1,640,640]{2,1,0:T(8,128)(2,1)S(1)}, bf16[1,640,640]{2,1,0:T(8,128)(2,1)S(1)}, u32[]{:S(2)}, u32[]{:S(2)}) collective-permute-start(bf16[1,640,640]{2,1,0:T(8,128)(2,1)S(1)} %get-tuple-element.19), channel_id=1, source_target_pairs={{1,0},{2,1},{3,2},{4,3},{5,4},{6,5},{7,6},{8,7},{9,8},{10,9},{11,1... | collective-permute-start | bytes 2457608 | tf_op jit(solution)/shard_map/ppermute | solution.py:281
  6.6 10.3 %copy-start.8 = (f32[1,640]{1,0:T(1,128)}, f32[1,640]{1,0:T(1,128)S(1)}, u32[]{:S(2)}) copy-start(f32[1,640]{1,0:T(1,128)S(1)} %reshape.18.gain_ref.gain_pre_ref) | copy-start | bytes 7684
  6.6 10.3 %copy-start.9 = (f32[1,640]{1,0:T(1,128)}, f32[1,640]{1,0:T(1,128)S(1)}, u32[]{:S(2)}) copy-start(f32[1,640]{1,0:T(1,128)S(1)} %reshape.19.gain_mid_ref) | copy-start | bytes 7684
  7.5 9.4 %copy-start.7 = (f32[40,1280]{1,0:T(8,128)S(1)}, f32[40,1280]{1,0:T(8,128)}, u32[]{:S(2)}) copy-start(f32[40,1280]{1,0:T(8,128)} %constant.10.clone.side_ref) | copy-start | bytes 614404
  10.4 8.3 %copy-start.2 = (f32[640,640]{1,0:T(8,128)}, f32[640,640]{1,0:T(8,128)S(1)}, u32[]{:S(2)}) copy-start(f32[640,640]{1,0:T(8,128)S(1)} %get-tuple-element.12.part_ref.part_hbm) | copy-start | bytes 4915204
  10.4 8.3 %copy-start.6 = (f32[640,640]{1,0:T(8,128)}, f32[640,640]{1,0:T(8,128)S(1)}, u32[]{:S(2)}) copy-start(f32[640,640]{1,0:T(8,128)S(1)} %get-tuple-element.13.other_part_hbm) | copy-start | bytes 4915204
  14.1 4.6 %copy-start.3 = (bf16[1,640,640]{2,1,0:T(8,128)(2,1)}, bf16[1,640,640]{2,1,0:T(8,128)(2,1)S(1)}, u32[]{:S(2)}) copy-start(bf16[1,640,640]{2,1,0:T(8,128)(2,1)S(1)} %collective-permute-done.before_ref) | copy-start | bytes 2457604
  16.9 1.8 %copy-start.4 = (bf16[1,640,640]{2,1,0:T(8,128)(2,1)}, bf16[1,640,640]{2,1,0:T(8,128)(2,1)S(1)}, u32[]{:S(2)}) copy-start(bf16[1,640,640]{2,1,0:T(8,128)(2,1)S(1)} %collective-permute-done.1.after_ref) | copy-start | bytes 2457604
  34.5 19.8 %all-to-all-start.1 = ((bf16[16,32,640]{2,1,0:T(8,128)(2,1)}), bf16[16,32,640]{2,1,0:T(8,128)(2,1)S(1)}, u32[]{:S(2)}, u32[]{:S(2)}) async-start(bf16[16,32,640]{2,1,0:T(8,128)(2,1)} %broadcast_in_dim.9), calls=%async_computation.1 | async-start | bytes 1310720 | tf_op jit(solution)/shard_map/all_to_all | solution.py:46
  54.2 3.0 %collective-permute-start.2 = (bf16[512,640]{1,0:T(8,128)(2,1)S(1)}, bf16[512,640]{1,0:T(8,128)(2,1)S(1)}, u32[]{:S(2)}, u32[]{:S(2)}) collective-permute-start(bf16[512,640]{1,0:T(8,128)(2,1)S(1)} %bitcast.4), channel_id=1, source_target_pairs={{0,1},{1,0},{2,3},{3,2},{4,5},{5,4},{6,7},{7,6},{8,9},{9,8},{10,11... | collective-permute-start | bytes 1966088 | tf_op jit(solution)/shard_map/ppermute | solution.py:339

commit v5 on v4

v5 whole, which is shorter than its diff:
```python
import functools
import math

import jax
import jax.numpy as jnp
import numpy as np
from jax import lax
from jax.experimental import pallas as pl
from jax.experimental.pallas import tpu as pltpu
from jax.sharding import PartitionSpec as P

HEAD_DIM = 64
PH = 32
PW = 20
PIX = PH * PW
C = 640
PAIRS = C // (2 * HEAD_DIM)
ROWS = 1024
ONES = 16
STRIP = 320
AXES = ("clip", "group")
MIB = 2**20
TAPS_VMEM = 24 * MIB
CONTEXT_VMEM = 24 * MIB
HIDDEN_VMEM = 56 * MIB
ATTENTION_VMEM = 52 * MIB
SCALE = math.log2(math.e) / math.sqrt(HEAD_DIM)
LOW, HIGH = 2.0**-100, 2.0**110


def place(device):
    clip, group = divmod(device, 32)
    x_low, y = divmod(clip, 4)
    x_high, rest = divmod(group, 16)
    z, core = divmod(rest, 2)
    return x_high * 2 + x_low, y, z, core


def groups_by(key):
    found = {}
    for device in range(256):
        found.setdefault(key(*place(device)), []).append(device)
    return list(found.values())


def exchange(copies, groups):
    return lax.all_to_all(copies, AXES, 0, 0, axis_index_groups=groups, tiled=False)


def dot(a, b):
    return jnp.dot(a, b, preferred_element_type=jnp.float32)


def normalize(values, gain):
    return values * lax.rsqrt(jnp.mean(values * values, -1, keepdims=True) + 1e-06) * gain


def time_bias(timestep, w_time):
    half = w_time.shape[0] // 2
    freqs = jnp.exp(-math.log(10000.0) * jnp.arange(half, dtype=jnp.float32) / half)
    angle = timestep.astype(jnp.float32)[0] * freqs
    embed = jnp.concatenate([jnp.cos(angle), jnp.sin(angle)])
    return jnp.dot(
        jax.nn.silu(embed)[None, :],
        w_time,
        precision=lax.Precision.HIGHEST,
        preferred_element_type=jnp.float32,
    )


def call(kernel, name, out_shape, in_specs, out_specs, flops, moved, vmem, **kwargs):
    return pl.pallas_call(
        kernel,
        out_shape=out_shape,
        in_specs=in_specs,
        out_specs=out_specs,
        name=name,
        compiler_params=pltpu.CompilerParams(vmem_limit_bytes=vmem),
        cost_estimate=pl.CostEstimate(flops=flops, bytes_accessed=moved, transcendentals=0),
        **kwargs,
    )


def copy_all(pairs, sems):
    copies = [pltpu.make_async_copy(a, b, sems.at[i]) for i, (a, b) in enumerate(pairs)]
    for copy in copies:
        copy.start()
    return copies


def strips():
    return [slice(start, start + STRIP) for start in range(0, PIX, STRIP)]


def own_taps(
    pick_ref, latents_ref, gain_ref, temb_ref, taps_ref, soon_ref, chosen_ref, other_ref, big_ref, sems
):
    first = pick_ref[0] == 0
    order = ((1, 0), (2, 1))
    copies = copy_all(
        [
            (taps_ref.at[order[i][j]], big_ref.at[pl.ds(C * i, C), pl.ds(C * j, C)])
            for i in range(2)
            for j in range(2)
        ],
        sems,
    )
    gain, temb = gain_ref[...], temb_ref[...]
    for copy in copies:
        copy.wait()
    for rows in strips():
        source = [latents_ref[f, rows].astype(jnp.float32) for f in range(2)]
        norm = jnp.concatenate([normalize(s, gain).astype(jnp.bfloat16) for s in source], axis=1)
        both = dot(norm, big_ref[...])
        parts = [source[f] + temb + both[:, C * f : C * f + C] for f in range(2)]
        chosen = jnp.where(first, parts[0], parts[1])
        soon_ref[rows] = chosen
        chosen_ref[rows] = chosen
        other_ref[rows] = jnp.where(first, parts[1], parts[0])


def context_rows(
    pick_ref, before_ref, after_ref, gain_pre_ref, gain_mid_ref, side_ref, part_ref, taps_ref, ctx_ref
):
    first = pick_ref[0] == 0
    tap = jnp.where(first, 0, 2)
    gain_pre, gain_mid = gain_pre_ref[...], gain_mid_ref[...]
    tile = side_ref.shape[0]
    sums = []
    for half in range(2):
        rows = slice(half * PIX // 2, (half + 1) * PIX // 2)
        halo = jnp.where(first, before_ref[0, rows], after_ref[0, rows]).astype(jnp.float32)
        norm = normalize(halo, gain_pre).astype(jnp.bfloat16)
        hidden = (part_ref[rows] + dot(norm, taps_ref[tap])).astype(jnp.bfloat16)
        norm = normalize(hidden.astype(jnp.float32), gain_mid).astype(jnp.bfloat16)
        norm = norm.astype(jnp.float32).reshape(PIX // 2 // tile, tile, C)
        for side in range(2):
            here = jnp.sum(norm * side_ref[:, C * side : C * side + C], axis=0)
            sums.append(jnp.sum(here, axis=0, keepdims=True))
    pooled = jnp.concatenate(sums, axis=0) * (4.0 / PIX)
    rows = normalize(pooled, 1.0).astype(jnp.bfloat16)
    for copy in range(ctx_ref.shape[0]):
        ctx_ref[copy] = rows


def hidden_queries(
    slot, pick_ref, before_ref, after_ref, gain_pre_ref, gain_mid_ref, part_hbm, taps_hbm, w_query_hbm,
    hidden_ref, query_ref, part_ref, tap_ref, w_query_ref, sems,
):
    first = (pick_ref[0] == 0) == (slot == 0)
    copies = copy_all(
        [
            (taps_hbm.at[jnp.where(first, 0, 2)], tap_ref),
            (part_hbm, part_ref),
            (w_query_hbm, w_query_ref),
        ],
        sems,
    )
    gain_pre, gain_mid = gain_pre_ref[...], gain_mid_ref[...]
    for copy in copies:
        copy.wait()
    halo = jnp.where(first, before_ref[0], after_ref[0]).astype(jnp.float32)
    norm = normalize(halo, gain_pre).astype(jnp.bfloat16)
    hidden = (part_ref[...] + dot(norm, tap_ref[...])).astype(jnp.bfloat16)
    hidden_ref[...] = hidden
    norm = normalize(hidden.astype(jnp.float32), gain_mid).astype(jnp.bfloat16)
    query_ref[...] = (dot(norm, w_query_ref[...]) * SCALE).T.astype(jnp.bfloat16)


def pair_rows(pair):
    return pl.ds(pl.multiple_of(128 * pair, 128), 128)


def attention(
    pick_ref, near_ref, far_ref, w_key_hbm, w_value_hbm, w_out_hbm, query_0, query_1, hidden_0,
    hidden_1, out_hbm, key_ref, value_ref, mixed_ref, w_both_ref, w_out_ref, query_ref, hidden_ref,
    out_ref, sems, out_sems,
):
    half = ROWS // 2
    moves = copy_all(
        [
            (source.at[:, pl.ds(128 * pair, 128)], w_both_ref.at[:, pl.ds(256 * pair + place, 128)])
            for pair in range(PAIRS)
            for source, place in ((w_key_hbm, 0), (w_value_hbm, 128))
        ]
        + [
            (query_0, query_ref.at[0]),
            (query_1, query_ref.at[1]),
            (w_out_hbm, w_out_ref),
            (hidden_0, hidden_ref.at[0]),
            (hidden_1, hidden_ref.at[1]),
        ],
        sems,
    )

    def context(pair, slot):
        lanes = pl.ds(pl.multiple_of(256 * pair, 256), 256)
        left = lax.broadcasted_iota(jnp.int32, (half, 128), 1) < HEAD_DIM
        for number, ctx_ref in enumerate((near_ref, far_ref)):
            rows = slice(half * number, half * number + half)
            both = dot(ctx_ref[...], w_both_ref[:, lanes])
            keys, values = both[:, :128], both[:, 128:].T.astype(jnp.bfloat16)
            for side in range(2):
                mine = left if side == 0 else ~left
                key_ref[slot, side, rows] = jnp.where(mine, keys, 0.0).astype(jnp.bfloat16)
                value_ref[slot, side, :HEAD_DIM, rows] = values[HEAD_DIM * side :][:HEAD_DIM]

    def project(frame):
        projected = dot(mixed_ref[frame].T, w_out_ref[...])
        out = (hidden_ref[frame].astype(jnp.float32) + projected).astype(jnp.bfloat16)
        out_ref[frame] = out
        place = jnp.where(pick_ref[0] == 0, frame, 1 - frame)
        return copy_all([(out_ref.at[frame], out_hbm.at[place])], out_sems.at[pl.ds(frame, 1)])

    moves, late = moves[: 2 * PAIRS], moves[2 * PAIRS :]
    value_ref[:, :, HEAD_DIM:] = jnp.ones((2, 2, ONES, ROWS), jnp.bfloat16)
    for move in moves + late[:2]:
        move.wait()
    inside = None
    context(0, 0)
    for pair in range(PAIRS):
        if pair + 1 < PAIRS:
            context(pair + 1, (pair + 1) % 2)
        for frame in range(2):
            for side in range(2):
                scores = dot(key_ref[pair % 2, side], query_ref[frame, 128 * pair : 128 * pair + 128])
                weights = jnp.exp2(scores).astype(jnp.bfloat16)
                total = dot(value_ref[pair % 2, side], weights)
                sums = total[HEAD_DIM : HEAD_DIM + 1]
                good = jnp.where((sums >= LOW) & (sums <= HIGH), 1.0, 0.0)
                inside = good if inside is None else jnp.minimum(inside, good)
                head = HEAD_DIM * (2 * pair + side)
                mixed = total[:HEAD_DIM] * (1.0 / sums)
                mixed_ref[frame, head : head + HEAD_DIM] = mixed.astype(jnp.bfloat16)
    for move in late[2:]:
        move.wait()
    writes = project(0) + project(1)
    worst = jnp.min(inside)
    for write in writes:
        write.wait()

    @pl.when(worst < 0.5)
    def _():
        def some_pixels(strip, pair):
            pixels = pl.ds(pl.multiple_of(strip * 128, 128), 128)
            for frame in range(2):
                query = query_ref[frame, pair_rows(pair), pixels]
                for side in range(2):
                    scores = dot(key_ref[0, side], query)
                    weights = jnp.exp2(scores - jnp.max(scores, 0, keepdims=True))
                    total = dot(value_ref[0, side], weights.astype(jnp.bfloat16))
                    mixed = total[:HEAD_DIM] * (1.0 / total[HEAD_DIM : HEAD_DIM + 1])
                    rows = pl.ds(pl.multiple_of(128 * pair + HEAD_DIM * side, HEAD_DIM), HEAD_DIM)
                    mixed_ref[frame, rows, pixels] = mixed.astype(jnp.bfloat16)
            return pair

        def one_pair(pair, carry):
            context(pair, 0)
            lax.fori_loop(0, PIX // 128, some_pixels, pair)
            return carry

        lax.fori_loop(0, PAIRS, one_pair, 0)
        for write in project(0) + project(1):
            write.wait()


def attend(*operands):
    frame, pair, square, half = (PIX, C), (2, PIX, C), (C, C), jnp.bfloat16
    here, there = pl.BlockSpec(memory_space=pltpu.VMEM), pl.BlockSpec(memory_space=pltpu.HBM)
    return call(
        attention,
        "attention",
        jax.ShapeDtypeStruct(pair, half),
        [pl.BlockSpec(memory_space=pltpu.SMEM), here, here] + [there] * 7,
        there,
        2 * 10**10,
        10 * 10**6,
        ATTENTION_VMEM,
        scratch_shapes=[
            pltpu.VMEM((2, 2, ROWS, 128), half),
            pltpu.VMEM((2, 2, HEAD_DIM + ONES, ROWS), half),
            pltpu.VMEM(pair, half),
            pltpu.VMEM((C, 2 * C), half),
            pltpu.VMEM(square, half),
            pltpu.VMEM(pair, half),
            pltpu.VMEM(pair, half),
            pltpu.VMEM(pair, half),
            pltpu.SemaphoreType.DMA((2 * PAIRS + 5,)),
            pltpu.SemaphoreType.DMA((2,)),
        ],
    )(*operands)


def shards(
    latents,
    timestep,
    context_frame,
    gain_pre,
    w_temporal,
    w_time,
    gain_mid,
    w_query,
    w_key,
    w_value,
    w_out,
):
    up = [(i, (i + 1) % 256) for i in range(256)]
    down = [(j, i) for i, j in up]
    after = lax.ppermute(latents[:1], AXES, down)
    before = lax.ppermute(latents[1:], AXES, up)

    gain_pre = gain_pre.reshape(1, C)
    gain_mid = gain_mid.reshape(1, C)
    frame, pair, square = (PIX, C), (2, PIX, C), (C, C)
    half, single = jnp.bfloat16, jnp.float32
    mac = 2 * PIX * C * C
    here, there = pl.BlockSpec(memory_space=pltpu.VMEM), pl.BlockSpec(memory_space=pltpu.HBM)
    scalar = pl.BlockSpec(memory_space=pltpu.SMEM)
    temb = time_bias(timestep, w_time)
    soon_part, part, other_part = call(
        own_taps,
        "own_taps",
        (jax.ShapeDtypeStruct(frame, single),) * 3,
        [scalar, here, here, here, there],
        (here, here, here),
        4 * mac,
        8 * 10**6,
        TAPS_VMEM,
        scratch_shapes=[pltpu.VMEM((2 * C, 2 * C), half), pltpu.SemaphoreType.DMA((4,))],
    )(context_frame, latents, gain_pre, temb, w_temporal)

    row = np.arange(2 * PW)
    left = np.broadcast_to((row % PW < PW // 2)[:, None], (2 * PW, C))
    sides = jnp.asarray(np.concatenate([left, ~left], axis=1), single)
    ctx = call(
        context_rows,
        "context_rows",
        jax.ShapeDtypeStruct((8, 4, C), half),
        [scalar, here, here, here, here, here, here, here],
        here,
        mac,
        8 * 10**6,
        CONTEXT_VMEM,
    )(context_frame, before, after, gain_pre, gain_mid, sides, soon_part, w_temporal)
    def frame_call(slot, frame_part):
        return call(
            functools.partial(hidden_queries, slot),
            "hidden_queries",
            (jax.ShapeDtypeStruct(frame, half), jax.ShapeDtypeStruct(frame, half)),
            [scalar, here, here, here, here, there, there, there],
            (here, here),
            2 * mac,
            6 * 10**6,
            HIDDEN_VMEM,
            scratch_shapes=[
                pltpu.VMEM(frame, single),
                pltpu.VMEM(square, half),
                pltpu.VMEM(square, half),
                pltpu.SemaphoreType.DMA((3,)),
            ],
        )(context_frame, before, after, gain_pre, gain_mid, frame_part, w_temporal, w_query)

    line = exchange(ctx, groups_by(lambda x, y, z, core: (x, y, core))).reshape(32, C)
    hidden_0, query_0 = frame_call(0, part)
    line, hidden_0, query_0 = lax.optimization_barrier((line, hidden_0, query_0))
    plane = exchange(
        jnp.broadcast_to(line[None], (16, 32, C)), groups_by(lambda x, y, z, core: (z, core))
    ).reshape(512, C)
    hidden_1, query_1 = frame_call(1, other_part)
    plane, hidden_1, query_1 = lax.optimization_barrier((plane, hidden_1, query_1))
    swapped = lax.ppermute(plane, AXES, [(i, i ^ 1) for i in range(256)])

    return attend(
        context_frame, plane, swapped, w_key, w_value, w_out, query_0, query_1, hidden_0, hidden_1
    )


def solution(mesh):
    return jax.shard_map(
        shards,
        mesh=mesh,
        in_specs=(
            P(("clip", "group"), None, None),
            P(),
            P(("clip", "group")),
            P(),
            P(),
            P(),
            P(),
            P(),
            P(),
            P(),
            P(),
        ),
        out_specs=P(("clip", "group"), None, None),
        check_vma=False,
    )
```

time: 103 us -> 127 us (1.23)
  Pallas kernels: 59.1 us -> 84.5 us
  starting transfers between devices: 12.8 us -> 27.8 us
  blocking collectives: 14.9 us -> 0 us
  waiting for transfers between devices: 10.3 us -> 6.9 us
  local copies, waits for them, and re-layouts: 2.68 us -> 5.01 us
    pallas_call x3 -> x4, Pallas kernels: 57.4 us -> 82.1 us  [the longest x1 66.1 us: attend(): call(attention, 'attention', jax.ShapeDtypeStruct(pair, half), [pl.BlockS...]
    all_to_all x1 -> x0, blocking collectives: 14.9 us -> none  [exchange(): lax.all_to_all(copies, AXES, 0, 0, axis_index_groups=groups, tiled=False)]
    all_to_all x1 -> x2, starting transfers between devices: 8.09 us -> 17.9 us  [exchange(): lax.all_to_all(copies, AXES, 0, 0, axis_index_groups=groups, tiled=False)]
    ppermute x1, starting transfers between devices: 1.27 us -> 6.51 us  [shards(): swapped = lax.ppermute(plane, AXES, [(i, i ^ 1) for i in range(256)])]
    ppermute x1, waiting for transfers between devices: 3.71 us -> 0.21 us  [shards(): before = lax.ppermute(latents[1:], AXES, up)]
    ppermute x1, starting transfers between devices: 3.1 us -> 0.01 us  [shards(): before = lax.ppermute(latents[1:], AXES, up)]
    ppermute x1, starting transfers between devices: 0.29 us -> 3.31 us  [shards(): after = lax.ppermute(latents[:1], AXES, down)]
    unnamed x24, local copies, waits for them, and re-layouts: 0.06 us -> 2.41 us
  transfers between devices with their start and end apart: 4 -> 5, of which waited for: 4 -> 5; matrix products, arithmetic and copies ran while one was open for 1% -> 1% of each run, Pallas kernels for 12% -> 13%
where the time goes in v5:
time: 127 us
  Pallas kernels  84.5 us (67%)
  starting transfers between devices  27.8 us (22%)
  waiting for transfers between devices  6.9 us (5%)
  local copies, waits for them, and re-layouts  5.01 us (4%)
  between operations  1.63 us (1%)
    pallas_call x1, Pallas kernels, attend(): call(attention, 'attention', jax.ShapeDtypeStruct(pair, half), [pl.BlockS...  66.1 us
    all_to_all x2, starting transfers between devices, exchange(): lax.all_to_all(copies, AXES, 0, 0, axis_index_groups=groups, tiled=False)  17.9 us
    pallas_call x2, Pallas kernels, frame_call(): call(functools.partial(hidden_queries, slot), 'hidden_queries', (jax.Shap...  13.1 us
    ppermute x1, starting transfers between devices, shards(): swapped = lax.ppermute(plane, AXES, [(i, i ^ 1) for i in range(256)])  6.51 us
    ppermute x1, starting transfers between devices, shards(): after = lax.ppermute(latents[:1], AXES, down)  3.31 us
    pallas_call x1, Pallas kernels, shards(): call(own_taps, 'own_taps', (jax.ShapeDtypeStruct(frame, single),) * 3, [s...  2.91 us
    all_to_all x2, waiting for transfers between devices, exchange(): lax.all_to_all(copies, AXES, 0, 0, axis_index_groups=groups, tiled=False)  2.87 us
  transfers between devices with their start and end apart: 5, of which 5 were waited for; matrix products, arithmetic and copies ran while one was open for 1% of the time, Pallas kernels for 13%

profile of v5, /device:TPU:1, one launch (start us, length us, event | category | flops | bytes accessed | tf_op | source)
XLA Modules:
  0.0 126.9 jit_solution(13410556678449405812)
XLA Ops:
  0.0 0.0 copy-start
  0.0 0.0 copy-start.1
  0.0 1.7 %fusion.2 = (bf16[1,640,640]{2,1,0:T(8,128)(2,1)S(1)}, bf16[1,640,640]{2,1,0:T(8,128)(2,1)S(1)}) fusion(bf16[2,640,640]{2,1,0:T(8,128)(2,1)} %latents_ref.1), kind=kLoop, calls=%fused_computation.5 | loop fusion | bytes 3276800 | tf_op jit(solution)/shard_map/slice | solution.py:309
  1.7 0.0 copy-start.4
  1.7 3.3 %collective-permute-start.1 = (bf16[1,640,640]{2,1,0:T(8,128)(2,1)S(1)}, bf16[1,640,640]{2,1,0:T(8,128)(2,1)S(1)}, u32[]{:S(2)}, u32[]{:S(2)}) collective-permute-start(bf16[1,640,640]{2,1,0:T(8,128)(2,1)S(1)} %get-tuple-element.31), channel_id=1, source_target_pairs={{1,0},{2,1},{3,2},{4,3},{5,4},{6,5},{7,6},{8,7},{9,8},{10,9},{11,1... | collective-permute-start | bytes 2457608 | tf_op jit(solution)/shard_map/ppermute | solution.py:309
  5.0 0.0 collective-permute-start
  6.3 0.0 copy-done.10
  6.4 0.0 copy-done.11
  6.4 0.0 copy-start.8
  6.4 0.0 copy-start.9
  6.4 0.1 fusion
  6.5 0.1 divide_multiply_fusion
  6.6 0.9 fusion.3.temb_ref
  7.5 0.0 copy-done.4
  7.5 0.0 copy-start.7
  7.5 2.9 %own_taps.1 = (f32[640,640]{1,0:T(8,128)S(1)}, f32[640,640]{1,0:T(8,128)S(1)}, f32[640,640]{1,0:T(8,128)S(1)}) custom-call(s32[1]{0:T(128)S(6)} %copy.14.pick_ref, bf16[2,640,640]{2,1,0:T(8,128)(2,1)S(1)} %copy-done.4, f32[1,640]{1,0:T(1,128)S(1)} %reshape.21.gain_ref.gain_pre_ref, f32[1,640]{1,0:T(1,128)S(1)} %fusion.3.temb_ref, ...), custom_call_target="tpu_custom_call" | custom-call | flops 2097152000 | bytes 8000000 | tf_op jit(solution)/shard_map/own_taps/pallas_call | solution.py:320
  10.4 0.0 copy-start.5
  10.4 1.2 copy-done.5
  11.6 1.2 copy-done.6
  12.8 2.1 %collective-permute-done.1.after_ref = bf16[1,640,640]{2,1,0:T(8,128)(2,1)S(1)} collective-permute-done((bf16[1,640,640]{2,1,0:T(8,128)(2,1)S(1)}, bf16[1,640,640]{2,1,0:T(8,128)(2,1)S(1)}, u32[]{:S(2)}, u32[]{:S(2)}) %collective-permute-start.1) | collective-permute-done | bytes 819232 | tf_op jit(solution)/shard_map/ppermute | solution.py:309
  14.9 0.2 collective-permute-done.before_ref
  15.1 2.4 %context_rows.1 = bf16[8,4,640]{2,1,0:T(4,128)(2,1)} custom-call(s32[1]{0:T(128)S(6)} %copy.14.pick_ref, bf16[1,640,640]{2,1,0:T(8,128)(2,1)S(1)} %collective-permute-done.before_ref, bf16[1,640,640]{2,1,0:T(8,128)(2,1)S(1)} %collective-permute-done.1.after_ref, f32[1,640]{1,0:T(1,128)S(1)} %reshape.21.gain_ref.gain_pre_ref, ...), custom_call_target="tpu_custom_call" | custom-call | flops 524288000 | bytes 8000000 | tf_op jit(solution)/shard_map/context_rows/pallas_call | solution.py:335
  17.5 9.8 %all-to-all-start = ((bf16[8,4,640]{2,1,0:T(4,128)(2,1)}), bf16[8,4,640]{2,1,0:T(4,128)(2,1)S(1)}, u32[]{:S(2)}, u32[]{:S(2)}) async-start(bf16[8,4,640]{2,1,0:T(4,128)(2,1)} %context_rows.1), calls=%async_computation | async-start | bytes 81920 | tf_op jit(solution)/shard_map/all_to_all | solution.py:47
  27.3 6.6 %hidden_queries.2 = (bf16[640,640]{1,0:T(8,128)(2,1)}, bf16[640,640]{1,0:T(8,128)(2,1)}) custom-call(s32[1]{0:T(128)S(6)} %copy.14.pick_ref, bf16[1,640,640]{2,1,0:T(8,128)(2,1)} %copy-done.3, bf16[1,640,640]{2,1,0:T(8,128)(2,1)} %copy-done.2, f32[1,640]{1,0:T(1,128)} %copy-done.8, f32[1,640]{1,0:T(1,128)} %copy-done.9, f32[640,640]{1,0:T(8,128)} %copy-done.6, ...), custom_call_target="tpu_custom_call" | custom-call | flops 1048576000 | bytes 6000000 | tf_op jit(solution)/shard_map/hidden_queries/pallas_call | solution.py:346
  33.9 0.4 all-to-all-done
  34.3 0.9 broadcast_in_dim.2
  35.2 8.1 %all-to-all-start.1 = ((bf16[16,32,640]{2,1,0:T(8,128)(2,1)}), bf16[16,32,640]{2,1,0:T(8,128)(2,1)S(1)}, u32[]{:S(2)}, u32[]{:S(2)}) async-start(bf16[16,32,640]{2,1,0:T(8,128)(2,1)} %broadcast_in_dim.2), calls=%async_computation.1 | async-start | bytes 1310720 | tf_op jit(solution)/shard_map/all_to_all | solution.py:47
  43.3 6.6 %hidden_queries.3 = (bf16[640,640]{1,0:T(8,128)(2,1)}, bf16[640,640]{1,0:T(8,128)(2,1)}) custom-call(s32[1]{0:T(128)S(6)} %copy.14.pick_ref, bf16[1,640,640]{2,1,0:T(8,128)(2,1)} %copy-done.3, bf16[1,640,640]{2,1,0:T(8,128)(2,1)} %copy-done.2, f32[1,640]{1,0:T(1,128)} %copy-done.8, f32[1,640]{1,0:T(1,128)} %copy-done.9, f32[640,640]{1,0:T(8,128)} %copy-done.5, ...), custom_call_target="tpu_custom_call" | custom-call | flops 1048576000 | bytes 6000000 | tf_op jit(solution)/shard_map/hidden_queries/pallas_call | solution.py:346
  49.9 2.5 %all-to-all-done.1 = bf16[16,32,640]{2,1,0:T(8,128)(2,1)S(1)} async-done(((bf16[16,32,640]{2,1,0:T(8,128)(2,1)}), bf16[16,32,640]{2,1,0:T(8,128)(2,1)S(1)}, u32[]{:S(2)}, u32[]{:S(2)}) %all-to-all-start.1) | async-done | bytes 655392 | tf_op jit(solution)/shard_map/all_to_all | solution.py:47
  52.4 6.5 %collective-permute-start.2 = (bf16[512,640]{1,0:T(8,128)(2,1)S(1)}, bf16[512,640]{1,0:T(8,128)(2,1)S(1)}, u32[]{:S(2)}, u32[]{:S(2)}) collective-permute-start(bf16[512,640]{1,0:T(8,128)(2,1)S(1)} %bitcast.4), channel_id=1, source_target_pairs={{0,1},{1,0},{2,3},{3,2},{4,5},{5,4},{6,7},{7,6},{8,9},{9,8},{10,11... | collective-permute-start | bytes 1966088 | tf_op jit(solution)/shard_map/ppermute | solution.py:371
  58.9 1.7 %collective-permute-done.2.far_ref = bf16[512,640]{1,0:T(8,128)(2,1)S(1)} collective-permute-done((bf16[512,640]{1,0:T(8,128)(2,1)S(1)}, bf16[512,640]{1,0:T(8,128)(2,1)S(1)}, u32[]{:S(2)}, u32[]{:S(2)}) %collective-permute-start.2) | collective-permute-done | bytes 655392 | tf_op jit(solution)/shard_map/ppermute | solution.py:371
  60.6 66.1 %attention.1 = bf16[2,640,640]{2,1,0:T(8,128)(2,1)} custom-call(s32[1]{0:T(128)S(6)} %copy.14.pick_ref, bf16[512,640]{1,0:T(8,128)(2,1)S(1)} %bitcast.5, bf16[512,640]{1,0:T(8,128)(2,1)S(1)} %collective-permute-done.2.far_ref, bf16[640,640]{1,0:T(8,128)(2,1)} %w_key_hbm.1, bf16[640,640]{1,0:T(8,128)(2,1)} %w_value_hbm.1, bf16[640,640]{1,0:T(8,128)(2,1)} %w_out_hbm.1, ...), custom_call_target="tpu_custom_call" | custom-call | flops 20000000000 | bytes 10000000 | tf_op jit(solution)/shard_map/attention/pallas_call | solution.py:270
  (16 shorter events, 0.1 us)
Async XLA Ops:
  0.0 6.5 %copy-start = (f32[640,640]{1,0:T(8,128)S(1)}, f32[640,640]{1,0:T(8,128)}, u32[]{:S(2)}) copy-start(f32[640,640]{1,0:T(8,128)} %param.17) | copy-start | bytes 4915204
  0.0 6.3 %copy-start.10 = (f32[640]{0:T(1024)S(1)}, f32[640]{0:T(1024)}, u32[]{:S(2)}) copy-start(f32[640]{0:T(1024)} %param.15) | copy-start | bytes 7684
  0.0 6.4 %copy-start.11 = (f32[640]{0:T(1024)S(1)}, f32[640]{0:T(1024)}, u32[]{:S(2)}) copy-start(f32[640]{0:T(1024)} %param.18) | copy-start | bytes 7684
  0.0 7.4 %copy-start.1 = (bf16[3,640,640]{2,1,0:T(8,128)(2,1)S(1)}, bf16[3,640,640]{2,1,0:T(8,128)(2,1)}, u32[]{:S(2)}) copy-start(bf16[3,640,640]{2,1,0:T(8,128)(2,1)} %taps_hbm.3) | copy-start | bytes 7372804
  1.7 5.7 %copy-start.4 = (bf16[2,640,640]{2,1,0:T(8,128)(2,1)S(1)}, bf16[2,640,640]{2,1,0:T(8,128)(2,1)}, u32[]{:S(2)}) copy-start(bf16[2,640,640]{2,1,0:T(8,128)(2,1)} %latents_ref.1) | copy-start | bytes 4915204
  1.7 13.1 %collective-permute-start.1 = (bf16[1,640,640]{2,1,0:T(8,128)(2,1)S(1)}, bf16[1,640,640]{2,1,0:T(8,128)(2,1)S(1)}, u32[]{:S(2)}, u32[]{:S(2)}) collective-permute-start(bf16[1,640,640]{2,1,0:T(8,128)(2,1)S(1)} %get-tuple-element.31), channel_id=1, source_target_pairs={{1,0},{2,1},{3,2},{4,3},{5,4},{6,5},{7,6},{8,7},{9,8},{10,9},{11,1... | collective-permute-start | bytes 2457608 | tf_op jit(solution)/shard_map/ppermute | solution.py:309
  5.0 10.0 %collective-permute-start = (bf16[1,640,640]{2,1,0:T(8,128)(2,1)S(1)}, bf16[1,640,640]{2,1,0:T(8,128)(2,1)S(1)}, u32[]{:S(2)}, u32[]{:S(2)}) collective-permute-start(bf16[1,640,640]{2,1,0:T(8,128)(2,1)S(1)} %get-tuple-element.32), channel_id=1, source_target_pairs={{0,1},{1,2},{2,3},{3,4},{4,5},{5,6},{6,7},{7,8},{8,9},{9,10},{10,1... | collective-permute-start | bytes 2457608 | tf_op jit(solution)/shard_map/ppermute | solution.py:310
  6.4 8.7 %copy-start.8 = (f32[1,640]{1,0:T(1,128)}, f32[1,640]{1,0:T(1,128)S(1)}, u32[]{:S(2)}) copy-start(f32[1,640]{1,0:T(1,128)S(1)} %reshape.21.gain_ref.gain_pre_ref) | copy-start | bytes 7684
  6.4 8.7 %copy-start.9 = (f32[1,640]{1,0:T(1,128)}, f32[1,640]{1,0:T(1,128)S(1)}, u32[]{:S(2)}) copy-start(f32[1,640]{1,0:T(1,128)S(1)} %reshape.22.gain_mid_ref) | copy-start | bytes 7684
  7.5 7.6 %copy-start.7 = (f32[40,1280]{1,0:T(8,128)S(1)}, f32[40,1280]{1,0:T(8,128)}, u32[]{:S(2)}) copy-start(f32[40,1280]{1,0:T(8,128)} %constant.10.clone.side_ref) | copy-start | bytes 614404
  10.4 1.2 copy-start.5
  11.6 1.2 copy-start.6
  14.9 2.6 %copy-start.2 = (bf16[1,640,640]{2,1,0:T(8,128)(2,1)}, bf16[1,640,640]{2,1,0:T(8,128)(2,1)S(1)}, u32[]{:S(2)}) copy-start(bf16[1,640,640]{2,1,0:T(8,128)(2,1)S(1)} %collective-permute-done.1.after_ref) | copy-start | bytes 2457604
  15.1 2.4 %copy-start.3 = (bf16[1,640,640]{2,1,0:T(8,128)(2,1)}, bf16[1,640,640]{2,1,0:T(8,128)(2,1)S(1)}, u32[]{:S(2)}) copy-start(bf16[1,640,640]{2,1,0:T(8,128)(2,1)S(1)} %collective-permute-done.before_ref) | copy-start | bytes 2457604
  17.5 16.8 %all-to-all-start = ((bf16[8,4,640]{2,1,0:T(4,128)(2,1)}), bf16[8,4,640]{2,1,0:T(4,128)(2,1)S(1)}, u32[]{:S(2)}, u32[]{:S(2)}) async-start(bf16[8,4,640]{2,1,0:T(4,128)(2,1)} %context_rows.1), calls=%async_computation | async-start | bytes 81920 | tf_op jit(solution)/shard_map/all_to_all | solution.py:47
  35.2 17.2 %all-to-all-start.1 = ((bf16[16,32,640]{2,1,0:T(8,128)(2,1)}), bf16[16,32,640]{2,1,0:T(8,128)(2,1)S(1)}, u32[]{:S(2)}, u32[]{:S(2)}) async-start(bf16[16,32,640]{2,1,0:T(8,128)(2,1)} %broadcast_in_dim.2), calls=%async_computation.1 | async-start | bytes 1310720 | tf_op jit(solution)/shard_map/all_to_all | solution.py:47
  52.4 8.2 %collective-permute-start.2 = (bf16[512,640]{1,0:T(8,128)(2,1)S(1)}, bf16[512,640]{1,0:T(8,128)(2,1)S(1)}, u32[]{:S(2)}, u32[]{:S(2)}) collective-permute-start(bf16[512,640]{1,0:T(8,128)(2,1)S(1)} %bitcast.4), channel_id=1, source_target_pairs={{0,1},{1,0},{2,3},{3,2},{4,5},{5,4},{6,7},{7,6},{8,9},{9,8},{10,11... | collective-permute-start | bytes 1966088 | tf_op jit(solution)/shard_map/ppermute | solution.py:371

commit v6 on v5

--- a/solution.py
+++ b/solution.py
@@ -17,6 +17,7 @@
 PAIRS = C // (2 * HEAD_DIM)
 ROWS = 1024
 ONES = 16
+PARTS = (slice(0, 384), slice(384, PIX))
 STRIP = 320
 AXES = ("clip", "group")
 MIB = 2**20
@@ -120,16 +121,17 @@
 
 
 def context_rows(
-    pick_ref, before_ref, after_ref, gain_pre_ref, gain_mid_ref, side_ref, part_ref, taps_ref, ctx_ref
+    pick_ref, apart_ref, beside_ref, beyond_ref, gain_pre_ref, gain_mid_ref, side_ref, part_ref,
+    taps_ref, ctx_ref,
 ):
-    first = pick_ref[0] == 0
-    tap = jnp.where(first, 0, 2)
+    tap = jnp.where(pick_ref[0] == 0, 0, 2)
+    far = apart_ref[0] == 1
     gain_pre, gain_mid = gain_pre_ref[...], gain_mid_ref[...]
     tile = side_ref.shape[0]
     sums = []
     for half in range(2):
         rows = slice(half * PIX // 2, (half + 1) * PIX // 2)
-        halo = jnp.where(first, before_ref[0, rows], after_ref[0, rows]).astype(jnp.float32)
+        halo = jnp.where(far, beyond_ref[0, rows], beside_ref[0, rows]).astype(jnp.float32)
         norm = normalize(halo, gain_pre).astype(jnp.bfloat16)
         hidden = (part_ref[rows] + dot(norm, taps_ref[tap])).astype(jnp.bfloat16)
         norm = normalize(hidden.astype(jnp.float32), gain_mid).astype(jnp.bfloat16)
@@ -144,27 +146,36 @@
 
 
 def hidden_queries(
-    slot, pick_ref, before_ref, after_ref, gain_pre_ref, gain_mid_ref, part_hbm, taps_hbm, w_query_hbm,
-    hidden_ref, query_ref, part_ref, tap_ref, w_query_ref, sems,
+    slot, pick_ref, apart_ref, gain_pre_ref, gain_mid_ref, beside_hbm, beyond_hbm, part_hbm, taps_hbm,
+    w_query_hbm, hidden_hbm, query_hbm, halo_ref, part_ref, tap_ref, w_query_ref, hidden_ref, query_ref, sems,
+    out_sems,
 ):
-    first = (pick_ref[0] == 0) == (slot == 0)
-    copies = copy_all(
+    tap = jnp.where((pick_ref[0] == 0) == (slot == 0), 0, 2)
+    far = (apart_ref[0] == 1) == (slot == 0)
+    halo_copy = pltpu.make_async_copy(beyond_hbm.at[0], halo_ref, sems.at[3])
+    pl.when(far)(halo_copy.start)
+    pl.when(~far)(pltpu.make_async_copy(beside_hbm.at[0], halo_ref, sems.at[3]).start)
+    tap_copy, part_copy, query_copy = copy_all(
         [
-            (taps_hbm.at[jnp.where(first, 0, 2)], tap_ref),
+            (taps_hbm.at[tap], tap_ref),
             (part_hbm, part_ref),
             (w_query_hbm, w_query_ref),
         ],
         sems,
     )
     gain_pre, gain_mid = gain_pre_ref[...], gain_mid_ref[...]
-    for copy in copies:
+    halo_copy.wait()
+    norm = normalize(halo_ref[...].astype(jnp.float32), gain_pre).astype(jnp.bfloat16)
+    tap_copy.wait()
+    part_copy.wait()
+    query_copy.wait()
+    for rows in PARTS:
+        hidden = (part_ref[rows] + dot(norm[rows], tap_ref[...])).astype(jnp.bfloat16)
+        hidden_ref[rows] = hidden
+        later = normalize(hidden.astype(jnp.float32), gain_mid).astype(jnp.bfloat16)
+        query_ref[:, rows] = (dot(later, w_query_ref[...]) * SCALE).T.astype(jnp.bfloat16)
+    for copy in copy_all([(hidden_ref, hidden_hbm), (query_ref, query_hbm)], out_sems):
         copy.wait()
-    halo = jnp.where(first, before_ref[0], after_ref[0]).astype(jnp.float32)
-    norm = normalize(halo, gain_pre).astype(jnp.bfloat16)
-    hidden = (part_ref[...] + dot(norm, tap_ref[...])).astype(jnp.bfloat16)
-    hidden_ref[...] = hidden
-    norm = normalize(hidden.astype(jnp.float32), gain_mid).astype(jnp.bfloat16)
-    query_ref[...] = (dot(norm, w_query_ref[...]) * SCALE).T.astype(jnp.bfloat16)
 
 
 def pair_rows(pair):
@@ -304,10 +315,14 @@
     w_value,
     w_out,
 ):
-    up = [(i, (i + 1) % 256) for i in range(256)]
-    down = [(j, i) for i, j in up]
-    after = lax.ppermute(latents[:1], AXES, down)
-    before = lax.ppermute(latents[1:], AXES, up)
+    core = lax.axis_index("group") % 2
+    pick = jnp.where(context_frame == 0, 0, 1)
+    apart = jnp.where(pick == core, 1, 0)
+    abroad = [(i, (i + 1) % 256 if i % 2 else (i - 1) % 256) for i in range(256)]
+    beyond = lax.ppermute(lax.dynamic_slice_in_dim(latents, core, 1, 0), AXES, abroad)
+    beside = lax.ppermute(
+        lax.dynamic_slice_in_dim(latents, 1 - core, 1, 0), AXES, [(i, i ^ 1) for i in range(256)]
+    )
 
     gain_pre = gain_pre.reshape(1, C)
     gain_mid = gain_mid.reshape(1, C)
@@ -327,7 +342,7 @@
         8 * 10**6,
         TAPS_VMEM,
         scratch_shapes=[pltpu.VMEM((2 * C, 2 * C), half), pltpu.SemaphoreType.DMA((4,))],
-    )(context_frame, latents, gain_pre, temb, w_temporal)
+    )(pick, latents, gain_pre, temb, w_temporal)
 
     row = np.arange(2 * PW)
     left = np.broadcast_to((row % PW < PW // 2)[:, None], (2 * PW, C))
@@ -336,29 +351,33 @@
         context_rows,
         "context_rows",
         jax.ShapeDtypeStruct((8, 4, C), half),
-        [scalar, here, here, here, here, here, here, here],
+        [scalar, scalar, here, here, here, here, here, here, here],
         here,
         mac,
         8 * 10**6,
         CONTEXT_VMEM,
-    )(context_frame, before, after, gain_pre, gain_mid, sides, soon_part, w_temporal)
+    )(pick, apart, beside, beyond, gain_pre, gain_mid, sides, soon_part, w_temporal)
     def frame_call(slot, frame_part):
         return call(
             functools.partial(hidden_queries, slot),
             "hidden_queries",
             (jax.ShapeDtypeStruct(frame, half), jax.ShapeDtypeStruct(frame, half)),
-            [scalar, here, here, here, here, there, there, there],
-            (here, here),
+            [scalar, scalar, here, here, there, there, there, there, there],
+            (there, there),
             2 * mac,
             6 * 10**6,
             HIDDEN_VMEM,
             scratch_shapes=[
+                pltpu.VMEM(frame, half),
                 pltpu.VMEM(frame, single),
                 pltpu.VMEM(square, half),
                 pltpu.VMEM(square, half),
-                pltpu.SemaphoreType.DMA((3,)),
+                pltpu.VMEM(frame, half),
+                pltpu.VMEM(frame, half),
+                pltpu.SemaphoreType.DMA((4,)),
+                pltpu.SemaphoreType.DMA((2,)),
             ],
-        )(context_frame, before, after, gain_pre, gain_mid, frame_part, w_temporal, w_query)
+        )(pick, apart, gain_pre, gain_mid, beside, beyond, frame_part, w_temporal, w_query)
 
     line = exchange(ctx, groups_by(lambda x, y, z, core: (x, y, core))).reshape(32, C)
     hidden_0, query_0 = frame_call(0, part)
@@ -371,7 +390,7 @@
     swapped = lax.ppermute(plane, AXES, [(i, i ^ 1) for i in range(256)])
 
     return attend(
-        context_frame, plane, swapped, w_key, w_value, w_out, query_0, query_1, hidden_0, hidden_1
+        pick, plane, swapped, w_key, w_value, w_out, query_0, query_1, hidden_0, hidden_1
     )
 
 

time: 127 us -> 125 us (0.984)
  starting transfers between devices: 27.8 us -> 24.7 us
    ppermute x2, starting transfers between devices: 3.31 us -> 11.5 us  [the longest x1 8.42 us: shards(): lax.ppermute(lax.dynamic_slice_in_dim(latents, 1 - core, 1, 0), AXES, [(i...]
    all_to_all x2, starting transfers between devices: 17.9 us -> 11.8 us  [exchange(): lax.all_to_all(copies, AXES, 0, 0, axis_index_groups=groups, tiled=False)]
    ppermute x1, starting transfers between devices: 6.51 us -> 1.33 us  [shards(): swapped = lax.ppermute(plane, AXES, [(i, i ^ 1) for i in range(256)])]
    all_to_all x2, waiting for transfers between devices: 2.87 us -> 6.32 us  [exchange(): lax.all_to_all(copies, AXES, 0, 0, axis_index_groups=groups, tiled=False)]
    ppermute x2, waiting for transfers between devices: 2.31 us -> 0.01 us  [the longest x1 0.01 us: shards(): lax.ppermute(lax.dynamic_slice_in_dim(latents, core, 1, 0), AXES, abroad)]
    dynamic_slice x0 -> x1, local copies, waits for them, and re-layouts: none -> 1.69 us  [shards(): lax.dynamic_slice_in_dim(latents, core, 1, 0)]
    slice x1 -> x0, local copies, waits for them, and re-layouts: 1.69 us -> none  [shards(): after = lax.ppermute(latents[:1], AXES, down)]
  transfers between devices with their start and end apart: 5 -> 5, of which waited for: 5 -> 3; matrix products, arithmetic and copies ran while one was open for 1% -> 1% of each run, Pallas kernels for 13% -> 12%
where the time goes in v6:
time: 125 us; the launch traced here: 124 us
  Pallas kernels  83.8 us (67%)
  starting transfers between devices  24.7 us (20%)
  waiting for transfers between devices  8.05 us (6%)
  local copies, waits for them, and re-layouts  5.02 us (4%)
  between operations  1.67 us (1%)
    pallas_call x1, Pallas kernels, attend(): call(attention, 'attention', jax.ShapeDtypeStruct(pair, half), [pl.BlockS...  66.1 us
    pallas_call x2, Pallas kernels, frame_call(): call(functools.partial(hidden_queries, slot), 'hidden_queries', (jax.Shap...  12.3 us
    all_to_all x2, starting transfers between devices, exchange(): lax.all_to_all(copies, AXES, 0, 0, axis_index_groups=groups, tiled=False)  11.8 us
    ppermute x1, starting transfers between devices, shards(): lax.ppermute(lax.dynamic_slice_in_dim(latents, 1 - core, 1, 0), AXES, [(i...  8.42 us
    all_to_all x2, waiting for transfers between devices, exchange(): lax.all_to_all(copies, AXES, 0, 0, axis_index_groups=groups, tiled=False)  6.32 us
    ppermute x1, starting transfers between devices, shards(): lax.ppermute(lax.dynamic_slice_in_dim(latents, core, 1, 0), AXES, abroad)  3.11 us
    pallas_call x1, Pallas kernels, shards(): call(own_taps, 'own_taps', (jax.ShapeDtypeStruct(frame, single),) * 3, [s...  2.95 us
  transfers between devices with their start and end apart: 5, of which 3 were waited for; matrix products, arithmetic and copies ran while one was open for 1% of the time, Pallas kernels for 12%

profile of v6, /device:TPU:1, one launch (start us, length us, event | category | flops | bytes accessed | tf_op | source)
XLA Modules:
  0.0 124.3 jit_solution(2728762664635238411)
XLA Ops:
  0.0 0.0 copy-start
  0.0 0.0 copy-start.1
  0.0 1.7 %constant_dynamic-slice_fusion = (bf16[1,640,640]{2,1,0:T(8,128)(2,1)S(1)}, bf16[1,640,640]{2,1,0:T(8,128)(2,1)S(1)}) fusion(bf16[2,640,640]{2,1,0:T(8,128)(2,1)} %latents_ref.1, s32[]{:T(128)S(6)} %select_n.24, s32[]{:T(128)S(6)} %select_n.23), kind=kLoop, calls=%fused_computation.5 | loop fusion | bytes 3276808 | tf_op jit(solution)/shard_map/dynamic_slice | solution.py:322
  1.7 0.0 copy-start.4
  1.7 3.1 %collective-permute-start.1 = (bf16[1,640,640]{2,1,0:T(8,128)(2,1)S(1)}, bf16[1,640,640]{2,1,0:T(8,128)(2,1)S(1)}, u32[]{:S(2)}, u32[]{:S(2)}) collective-permute-start(bf16[1,640,640]{2,1,0:T(8,128)(2,1)S(1)} %get-tuple-element.31), channel_id=1, source_target_pairs={{0,255},{1,2},{2,1},{3,4},{4,3},{5,6},{6,5},{7,8},{8,7},{9,10},{10... | collective-permute-start | bytes 2457608 | tf_op jit(solution)/shard_map/ppermute | solution.py:322
  4.8 8.4 %collective-permute-start = (bf16[1,640,640]{2,1,0:T(8,128)(2,1)S(1)}, bf16[1,640,640]{2,1,0:T(8,128)(2,1)S(1)}, u32[]{:S(2)}, u32[]{:S(2)}) collective-permute-start(bf16[1,640,640]{2,1,0:T(8,128)(2,1)S(1)} %get-tuple-element.32), channel_id=1, source_target_pairs={{0,1},{1,0},{2,3},{3,2},{4,5},{5,4},{6,7},{7,6},{8,9},{9,8},{10,11... | collective-permute-start | bytes 2457608 | tf_op jit(solution)/shard_map/ppermute | solution.py:323
  14.6 0.0 copy-done.10
  14.6 0.1 fusion
  14.7 0.1 divide_multiply_fusion
  14.8 0.0 copy-done
  14.8 0.9 fusion.2.temb_ref
  15.7 0.0 copy-start.7
  15.7 3.0 %own_taps.1 = (f32[640,640]{1,0:T(8,128)S(1)}, f32[640,640]{1,0:T(8,128)S(1)}, f32[640,640]{1,0:T(8,128)S(1)}) custom-call(s32[1]{0:T(128)S(6)} %select_n.20.pick_ref, bf16[2,640,640]{2,1,0:T(8,128)(2,1)S(1)} %copy-done.4, f32[1,640]{1,0:T(1,128)S(1)} %reshape.21.gain_ref.gain_pre_ref, f32[1,640]{1,0:T(1,128)S(1)} %fusion.2.temb_ref, ...), custom_call_target="tpu_custom_call" | custom-call | flops 2097152000 | bytes 8000000 | tf_op jit(solution)/shard_map/own_taps/pallas_call | solution.py:335
  18.7 1.2 copy-done.5
  19.9 1.2 copy-done.6
  21.0 0.0 collective-permute-done.1.beyond_ref.beyond_hbm
  21.0 0.0 collective-permute-done.beside_ref.beside_hbm
  21.0 0.0 copy-start.3
  21.1 0.0 copy-done.8
  21.1 0.0 copy-done.9
  21.1 0.0 copy-done.7
  21.1 2.4 %context_rows.1 = bf16[8,4,640]{2,1,0:T(4,128)(2,1)} custom-call(s32[1]{0:T(128)S(6)} %select_n.20.pick_ref, s32[1]{0:T(128)S(6)} %select_n.22.apart_ref, bf16[1,640,640]{2,1,0:T(8,128)(2,1)S(1)} %collective-permute-done.beside_ref.beside_hbm, bf16[1,640,640]{2,1,0:T(8,128)(2,1)S(1)} %collective-permute-done.1.beyond_ref.beyond_hbm, ...), custom_call_target="tpu_custom_call" | custom-call | flops 524288000 | bytes 8000000 | tf_op jit(solution)/shard_map/context_rows/pallas_call | solution.py:350
  23.5 3.8 %all-to-all-start = ((bf16[8,4,640]{2,1,0:T(4,128)(2,1)}), bf16[8,4,640]{2,1,0:T(4,128)(2,1)S(1)}, u32[]{:S(2)}, u32[]{:S(2)}) async-start(bf16[8,4,640]{2,1,0:T(4,128)(2,1)} %context_rows.1), calls=%async_computation | async-start | bytes 81920 | tf_op jit(solution)/shard_map/all_to_all | solution.py:48
  27.3 6.1 %hidden_queries.2 = (bf16[640,640]{1,0:T(8,128)(2,1)}, bf16[640,640]{1,0:T(8,128)(2,1)}) custom-call(s32[1]{0:T(128)S(6)} %select_n.20.pick_ref, s32[1]{0:T(128)S(6)} %select_n.22.apart_ref, f32[1,640]{1,0:T(1,128)} %copy-done.8, f32[1,640]{1,0:T(1,128)} %copy-done.9, bf16[1,640,640]{2,1,0:T(8,128)(2,1)} %copy-done.3, bf16[1,640,640]{2,1,0:T(8,128)(2,1)} %copy-done.2, ...), custom_call_target="tpu_custom_call" | custom-call | flops 1048576000 | bytes 6000000 | tf_op jit(solution)/shard_map/hidden_queries/pallas_call | solution.py:361
  33.5 0.9 all-to-all-done
  34.4 0.9 broadcast_in_dim.8
  35.3 8.0 %all-to-all-start.1 = ((bf16[16,32,640]{2,1,0:T(8,128)(2,1)}), bf16[16,32,640]{2,1,0:T(8,128)(2,1)S(1)}, u32[]{:S(2)}, u32[]{:S(2)}) async-start(bf16[16,32,640]{2,1,0:T(8,128)(2,1)} %broadcast_in_dim.8), calls=%async_computation.1 | async-start | bytes 1310720 | tf_op jit(solution)/shard_map/all_to_all | solution.py:48
  43.3 6.1 %hidden_queries.3 = (bf16[640,640]{1,0:T(8,128)(2,1)}, bf16[640,640]{1,0:T(8,128)(2,1)}) custom-call(s32[1]{0:T(128)S(6)} %select_n.20.pick_ref, s32[1]{0:T(128)S(6)} %select_n.22.apart_ref, f32[1,640]{1,0:T(1,128)} %copy-done.8, f32[1,640]{1,0:T(1,128)} %copy-done.9, bf16[1,640,640]{2,1,0:T(8,128)(2,1)} %copy-done.3, bf16[1,640,640]{2,1,0:T(8,128)(2,1)} %copy-done.2, ...), custom_call_target="tpu_custom_call" | custom-call | flops 1048576000 | bytes 6000000 | tf_op jit(solution)/shard_map/hidden_queries/pallas_call | solution.py:361
  49.5 5.4 %all-to-all-done.1 = bf16[16,32,640]{2,1,0:T(8,128)(2,1)S(1)} async-done(((bf16[16,32,640]{2,1,0:T(8,128)(2,1)}), bf16[16,32,640]{2,1,0:T(8,128)(2,1)S(1)}, u32[]{:S(2)}, u32[]{:S(2)}) %all-to-all-start.1) | async-done | bytes 655392 | tf_op jit(solution)/shard_map/all_to_all | solution.py:48
  54.9 1.3 %collective-permute-start.2 = (bf16[512,640]{1,0:T(8,128)(2,1)S(1)}, bf16[512,640]{1,0:T(8,128)(2,1)S(1)}, u32[]{:S(2)}, u32[]{:S(2)}) collective-permute-start(bf16[512,640]{1,0:T(8,128)(2,1)S(1)} %bitcast.5), channel_id=1, source_target_pairs={{0,1},{1,0},{2,3},{3,2},{4,5},{5,4},{6,7},{7,6},{8,9},{9,8},{10,11... | collective-permute-start | bytes 1966088 | tf_op jit(solution)/shard_map/ppermute | solution.py:390
  56.2 1.7 %collective-permute-done.2.far_ref = bf16[512,640]{1,0:T(8,128)(2,1)S(1)} collective-permute-done((bf16[512,640]{1,0:T(8,128)(2,1)S(1)}, bf16[512,640]{1,0:T(8,128)(2,1)S(1)}, u32[]{:S(2)}, u32[]{:S(2)}) %collective-permute-start.2) | collective-permute-done | bytes 655392 | tf_op jit(solution)/shard_map/ppermute | solution.py:390
  57.9 66.1 %attention.1 = bf16[2,640,640]{2,1,0:T(8,128)(2,1)} custom-call(s32[1]{0:T(128)S(6)} %select_n.20.pick_ref, bf16[512,640]{1,0:T(8,128)(2,1)S(1)} %bitcast.6, bf16[512,640]{1,0:T(8,128)(2,1)S(1)} %collective-permute-done.2.far_ref, bf16[640,640]{1,0:T(8,128)(2,1)} %w_key_hbm.1, bf16[640,640]{1,0:T(8,128)(2,1)} %w_value_hbm.1, bf16[640,640]{1,0:T(8,128)(2,1)} %w_out_hbm.1, ...), custom_call_target="tpu_custom_call" | custom-call | flops 20000000000 | bytes 10000000 | tf_op jit(solution)/shard_map/attention/pallas_call | solution.py:281
  (16 shorter events, 0.1 us)
Async XLA Ops:
  0.0 14.8 %copy-start = (f32[640,640]{1,0:T(8,128)S(1)}, f32[640,640]{1,0:T(8,128)}, u32[]{:S(2)}) copy-start(f32[640,640]{1,0:T(8,128)} %param.17) | copy-start | bytes 4915204
  0.0 14.6 %copy-start.10 = (f32[640]{0:T(1024)S(1)}, f32[640]{0:T(1024)}, u32[]{:S(2)}) copy-start(f32[640]{0:T(1024)} %param.15) | copy-start | bytes 7684
  0.0 14.6 %copy-start.11 = (f32[640]{0:T(1024)S(1)}, f32[640]{0:T(1024)}, u32[]{:S(2)}) copy-start(f32[640]{0:T(1024)} %param.18) | copy-start | bytes 7684
  0.0 15.7 %copy-start.1 = (bf16[3,640,640]{2,1,0:T(8,128)(2,1)S(1)}, bf16[3,640,640]{2,1,0:T(8,128)(2,1)}, u32[]{:S(2)}) copy-start(bf16[3,640,640]{2,1,0:T(8,128)(2,1)} %taps_hbm.3) | copy-start | bytes 7372804
  1.7 14.0 %copy-start.4 = (bf16[2,640,640]{2,1,0:T(8,128)(2,1)S(1)}, bf16[2,640,640]{2,1,0:T(8,128)(2,1)}, u32[]{:S(2)}) copy-start(bf16[2,640,640]{2,1,0:T(8,128)(2,1)} %latents_ref.1) | copy-start | bytes 4915204
  1.7 19.3 %collective-permute-start.1 = (bf16[1,640,640]{2,1,0:T(8,128)(2,1)S(1)}, bf16[1,640,640]{2,1,0:T(8,128)(2,1)S(1)}, u32[]{:S(2)}, u32[]{:S(2)}) collective-permute-start(bf16[1,640,640]{2,1,0:T(8,128)(2,1)S(1)} %get-tuple-element.31), channel_id=1, source_target_pairs={{0,255},{1,2},{2,1},{3,4},{4,3},{5,6},{6,5},{7,8},{8,7},{9,10},{10... | collective-permute-start | bytes 2457608 | tf_op jit(solution)/shard_map/ppermute | solution.py:322
  4.8 16.2 %collective-permute-start = (bf16[1,640,640]{2,1,0:T(8,128)(2,1)S(1)}, bf16[1,640,640]{2,1,0:T(8,128)(2,1)S(1)}, u32[]{:S(2)}, u32[]{:S(2)}) collective-permute-start(bf16[1,640,640]{2,1,0:T(8,128)(2,1)S(1)} %get-tuple-element.32), channel_id=1, source_target_pairs={{0,1},{1,0},{2,3},{3,2},{4,5},{5,4},{6,7},{7,6},{8,9},{9,8},{10,11... | collective-permute-start | bytes 2457608 | tf_op jit(solution)/shard_map/ppermute | solution.py:323
  14.6 6.5 %copy-start.8 = (f32[1,640]{1,0:T(1,128)}, f32[1,640]{1,0:T(1,128)S(1)}, u32[]{:S(2)}) copy-start(f32[1,640]{1,0:T(1,128)S(1)} %reshape.21.gain_ref.gain_pre_ref) | copy-start | bytes 7684
  14.6 6.4 %copy-start.9 = (f32[1,640]{1,0:T(1,128)}, f32[1,640]{1,0:T(1,128)S(1)}, u32[]{:S(2)}) copy-start(f32[1,640]{1,0:T(1,128)S(1)} %reshape.22.gain_mid_ref) | copy-start | bytes 7684
  15.7 5.4 %copy-start.7 = (f32[40,1280]{1,0:T(8,128)S(1)}, f32[40,1280]{1,0:T(8,128)}, u32[]{:S(2)}) copy-start(f32[40,1280]{1,0:T(8,128)} %constant.36.clone.side_ref) | copy-start | bytes 614404
  18.7 1.2 copy-start.5
  19.9 1.2 copy-start.6
  21.0 2.5 %copy-start.2 = (bf16[1,640,640]{2,1,0:T(8,128)(2,1)}, bf16[1,640,640]{2,1,0:T(8,128)(2,1)S(1)}, u32[]{:S(2)}) copy-start(bf16[1,640,640]{2,1,0:T(8,128)(2,1)S(1)} %collective-permute-done.1.beyond_ref.beyond_hbm) | copy-start | bytes 2457604
  21.0 2.5 %copy-start.3 = (bf16[1,640,640]{2,1,0:T(8,128)(2,1)}, bf16[1,640,640]{2,1,0:T(8,128)(2,1)S(1)}, u32[]{:S(2)}) copy-start(bf16[1,640,640]{2,1,0:T(8,128)(2,1)S(1)} %collective-permute-done.beside_ref.beside_hbm) | copy-start | bytes 2457604
  23.5 10.9 %all-to-all-start = ((bf16[8,4,640]{2,1,0:T(4,128)(2,1)}), bf16[8,4,640]{2,1,0:T(4,128)(2,1)S(1)}, u32[]{:S(2)}, u32[]{:S(2)}) async-start(bf16[8,4,640]{2,1,0:T(4,128)(2,1)} %context_rows.1), calls=%async_computation | async-start | bytes 81920 | tf_op jit(solution)/shard_map/all_to_all | solution.py:48
  35.3 19.6 %all-to-all-start.1 = ((bf16[16,32,640]{2,1,0:T(8,128)(2,1)}), bf16[16,32,640]{2,1,0:T(8,128)(2,1)S(1)}, u32[]{:S(2)}, u32[]{:S(2)}) async-start(bf16[16,32,640]{2,1,0:T(8,128)(2,1)} %broadcast_in_dim.8), calls=%async_computation.1 | async-start | bytes 1310720 | tf_op jit(solution)/shard_map/all_to_all | solution.py:48
  54.9 3.1 %collective-permute-start.2 = (bf16[512,640]{1,0:T(8,128)(2,1)S(1)}, bf16[512,640]{1,0:T(8,128)(2,1)S(1)}, u32[]{:S(2)}, u32[]{:S(2)}) collective-permute-start(bf16[512,640]{1,0:T(8,128)(2,1)S(1)} %bitcast.5), channel_id=1, source_target_pairs={{0,1},{1,0},{2,3},{3,2},{4,5},{5,4},{6,7},{7,6},{8,9},{9,8},{10,11... | collective-permute-start | bytes 1966088 | tf_op jit(solution)/shard_map/ppermute | solution.py:390

commit v7 on v6

--- a/solution.py
+++ b/solution.py
@@ -350,7 +350,7 @@
     ctx = call(
         context_rows,
         "context_rows",
-        jax.ShapeDtypeStruct((8, 4, C), half),
+        jax.ShapeDtypeStruct((32, 4, C), half),
         [scalar, scalar, here, here, here, here, here, here, here],
         here,
         mac,
@@ -379,12 +379,11 @@
             ],
         )(pick, apart, gain_pre, gain_mid, beside, beyond, frame_part, w_temporal, w_query)
 
-    line = exchange(ctx, groups_by(lambda x, y, z, core: (x, y, core))).reshape(32, C)
+    line = exchange(ctx, groups_by(lambda x, y, z, core: (x % 2, y % 2, core))).reshape(128, C)
     hidden_0, query_0 = frame_call(0, part)
     line, hidden_0, query_0 = lax.optimization_barrier((line, hidden_0, query_0))
-    plane = exchange(
-        jnp.broadcast_to(line[None], (16, 32, C)), groups_by(lambda x, y, z, core: (z, core))
-    ).reshape(512, C)
+    near = groups_by(lambda x, y, z, core: ((x + core) % 4 // 2, (y + core) % 4 // 2, z, core))
+    plane = exchange(jnp.broadcast_to(line[None], (4, 128, C)), near).reshape(512, C)
     hidden_1, query_1 = frame_call(1, other_part)
     plane, hidden_1, query_1 = lax.optimization_barrier((plane, hidden_1, query_1))
     swapped = lax.ppermute(plane, AXES, [(i, i ^ 1) for i in range(256)])

time: 125 us -> 127 us (1.016)
  waiting for transfers between devices: 8.05 us -> 9.61 us
    all_to_all x2, starting transfers between devices: 11.8 us -> 13.7 us  [exchange(): lax.all_to_all(copies, AXES, 0, 0, axis_index_groups=groups, tiled=False)]
    ppermute x1, starting transfers between devices: 1.33 us -> 0.01 us  [shards(): swapped = lax.ppermute(plane, AXES, [(i, i ^ 1) for i in range(256)])]
where the time goes in v7:
time: 127 us; the launch traced here: 126 us
  Pallas kernels  83.8 us (66%)
  starting transfers between devices  25.2 us (20%)
  waiting for transfers between devices  9.61 us (8%)
  local copies, waits for them, and re-layouts  5.04 us (4%)
  between operations  1.68 us (1%)
    pallas_call x1, Pallas kernels, attend(): call(attention, 'attention', jax.ShapeDtypeStruct(pair, half), [pl.BlockS...  66.1 us
    all_to_all x2, starting transfers between devices, exchange(): lax.all_to_all(copies, AXES, 0, 0, axis_index_groups=groups, tiled=False)  13.7 us
    pallas_call x2, Pallas kernels, frame_call(): call(functools.partial(hidden_queries, slot), 'hidden_queries', (jax.Shap...  12.3 us
    ppermute x1, starting transfers between devices, shards(): lax.ppermute(lax.dynamic_slice_in_dim(latents, 1 - core, 1, 0), AXES, [(i...  8.42 us
    all_to_all x2, waiting for transfers between devices, exchange(): lax.all_to_all(copies, AXES, 0, 0, axis_index_groups=groups, tiled=False)  7.51 us
    ppermute x1, starting transfers between devices, shards(): lax.ppermute(lax.dynamic_slice_in_dim(latents, core, 1, 0), AXES, abroad)  3.11 us
    pallas_call x1, Pallas kernels, shards(): call(own_taps, 'own_taps', (jax.ShapeDtypeStruct(frame, single),) * 3, [s...  2.95 us
  transfers between devices with their start and end apart: 5, of which 3 were waited for; matrix products, arithmetic and copies ran while one was open for 1% of the time, Pallas kernels for 12%

profile of v7, /device:TPU:1, one launch (start us, length us, event | category | flops | bytes accessed | tf_op | source)
XLA Modules:
  0.0 126.4 jit_solution(4134487289588368048)
XLA Ops:
  0.0 0.0 copy-start
  0.0 0.0 copy-start.1
  0.0 1.7 %constant_dynamic-slice_fusion = (bf16[1,640,640]{2,1,0:T(8,128)(2,1)S(1)}, bf16[1,640,640]{2,1,0:T(8,128)(2,1)S(1)}) fusion(bf16[2,640,640]{2,1,0:T(8,128)(2,1)} %latents_ref.1, s32[]{:T(128)S(6)} %select_n.24, s32[]{:T(128)S(6)} %select_n.23), kind=kLoop, calls=%fused_computation.5 | loop fusion | bytes 3276808 | tf_op jit(solution)/shard_map/dynamic_slice | solution.py:322
  1.7 0.0 copy-start.4
  1.7 3.1 %collective-permute-start.1 = (bf16[1,640,640]{2,1,0:T(8,128)(2,1)S(1)}, bf16[1,640,640]{2,1,0:T(8,128)(2,1)S(1)}, u32[]{:S(2)}, u32[]{:S(2)}) collective-permute-start(bf16[1,640,640]{2,1,0:T(8,128)(2,1)S(1)} %get-tuple-element.31), channel_id=1, source_target_pairs={{0,255},{1,2},{2,1},{3,4},{4,3},{5,6},{6,5},{7,8},{8,7},{9,10},{10... | collective-permute-start | bytes 2457608 | tf_op jit(solution)/shard_map/ppermute | solution.py:322
  4.8 8.4 %collective-permute-start = (bf16[1,640,640]{2,1,0:T(8,128)(2,1)S(1)}, bf16[1,640,640]{2,1,0:T(8,128)(2,1)S(1)}, u32[]{:S(2)}, u32[]{:S(2)}) collective-permute-start(bf16[1,640,640]{2,1,0:T(8,128)(2,1)S(1)} %get-tuple-element.32), channel_id=1, source_target_pairs={{0,1},{1,0},{2,3},{3,2},{4,5},{5,4},{6,7},{7,6},{8,9},{9,8},{10,11... | collective-permute-start | bytes 2457608 | tf_op jit(solution)/shard_map/ppermute | solution.py:323
  14.6 0.0 copy-done.10
  14.6 0.0 copy-done.11
  14.6 0.0 copy-start.8
  14.6 0.0 copy-start.9
  14.6 0.1 fusion
  14.7 0.1 divide_multiply_fusion
  14.8 0.0 copy-done
  14.8 0.9 fusion.2.temb_ref
  15.7 0.0 copy-done.1
  15.7 0.0 copy-start.7
  15.7 3.0 %own_taps.1 = (f32[640,640]{1,0:T(8,128)S(1)}, f32[640,640]{1,0:T(8,128)S(1)}, f32[640,640]{1,0:T(8,128)S(1)}) custom-call(s32[1]{0:T(128)S(6)} %select_n.20.pick_ref, bf16[2,640,640]{2,1,0:T(8,128)(2,1)S(1)} %copy-done.4, f32[1,640]{1,0:T(1,128)S(1)} %reshape.21.gain_ref.gain_pre_ref, f32[1,640]{1,0:T(1,128)S(1)} %fusion.2.temb_ref, ...), custom_call_target="tpu_custom_call" | custom-call | flops 2097152000 | bytes 8000000 | tf_op jit(solution)/shard_map/own_taps/pallas_call | solution.py:335
  18.7 1.2 copy-done.5
  19.9 1.2 copy-done.6
  21.0 0.0 collective-permute-done.1.beyond_ref.beyond_hbm
  21.0 0.0 collective-permute-done.beside_ref.beside_hbm
  21.1 2.5 %context_rows.1 = bf16[32,4,640]{2,1,0:T(4,128)(2,1)} custom-call(s32[1]{0:T(128)S(6)} %select_n.20.pick_ref, s32[1]{0:T(128)S(6)} %select_n.22.apart_ref, bf16[1,640,640]{2,1,0:T(8,128)(2,1)S(1)} %collective-permute-done.beside_ref.beside_hbm, bf16[1,640,640]{2,1,0:T(8,128)(2,1)S(1)} %collective-permute-done.1.beyond_ref.beyond_hbm, ...), custom_call_target="tpu_custom_call" | custom-call | flops 524288000 | bytes 8000000 | tf_op jit(solution)/shard_map/context_rows/pallas_call | solution.py:350
  23.6 10.2 %all-to-all-start = ((bf16[32,4,640]{2,1,0:T(4,128)(2,1)}), bf16[32,4,640]{2,1,0:T(4,128)(2,1)S(1)}, u32[]{:S(2)}, u32[]{:S(2)}) async-start(bf16[32,4,640]{2,1,0:T(4,128)(2,1)} %context_rows.1), calls=%async_computation | async-start | bytes 327680 | tf_op jit(solution)/shard_map/all_to_all | solution.py:48
  33.8 6.1 %hidden_queries.2 = (bf16[640,640]{1,0:T(8,128)(2,1)}, bf16[640,640]{1,0:T(8,128)(2,1)}) custom-call(s32[1]{0:T(128)S(6)} %select_n.20.pick_ref, s32[1]{0:T(128)S(6)} %select_n.22.apart_ref, f32[1,640]{1,0:T(1,128)} %copy-done.8, f32[1,640]{1,0:T(1,128)} %copy-done.9, bf16[1,640,640]{2,1,0:T(8,128)(2,1)} %copy-done.3, bf16[1,640,640]{2,1,0:T(8,128)(2,1)} %copy-done.2, ...), custom_call_target="tpu_custom_call" | custom-call | flops 1048576000 | bytes 6000000 | tf_op jit(solution)/shard_map/hidden_queries/pallas_call | solution.py:361
  39.9 6.0 %all-to-all-done = bf16[32,4,640]{2,1,0:T(4,128)(2,1)S(1)} async-done(((bf16[32,4,640]{2,1,0:T(4,128)(2,1)}), bf16[32,4,640]{2,1,0:T(4,128)(2,1)S(1)}, u32[]{:S(2)}, u32[]{:S(2)}) %all-to-all-start) | async-done | bytes 163872 | tf_op jit(solution)/shard_map/all_to_all | solution.py:48
  46.0 0.9 broadcast_in_dim.8
  46.9 3.5 %all-to-all-start.1 = ((bf16[4,128,640]{2,1,0:T(8,128)(2,1)}), bf16[4,128,640]{2,1,0:T(8,128)(2,1)S(1)}, u32[]{:S(2)}, u32[]{:S(2)}) async-start(bf16[4,128,640]{2,1,0:T(8,128)(2,1)} %broadcast_in_dim.8), calls=%async_computation.1 | async-start | bytes 1310720 | tf_op jit(solution)/shard_map/all_to_all | solution.py:48
  50.4 6.1 %hidden_queries.3 = (bf16[640,640]{1,0:T(8,128)(2,1)}, bf16[640,640]{1,0:T(8,128)(2,1)}) custom-call(s32[1]{0:T(128)S(6)} %select_n.20.pick_ref, s32[1]{0:T(128)S(6)} %select_n.22.apart_ref, f32[1,640]{1,0:T(1,128)} %copy-done.8, f32[1,640]{1,0:T(1,128)} %copy-done.9, bf16[1,640,640]{2,1,0:T(8,128)(2,1)} %copy-done.3, bf16[1,640,640]{2,1,0:T(8,128)(2,1)} %copy-done.2, ...), custom_call_target="tpu_custom_call" | custom-call | flops 1048576000 | bytes 6000000 | tf_op jit(solution)/shard_map/hidden_queries/pallas_call | solution.py:361
  56.5 1.5 %all-to-all-done.1 = bf16[4,128,640]{2,1,0:T(8,128)(2,1)S(1)} async-done(((bf16[4,128,640]{2,1,0:T(8,128)(2,1)}), bf16[4,128,640]{2,1,0:T(8,128)(2,1)S(1)}, u32[]{:S(2)}, u32[]{:S(2)}) %all-to-all-start.1) | async-done | bytes 655392 | tf_op jit(solution)/shard_map/all_to_all | solution.py:48
  58.0 0.0 collective-permute-start.2
  58.0 2.1 %collective-permute-done.2.far_ref = bf16[512,640]{1,0:T(8,128)(2,1)S(1)} collective-permute-done((bf16[512,640]{1,0:T(8,128)(2,1)S(1)}, bf16[512,640]{1,0:T(8,128)(2,1)S(1)}, u32[]{:S(2)}, u32[]{:S(2)}) %collective-permute-start.2) | collective-permute-done | bytes 655392 | tf_op jit(solution)/shard_map/ppermute | solution.py:389
  60.1 66.1 %attention.1 = bf16[2,640,640]{2,1,0:T(8,128)(2,1)} custom-call(s32[1]{0:T(128)S(6)} %select_n.20.pick_ref, bf16[512,640]{1,0:T(8,128)(2,1)S(1)} %bitcast.6, bf16[512,640]{1,0:T(8,128)(2,1)S(1)} %collective-permute-done.2.far_ref, bf16[640,640]{1,0:T(8,128)(2,1)} %w_key_hbm.1, bf16[640,640]{1,0:T(8,128)(2,1)} %w_value_hbm.1, bf16[640,640]{1,0:T(8,128)(2,1)} %w_out_hbm.1, ...), custom_call_target="tpu_custom_call" | custom-call | flops 20000000000 | bytes 10000000 | tf_op jit(solution)/shard_map/attention/pallas_call | solution.py:281
  (16 shorter events, 0.1 us)
Async XLA Ops:
  0.0 14.8 %copy-start = (f32[640,640]{1,0:T(8,128)S(1)}, f32[640,640]{1,0:T(8,128)}, u32[]{:S(2)}) copy-start(f32[640,640]{1,0:T(8,128)} %param.17) | copy-start | bytes 4915204
  0.0 14.6 %copy-start.10 = (f32[640]{0:T(1024)S(1)}, f32[640]{0:T(1024)}, u32[]{:S(2)}) copy-start(f32[640]{0:T(1024)} %param.15) | copy-start | bytes 7684
  0.0 14.6 %copy-start.11 = (f32[640]{0:T(1024)S(1)}, f32[640]{0:T(1024)}, u32[]{:S(2)}) copy-start(f32[640]{0:T(1024)} %param.18) | copy-start | bytes 7684
  0.0 15.7 %copy-start.1 = (bf16[3,640,640]{2,1,0:T(8,128)(2,1)S(1)}, bf16[3,640,640]{2,1,0:T(8,128)(2,1)}, u32[]{:S(2)}) copy-start(bf16[3,640,640]{2,1,0:T(8,128)(2,1)} %taps_hbm.3) | copy-start | bytes 7372804
  1.7 14.0 %copy-start.4 = (bf16[2,640,640]{2,1,0:T(8,128)(2,1)S(1)}, bf16[2,640,640]{2,1,0:T(8,128)(2,1)}, u32[]{:S(2)}) copy-start(bf16[2,640,640]{2,1,0:T(8,128)(2,1)} %latents_ref.1) | copy-start | bytes 4915204
  1.7 19.3 %collective-permute-start.1 = (bf16[1,640,640]{2,1,0:T(8,128)(2,1)S(1)}, bf16[1,640,640]{2,1,0:T(8,128)(2,1)S(1)}, u32[]{:S(2)}, u32[]{:S(2)}) collective-permute-start(bf16[1,640,640]{2,1,0:T(8,128)(2,1)S(1)} %get-tuple-element.31), channel_id=1, source_target_pairs={{0,255},{1,2},{2,1},{3,4},{4,3},{5,6},{6,5},{7,8},{8,7},{9,10},{10... | collective-permute-start | bytes 2457608 | tf_op jit(solution)/shard_map/ppermute | solution.py:322
  4.8 16.2 %collective-permute-start = (bf16[1,640,640]{2,1,0:T(8,128)(2,1)S(1)}, bf16[1,640,640]{2,1,0:T(8,128)(2,1)S(1)}, u32[]{:S(2)}, u32[]{:S(2)}) collective-permute-start(bf16[1,640,640]{2,1,0:T(8,128)(2,1)S(1)} %get-tuple-element.32), channel_id=1, source_target_pairs={{0,1},{1,0},{2,3},{3,2},{4,5},{5,4},{6,7},{7,6},{8,9},{9,8},{10,11... | collective-permute-start | bytes 2457608 | tf_op jit(solution)/shard_map/ppermute | solution.py:323
  14.6 6.5 %copy-start.8 = (f32[1,640]{1,0:T(1,128)}, f32[1,640]{1,0:T(1,128)S(1)}, u32[]{:S(2)}) copy-start(f32[1,640]{1,0:T(1,128)S(1)} %reshape.21.gain_ref.gain_pre_ref) | copy-start | bytes 7684
  14.6 6.4 %copy-start.9 = (f32[1,640]{1,0:T(1,128)}, f32[1,640]{1,0:T(1,128)S(1)}, u32[]{:S(2)}) copy-start(f32[1,640]{1,0:T(1,128)S(1)} %reshape.22.gain_mid_ref) | copy-start | bytes 7684
  15.7 5.4 %copy-start.7 = (f32[40,1280]{1,0:T(8,128)S(1)}, f32[40,1280]{1,0:T(8,128)}, u32[]{:S(2)}) copy-start(f32[40,1280]{1,0:T(8,128)} %constant.36.clone.side_ref) | copy-start | bytes 614404
  18.7 1.2 copy-start.5
  19.9 1.2 copy-start.6
  21.0 2.5 %copy-start.2 = (bf16[1,640,640]{2,1,0:T(8,128)(2,1)}, bf16[1,640,640]{2,1,0:T(8,128)(2,1)S(1)}, u32[]{:S(2)}) copy-start(bf16[1,640,640]{2,1,0:T(8,128)(2,1)S(1)} %collective-permute-done.1.beyond_ref.beyond_hbm) | copy-start | bytes 2457604
  21.0 2.5 %copy-start.3 = (bf16[1,640,640]{2,1,0:T(8,128)(2,1)}, bf16[1,640,640]{2,1,0:T(8,128)(2,1)S(1)}, u32[]{:S(2)}) copy-start(bf16[1,640,640]{2,1,0:T(8,128)(2,1)S(1)} %collective-permute-done.beside_ref.beside_hbm) | copy-start | bytes 2457604
  23.6 22.4 %all-to-all-start = ((bf16[32,4,640]{2,1,0:T(4,128)(2,1)}), bf16[32,4,640]{2,1,0:T(4,128)(2,1)S(1)}, u32[]{:S(2)}, u32[]{:S(2)}) async-start(bf16[32,4,640]{2,1,0:T(4,128)(2,1)} %context_rows.1), calls=%async_computation | async-start | bytes 327680 | tf_op jit(solution)/shard_map/all_to_all | solution.py:48
  46.9 11.2 %all-to-all-start.1 = ((bf16[4,128,640]{2,1,0:T(8,128)(2,1)}), bf16[4,128,640]{2,1,0:T(8,128)(2,1)S(1)}, u32[]{:S(2)}, u32[]{:S(2)}) async-start(bf16[4,128,640]{2,1,0:T(8,128)(2,1)} %broadcast_in_dim.8), calls=%async_computation.1 | async-start | bytes 1310720 | tf_op jit(solution)/shard_map/all_to_all | solution.py:48
  58.0 2.1 %collective-permute-start.2 = (bf16[512,640]{1,0:T(8,128)(2,1)S(1)}, bf16[512,640]{1,0:T(8,128)(2,1)S(1)}, u32[]{:S(2)}, u32[]{:S(2)}) collective-permute-start(bf16[512,640]{1,0:T(8,128)(2,1)S(1)} %bitcast.5), channel_id=1, source_target_pairs={{0,1},{1,0},{2,3},{3,2},{4,5},{5,4},{6,7},{7,6},{8,9},{9,8},{10,11... | collective-permute-start | bytes 1966088 | tf_op jit(solution)/shard_map/ppermute | solution.py:389

commit v8 on v6

--- a/solution.py
+++ b/solution.py
@@ -17,7 +17,6 @@
 PAIRS = C // (2 * HEAD_DIM)
 ROWS = 1024
 ONES = 16
-PARTS = (slice(0, 384), slice(384, PIX))
 STRIP = 320
 AXES = ("clip", "group")
 MIB = 2**20
@@ -146,36 +145,38 @@
 
 
 def hidden_queries(
-    slot, pick_ref, apart_ref, gain_pre_ref, gain_mid_ref, beside_hbm, beyond_hbm, part_hbm, taps_hbm,
-    w_query_hbm, hidden_hbm, query_hbm, halo_ref, part_ref, tap_ref, w_query_ref, hidden_ref, query_ref, sems,
-    out_sems,
+    pick_ref, apart_ref, gain_pre_ref, gain_mid_ref, beside_hbm, beyond_hbm, part_hbm, other_part_hbm,
+    taps_hbm, w_query_hbm, hidden_0, hidden_1, query_0, query_1, halo_ref, part_ref, tap_ref,
+    w_query_ref, hidden_ref, query_ref, sems, halo_sems, out_sems,
 ):
-    tap = jnp.where((pick_ref[0] == 0) == (slot == 0), 0, 2)
-    far = (apart_ref[0] == 1) == (slot == 0)
-    halo_copy = pltpu.make_async_copy(beyond_hbm.at[0], halo_ref, sems.at[3])
-    pl.when(far)(halo_copy.start)
-    pl.when(~far)(pltpu.make_async_copy(beside_hbm.at[0], halo_ref, sems.at[3]).start)
-    tap_copy, part_copy, query_copy = copy_all(
-        [
-            (taps_hbm.at[tap], tap_ref),
-            (part_hbm, part_ref),
-            (w_query_hbm, w_query_ref),
-        ],
-        sems,
-    )
+    loads = []
+    for slot, part in enumerate((part_hbm, other_part_hbm)):
+        far = (apart_ref[0] == 1) == (slot == 0)
+        tap = jnp.where((pick_ref[0] == 0) == (slot == 0), 0, 2)
+        place = halo_ref.at[slot]
+        halo_copy = pltpu.make_async_copy(beyond_hbm.at[0], place, halo_sems.at[slot])
+        pl.when(far)(halo_copy.start)
+        pl.when(~far)(pltpu.make_async_copy(beside_hbm.at[0], place, halo_sems.at[slot]).start)
+        pairs = [(taps_hbm.at[tap], tap_ref.at[slot]), (part, part_ref.at[slot])]
+        if slot == 0:
+            pairs.append((w_query_hbm, w_query_ref))
+        loads.append([halo_copy] + copy_all(pairs, sems.at[pl.ds(3 * slot, 3 - slot)]))
     gain_pre, gain_mid = gain_pre_ref[...], gain_mid_ref[...]
-    halo_copy.wait()
-    norm = normalize(halo_ref[...].astype(jnp.float32), gain_pre).astype(jnp.bfloat16)
-    tap_copy.wait()
-    part_copy.wait()
-    query_copy.wait()
-    for rows in PARTS:
-        hidden = (part_ref[rows] + dot(norm[rows], tap_ref[...])).astype(jnp.bfloat16)
-        hidden_ref[rows] = hidden
-        later = normalize(hidden.astype(jnp.float32), gain_mid).astype(jnp.bfloat16)
-        query_ref[:, rows] = (dot(later, w_query_ref[...]) * SCALE).T.astype(jnp.bfloat16)
-    for copy in copy_all([(hidden_ref, hidden_hbm), (query_ref, query_hbm)], out_sems):
-        copy.wait()
+    writes = []
+    for slot, (hidden_out, query_out) in enumerate(((hidden_0, query_0), (hidden_1, query_1))):
+        for load in loads[slot]:
+            load.wait()
+        norm = normalize(halo_ref[slot].astype(jnp.float32), gain_pre).astype(jnp.bfloat16)
+        hidden = (part_ref[slot] + dot(norm, tap_ref[slot])).astype(jnp.bfloat16)
+        hidden_ref[slot] = hidden
+        norm = normalize(hidden.astype(jnp.float32), gain_mid).astype(jnp.bfloat16)
+        query_ref[slot] = (dot(norm, w_query_ref[...]) * SCALE).T.astype(jnp.bfloat16)
+        writes += copy_all(
+            [(hidden_ref.at[slot], hidden_out), (query_ref.at[slot], query_out)],
+            out_sems.at[pl.ds(2 * slot, 2)],
+        )
+    for write in writes:
+        write.wait()
 
 
 def pair_rows(pair):
@@ -357,36 +358,35 @@
         8 * 10**6,
         CONTEXT_VMEM,
     )(pick, apart, beside, beyond, gain_pre, gain_mid, sides, soon_part, w_temporal)
-    def frame_call(slot, frame_part):
-        return call(
-            functools.partial(hidden_queries, slot),
-            "hidden_queries",
-            (jax.ShapeDtypeStruct(frame, half), jax.ShapeDtypeStruct(frame, half)),
-            [scalar, scalar, here, here, there, there, there, there, there],
-            (there, there),
-            2 * mac,
-            6 * 10**6,
-            HIDDEN_VMEM,
-            scratch_shapes=[
-                pltpu.VMEM(frame, half),
-                pltpu.VMEM(frame, single),
-                pltpu.VMEM(square, half),
-                pltpu.VMEM(square, half),
-                pltpu.VMEM(frame, half),
-                pltpu.VMEM(frame, half),
-                pltpu.SemaphoreType.DMA((4,)),
-                pltpu.SemaphoreType.DMA((2,)),
-            ],
-        )(pick, apart, gain_pre, gain_mid, beside, beyond, frame_part, w_temporal, w_query)
+    hidden_0, hidden_1, query_0, query_1 = call(
+        hidden_queries,
+        "hidden_queries",
+        (jax.ShapeDtypeStruct(frame, half),) * 4,
+        [scalar, scalar, here, here] + [there] * 6,
+        (there,) * 4,
+        4 * mac,
+        12 * 10**6,
+        HIDDEN_VMEM,
+        scratch_shapes=[
+            pltpu.VMEM(pair, half),
+            pltpu.VMEM(pair, single),
+            pltpu.VMEM(pair, half),
+            pltpu.VMEM(square, half),
+            pltpu.VMEM(pair, half),
+            pltpu.VMEM(pair, half),
+            pltpu.SemaphoreType.DMA((5,)),
+            pltpu.SemaphoreType.DMA((2,)),
+            pltpu.SemaphoreType.DMA((4,)),
+        ],
+    )(pick, apart, gain_pre, gain_mid, beside, beyond, part, other_part, w_temporal, w_query)
 
     line = exchange(ctx, groups_by(lambda x, y, z, core: (x, y, core))).reshape(32, C)
-    hidden_0, query_0 = frame_call(0, part)
-    line, hidden_0, query_0 = lax.optimization_barrier((line, hidden_0, query_0))
     plane = exchange(
         jnp.broadcast_to(line[None], (16, 32, C)), groups_by(lambda x, y, z, core: (z, core))
     ).reshape(512, C)
-    hidden_1, query_1 = frame_call(1, other_part)
-    plane, hidden_1, query_1 = lax.optimization_barrier((plane, hidden_1, query_1))
+    plane, hidden_0, hidden_1, query_0, query_1 = lax.optimization_barrier(
+        (plane, hidden_0, hidden_1, query_0, query_1)
+    )
     swapped = lax.ppermute(plane, AXES, [(i, i ^ 1) for i in range(256)])
 
     return attend(

time: 125 us -> 124 us (level)
  blocking collectives: 0 us -> 11.8 us
  Pallas kernels: 83.8 us -> 79.3 us
  starting transfers between devices: 24.7 us -> 21 us
  waiting for transfers between devices: 8.05 us -> 4.83 us
    all_to_all x0 -> x1, blocking collectives: none -> 11.8 us  [exchange(): lax.all_to_all(copies, AXES, 0, 0, axis_index_groups=groups, tiled=False)]
    pallas_call x2 -> x1, Pallas kernels: 12.3 us -> 8.43 us  [shards(): call(hidden_queries, 'hidden_queries', (jax.ShapeDtypeStruct(frame, half)...]
    all_to_all x2 -> x1, starting transfers between devices: 11.8 us -> 8.13 us  [exchange(): lax.all_to_all(copies, AXES, 0, 0, axis_index_groups=groups, tiled=False)]
    all_to_all x2 -> x1, waiting for transfers between devices: 6.32 us -> 3.1 us  [exchange(): lax.all_to_all(copies, AXES, 0, 0, axis_index_groups=groups, tiled=False)]
  transfers between devices with their start and end apart: 5 -> 4, of which waited for: 3 -> 2; matrix products, arithmetic and copies ran while one was open for 1% -> 1% of each run, Pallas kernels for 12% -> 9%
where the time goes in v8:
time: 124 us; the launch traced here: 123 us
  Pallas kernels  79.3 us (64%)
  starting transfers between devices  21 us (17%)
  blocking collectives  11.8 us (10%)
  waiting for transfers between devices  4.83 us (4%)
  local copies, waits for them, and re-layouts  3.83 us (3%)
  between operations  1.69 us (1%)
    pallas_call x1, Pallas kernels, attend(): call(attention, 'attention', jax.ShapeDtypeStruct(pair, half), [pl.BlockS...  66.1 us
    all_to_all x1, blocking collectives, exchange(): lax.all_to_all(copies, AXES, 0, 0, axis_index_groups=groups, tiled=False)  11.8 us
    pallas_call x1, Pallas kernels, shards(): call(hidden_queries, 'hidden_queries', (jax.ShapeDtypeStruct(frame, half)...  8.43 us
    ppermute x1, starting transfers between devices, shards(): lax.ppermute(lax.dynamic_slice_in_dim(latents, 1 - core, 1, 0), AXES, [(i...  8.42 us
    all_to_all x1, starting transfers between devices, exchange(): lax.all_to_all(copies, AXES, 0, 0, axis_index_groups=groups, tiled=False)  8.13 us
    ppermute x1, starting transfers between devices, shards(): lax.ppermute(lax.dynamic_slice_in_dim(latents, core, 1, 0), AXES, abroad)  3.11 us
    all_to_all x1, waiting for transfers between devices, exchange(): lax.all_to_all(copies, AXES, 0, 0, axis_index_groups=groups, tiled=False)  3.1 us
    pallas_call x1, Pallas kernels, shards(): call(own_taps, 'own_taps', (jax.ShapeDtypeStruct(frame, single),) * 3, [s...  2.95 us
  transfers between devices with their start and end apart: 4, of which 2 were waited for; matrix products, arithmetic and copies ran while one was open for 1% of the time, Pallas kernels for 9%

profile of v8, /device:TPU:1, one launch (start us, length us, event | category | flops | bytes accessed | tf_op | source)
XLA Modules:
  0.0 123.5 jit_solution(4471957754789400630)
XLA Ops:
  0.0 0.0 copy-start
  0.0 0.0 copy-start.1
  0.0 1.7 %constant_dynamic-slice_fusion = (bf16[1,640,640]{2,1,0:T(8,128)(2,1)S(1)}, bf16[1,640,640]{2,1,0:T(8,128)(2,1)S(1)}) fusion(bf16[2,640,640]{2,1,0:T(8,128)(2,1)} %latents_ref.1, s32[]{:T(128)S(6)} %select_n.24, s32[]{:T(128)S(6)} %select_n.23), kind=kLoop, calls=%fused_computation.5 | loop fusion | bytes 3276808 | tf_op jit(solution)/shard_map/dynamic_slice | solution.py:323
  1.7 0.0 copy-start.4
  1.7 3.1 %collective-permute-start.1 = (bf16[1,640,640]{2,1,0:T(8,128)(2,1)S(1)}, bf16[1,640,640]{2,1,0:T(8,128)(2,1)S(1)}, u32[]{:S(2)}, u32[]{:S(2)}) collective-permute-start(bf16[1,640,640]{2,1,0:T(8,128)(2,1)S(1)} %get-tuple-element.29), channel_id=1, source_target_pairs={{0,255},{1,2},{2,1},{3,4},{4,3},{5,6},{6,5},{7,8},{8,7},{9,10},{10... | collective-permute-start | bytes 2457608 | tf_op jit(solution)/shard_map/ppermute | solution.py:323
  4.8 8.4 %collective-permute-start = (bf16[1,640,640]{2,1,0:T(8,128)(2,1)S(1)}, bf16[1,640,640]{2,1,0:T(8,128)(2,1)S(1)}, u32[]{:S(2)}, u32[]{:S(2)}) collective-permute-start(bf16[1,640,640]{2,1,0:T(8,128)(2,1)S(1)} %get-tuple-element.30), channel_id=1, source_target_pairs={{0,1},{1,0},{2,3},{3,2},{4,5},{5,4},{6,7},{7,6},{8,9},{9,8},{10,11... | collective-permute-start | bytes 2457608 | tf_op jit(solution)/shard_map/ppermute | solution.py:324
  14.6 0.0 copy-done.10
  14.6 0.0 copy-done.11
  14.6 0.0 copy-start.8
  14.6 0.0 copy-start.9
  14.6 0.1 fusion
  14.7 0.1 divide_multiply_fusion
  14.8 0.9 fusion.2.temb_ref
  15.7 0.0 copy-start.7
  15.7 3.0 %own_taps.1 = (f32[640,640]{1,0:T(8,128)S(1)}, f32[640,640]{1,0:T(8,128)S(1)}, f32[640,640]{1,0:T(8,128)S(1)}) custom-call(s32[1]{0:T(128)S(6)} %select_n.20.pick_ref, bf16[2,640,640]{2,1,0:T(8,128)(2,1)S(1)} %copy-done.4, f32[1,640]{1,0:T(1,128)S(1)} %reshape.18.gain_ref.gain_pre_ref, f32[1,640]{1,0:T(1,128)S(1)} %fusion.2.temb_ref, ...), custom_call_target="tpu_custom_call" | custom-call | flops 2097152000 | bytes 8000000 | tf_op jit(solution)/shard_map/own_taps/pallas_call | solution.py:336
  18.7 0.0 copy-start.5
  18.7 1.2 copy-done.5
  19.8 0.0 collective-permute-done.1.beyond_ref.beyond_hbm
  19.8 0.0 collective-permute-done.beside_ref.beside_hbm
  19.9 0.0 copy-start.3
  19.9 0.0 copy-done.8
  19.9 0.0 copy-done.9
  19.9 0.0 copy-done.7
  19.9 1.8 %context_rows.1 = bf16[8,4,640]{2,1,0:T(4,128)(2,1)S(1)} custom-call(s32[1]{0:T(128)S(6)} %select_n.20.pick_ref, s32[1]{0:T(128)S(6)} %select_n.22.apart_ref, bf16[1,640,640]{2,1,0:T(8,128)(2,1)S(1)} %collective-permute-done.beside_ref.beside_hbm, bf16[1,640,640]{2,1,0:T(8,128)(2,1)S(1)} %collective-permute-done.1.beyond_ref.beyond_hbm, ...), custom_call_target="tpu_custom_call" | custom-call | flops 524288000 | bytes 8000000 | tf_op jit(solution)/shard_map/context_rows/pallas_call | solution.py:351
  21.7 11.8 %all_to_all.10 = bf16[8,4,640]{2,1,0:T(4,128)(2,1)S(1)} all-to-all(bf16[8,4,640]{2,1,0:T(4,128)(2,1)S(1)} %context_rows.1), channel_id=1, replica_groups={{0,2,4,6,8,10,12,14},{1,3,5,7,9,11,13,15},{16,18,20,22,24,26,28,30},{17..., dimensions={0} | all-to-all | bytes 81920 | tf_op jit(solution)/shard_map/all_to_all | solution.py:47
  33.5 0.9 broadcast_in_dim.15
  34.4 8.1 %all-to-all-start.1 = ((bf16[16,32,640]{2,1,0:T(8,128)(2,1)}), bf16[16,32,640]{2,1,0:T(8,128)(2,1)S(1)}, u32[]{:S(2)}, u32[]{:S(2)}) async-start(bf16[16,32,640]{2,1,0:T(8,128)(2,1)} %broadcast_in_dim.15), calls=%async_computation.1 | async-start | bytes 1310720 | tf_op jit(solution)/shard_map/all_to_all | solution.py:47
  42.6 8.4 %hidden_queries.1 = (bf16[640,640]{1,0:T(8,128)(2,1)}, bf16[640,640]{1,0:T(8,128)(2,1)}, bf16[640,640]{1,0:T(8,128)(2,1)}, bf16[640,640]{1,0:T(8,128)(2,1)}) custom-call(s32[1]{0:T(128)S(6)} %select_n.20.pick_ref, s32[1]{0:T(128)S(6)} %select_n.22.apart_ref, f32[1,640]{1,0:T(1,128)} %copy-done.8, f32[1,640]{1,0:T(1,128)} %copy-done.9, ...), custom_call_target="tpu_custom_call" | custom-call | flops 2097152000 | bytes 12000000 | tf_op jit(solution)/shard_map/hidden_queries/pallas_call | solution.py:361
  51.0 3.1 %all-to-all-done.1 = bf16[16,32,640]{2,1,0:T(8,128)(2,1)S(1)} async-done(((bf16[16,32,640]{2,1,0:T(8,128)(2,1)}), bf16[16,32,640]{2,1,0:T(8,128)(2,1)S(1)}, u32[]{:S(2)}, u32[]{:S(2)}) %all-to-all-start.1) | async-done | bytes 655392 | tf_op jit(solution)/shard_map/all_to_all | solution.py:47
  54.1 1.3 %collective-permute-start.2 = (bf16[512,640]{1,0:T(8,128)(2,1)S(1)}, bf16[512,640]{1,0:T(8,128)(2,1)S(1)}, u32[]{:S(2)}, u32[]{:S(2)}) collective-permute-start(bf16[512,640]{1,0:T(8,128)(2,1)S(1)} %bitcast.5), channel_id=1, source_target_pairs={{0,1},{1,0},{2,3},{3,2},{4,5},{5,4},{6,7},{7,6},{8,9},{9,8},{10,11... | collective-permute-start | bytes 1966088 | tf_op jit(solution)/shard_map/ppermute | solution.py:390
  55.4 1.7 %collective-permute-done.2.far_ref = bf16[512,640]{1,0:T(8,128)(2,1)S(1)} collective-permute-done((bf16[512,640]{1,0:T(8,128)(2,1)S(1)}, bf16[512,640]{1,0:T(8,128)(2,1)S(1)}, u32[]{:S(2)}, u32[]{:S(2)}) %collective-permute-start.2) | collective-permute-done | bytes 655392 | tf_op jit(solution)/shard_map/ppermute | solution.py:390
  57.2 66.1 %attention.1 = bf16[2,640,640]{2,1,0:T(8,128)(2,1)} custom-call(s32[1]{0:T(128)S(6)} %select_n.20.pick_ref, bf16[512,640]{1,0:T(8,128)(2,1)S(1)} %bitcast.6, bf16[512,640]{1,0:T(8,128)(2,1)S(1)} %collective-permute-done.2.far_ref, bf16[640,640]{1,0:T(8,128)(2,1)} %w_key_hbm.1, bf16[640,640]{1,0:T(8,128)(2,1)} %w_value_hbm.1, bf16[640,640]{1,0:T(8,128)(2,1)} %w_out_hbm.1, ...), custom_call_target="tpu_custom_call" | custom-call | flops 20000000000 | bytes 10000000 | tf_op jit(solution)/shard_map/attention/pallas_call | solution.py:282
  (14 shorter events, 0.0 us)
Async XLA Ops:
  0.0 14.8 %copy-start = (f32[640,640]{1,0:T(8,128)S(1)}, f32[640,640]{1,0:T(8,128)}, u32[]{:S(2)}) copy-start(f32[640,640]{1,0:T(8,128)} %param.17) | copy-start | bytes 4915204
  0.0 14.6 %copy-start.10 = (f32[640]{0:T(1024)S(1)}, f32[640]{0:T(1024)}, u32[]{:S(2)}) copy-start(f32[640]{0:T(1024)} %param.15) | copy-start | bytes 7684
  0.0 14.6 %copy-start.11 = (f32[640]{0:T(1024)S(1)}, f32[640]{0:T(1024)}, u32[]{:S(2)}) copy-start(f32[640]{0:T(1024)} %param.18) | copy-start | bytes 7684
  0.0 15.7 %copy-start.1 = (bf16[3,640,640]{2,1,0:T(8,128)(2,1)S(1)}, bf16[3,640,640]{2,1,0:T(8,128)(2,1)}, u32[]{:S(2)}) copy-start(bf16[3,640,640]{2,1,0:T(8,128)(2,1)} %taps_hbm.1) | copy-start | bytes 7372804
  1.7 14.0 %copy-start.4 = (bf16[2,640,640]{2,1,0:T(8,128)(2,1)S(1)}, bf16[2,640,640]{2,1,0:T(8,128)(2,1)}, u32[]{:S(2)}) copy-start(bf16[2,640,640]{2,1,0:T(8,128)(2,1)} %latents_ref.1) | copy-start | bytes 4915204
  1.7 18.1 %collective-permute-start.1 = (bf16[1,640,640]{2,1,0:T(8,128)(2,1)S(1)}, bf16[1,640,640]{2,1,0:T(8,128)(2,1)S(1)}, u32[]{:S(2)}, u32[]{:S(2)}) collective-permute-start(bf16[1,640,640]{2,1,0:T(8,128)(2,1)S(1)} %get-tuple-element.29), channel_id=1, source_target_pairs={{0,255},{1,2},{2,1},{3,4},{4,3},{5,6},{6,5},{7,8},{8,7},{9,10},{10... | collective-permute-start | bytes 2457608 | tf_op jit(solution)/shard_map/ppermute | solution.py:323
  4.8 15.0 %collective-permute-start = (bf16[1,640,640]{2,1,0:T(8,128)(2,1)S(1)}, bf16[1,640,640]{2,1,0:T(8,128)(2,1)S(1)}, u32[]{:S(2)}, u32[]{:S(2)}) collective-permute-start(bf16[1,640,640]{2,1,0:T(8,128)(2,1)S(1)} %get-tuple-element.30), channel_id=1, source_target_pairs={{0,1},{1,0},{2,3},{3,2},{4,5},{5,4},{6,7},{7,6},{8,9},{9,8},{10,11... | collective-permute-start | bytes 2457608 | tf_op jit(solution)/shard_map/ppermute | solution.py:324
  14.6 5.3 %copy-start.8 = (f32[1,640]{1,0:T(1,128)}, f32[1,640]{1,0:T(1,128)S(1)}, u32[]{:S(2)}) copy-start(f32[1,640]{1,0:T(1,128)S(1)} %reshape.18.gain_ref.gain_pre_ref) | copy-start | bytes 7684
  14.6 5.3 %copy-start.9 = (f32[1,640]{1,0:T(1,128)}, f32[1,640]{1,0:T(1,128)S(1)}, u32[]{:S(2)}) copy-start(f32[1,640]{1,0:T(1,128)S(1)} %reshape.19.gain_mid_ref) | copy-start | bytes 7684
  15.7 4.2 %copy-start.7 = (f32[40,1280]{1,0:T(8,128)S(1)}, f32[40,1280]{1,0:T(8,128)}, u32[]{:S(2)}) copy-start(f32[40,1280]{1,0:T(8,128)} %constant.36.clone.side_ref) | copy-start | bytes 614404
  18.7 1.2 copy-start.5
  19.8 1.9 %copy-start.6 = (f32[640,640]{1,0:T(8,128)}, f32[640,640]{1,0:T(8,128)S(1)}, u32[]{:S(2)}) copy-start(f32[640,640]{1,0:T(8,128)S(1)} %get-tuple-element.19.other_part_hbm) | copy-start | bytes 4915204
  19.8 1.9 %copy-start.2 = (bf16[1,640,640]{2,1,0:T(8,128)(2,1)}, bf16[1,640,640]{2,1,0:T(8,128)(2,1)S(1)}, u32[]{:S(2)}) copy-start(bf16[1,640,640]{2,1,0:T(8,128)(2,1)S(1)} %collective-permute-done.1.beyond_ref.beyond_hbm) | copy-start | bytes 2457604
  19.9 1.9 %copy-start.3 = (bf16[1,640,640]{2,1,0:T(8,128)(2,1)}, bf16[1,640,640]{2,1,0:T(8,128)(2,1)S(1)}, u32[]{:S(2)}) copy-start(bf16[1,640,640]{2,1,0:T(8,128)(2,1)S(1)} %collective-permute-done.beside_ref.beside_hbm) | copy-start | bytes 2457604
  34.4 19.7 %all-to-all-start.1 = ((bf16[16,32,640]{2,1,0:T(8,128)(2,1)}), bf16[16,32,640]{2,1,0:T(8,128)(2,1)S(1)}, u32[]{:S(2)}, u32[]{:S(2)}) async-start(bf16[16,32,640]{2,1,0:T(8,128)(2,1)} %broadcast_in_dim.15), calls=%async_computation.1 | async-start | bytes 1310720 | tf_op jit(solution)/shard_map/all_to_all | solution.py:47
  54.1 3.1 %collective-permute-start.2 = (bf16[512,640]{1,0:T(8,128)(2,1)S(1)}, bf16[512,640]{1,0:T(8,128)(2,1)S(1)}, u32[]{:S(2)}, u32[]{:S(2)}) collective-permute-start(bf16[512,640]{1,0:T(8,128)(2,1)S(1)} %bitcast.5), channel_id=1, source_target_pairs={{0,1},{1,0},{2,3},{3,2},{4,5},{5,4},{6,7},{7,6},{8,9},{9,8},{10,11... | collective-permute-start | bytes 1966088 | tf_op jit(solution)/shard_map/ppermute | solution.py:390

commit v9 on v8

--- a/solution.py
+++ b/solution.py
@@ -189,20 +189,16 @@
     out_ref, sems, out_sems,
 ):
     half = ROWS // 2
-    moves = copy_all(
+    weights_in = copy_all(
         [
             (source.at[:, pl.ds(128 * pair, 128)], w_both_ref.at[:, pl.ds(256 * pair + place, 128)])
             for pair in range(PAIRS)
             for source, place in ((w_key_hbm, 0), (w_value_hbm, 128))
-        ]
-        + [
-            (query_0, query_ref.at[0]),
-            (query_1, query_ref.at[1]),
-            (w_out_hbm, w_out_ref),
-            (hidden_0, hidden_ref.at[0]),
-            (hidden_1, hidden_ref.at[1]),
         ],
-        sems,
+        sems.at[pl.ds(0, 2 * PAIRS)],
+    )
+    queries_in = copy_all(
+        [(query_0, query_ref.at[0]), (query_1, query_ref.at[1])], sems.at[pl.ds(2 * PAIRS, 2)]
     )
 
     def context(pair, slot):
@@ -224,12 +220,21 @@
         place = jnp.where(pick_ref[0] == 0, frame, 1 - frame)
         return copy_all([(out_ref.at[frame], out_hbm.at[place])], out_sems.at[pl.ds(frame, 1)])
 
-    moves, late = moves[: 2 * PAIRS], moves[2 * PAIRS :]
     value_ref[:, :, HEAD_DIM:] = jnp.ones((2, 2, ONES, ROWS), jnp.bfloat16)
-    for move in moves + late[:2]:
+    for move in weights_in[:2]:
         move.wait()
+    context(0, 0)
+    for move in weights_in[2:] + queries_in:
+        move.wait()
+    late = copy_all(
+        [
+            (w_out_hbm, w_out_ref),
+            (hidden_0, hidden_ref.at[0]),
+            (hidden_1, hidden_ref.at[1]),
+        ],
+        sems.at[pl.ds(2 * PAIRS + 2, 3)],
+    )
     inside = None
-    context(0, 0)
     for pair in range(PAIRS):
         if pair + 1 < PAIRS:
             context(pair + 1, (pair + 1) % 2)
@@ -244,7 +249,7 @@
                 head = HEAD_DIM * (2 * pair + side)
                 mixed = total[:HEAD_DIM] * (1.0 / sums)
                 mixed_ref[frame, head : head + HEAD_DIM] = mixed.astype(jnp.bfloat16)
-    for move in late[2:]:
+    for move in late:
         move.wait()
     writes = project(0) + project(1)
     worst = jnp.min(inside)

time: 124 us -> 123 us (level)
  no operation moved by 1% of the time
where the time goes in v9:
time: 123 us
  Pallas kernels  78.9 us (64%)
  starting transfers between devices  21 us (17%)
  blocking collectives  11.8 us (10%)
  waiting for transfers between devices  4.81 us (4%)
  local copies, waits for them, and re-layouts  3.83 us (3%)
  between operations  1.69 us (1%)
    pallas_call x1, Pallas kernels, attend(): call(attention, 'attention', jax.ShapeDtypeStruct(pair, half), [pl.BlockS...  65.7 us
    all_to_all x1, blocking collectives, exchange(): lax.all_to_all(copies, AXES, 0, 0, axis_index_groups=groups, tiled=False)  11.8 us
    pallas_call x1, Pallas kernels, shards(): call(hidden_queries, 'hidden_queries', (jax.ShapeDtypeStruct(frame, half)...  8.45 us
    ppermute x1, starting transfers between devices, shards(): lax.ppermute(lax.dynamic_slice_in_dim(latents, 1 - core, 1, 0), AXES, [(i...  8.42 us
    all_to_all x1, starting transfers between devices, exchange(): lax.all_to_all(copies, AXES, 0, 0, axis_index_groups=groups, tiled=False)  8.13 us
    ppermute x1, starting transfers between devices, shards(): lax.ppermute(lax.dynamic_slice_in_dim(latents, core, 1, 0), AXES, abroad)  3.11 us
    all_to_all x1, waiting for transfers between devices, exchange(): lax.all_to_all(copies, AXES, 0, 0, axis_index_groups=groups, tiled=False)  3.08 us
    pallas_call x1, Pallas kernels, shards(): call(own_taps, 'own_taps', (jax.ShapeDtypeStruct(frame, single),) * 3, [s...  2.95 us
  transfers between devices with their start and end apart: 4, of which 2 were waited for; matrix products, arithmetic and copies ran while one was open for 1% of the time, Pallas kernels for 9%

profile of v9, /device:TPU:1, one launch (start us, length us, event | category | flops | bytes accessed | tf_op | source)
XLA Modules:
  0.0 123.0 jit_solution(16732739036823511627)
XLA Ops:
  0.0 0.0 copy-start
  0.0 0.0 copy-start.1
  0.0 1.7 %constant_dynamic-slice_fusion = (bf16[1,640,640]{2,1,0:T(8,128)(2,1)S(1)}, bf16[1,640,640]{2,1,0:T(8,128)(2,1)S(1)}) fusion(bf16[2,640,640]{2,1,0:T(8,128)(2,1)} %latents_ref.1, s32[]{:T(128)S(6)} %select_n.24, s32[]{:T(128)S(6)} %select_n.23), kind=kLoop, calls=%fused_computation.5 | loop fusion | bytes 3276808 | tf_op jit(solution)/shard_map/dynamic_slice | solution.py:328
  1.7 0.0 copy-start.4
  1.7 3.1 %collective-permute-start.1 = (bf16[1,640,640]{2,1,0:T(8,128)(2,1)S(1)}, bf16[1,640,640]{2,1,0:T(8,128)(2,1)S(1)}, u32[]{:S(2)}, u32[]{:S(2)}) collective-permute-start(bf16[1,640,640]{2,1,0:T(8,128)(2,1)S(1)} %get-tuple-element.29), channel_id=1, source_target_pairs={{0,255},{1,2},{2,1},{3,4},{4,3},{5,6},{6,5},{7,8},{8,7},{9,10},{10... | collective-permute-start | bytes 2457608 | tf_op jit(solution)/shard_map/ppermute | solution.py:328
  4.8 8.4 %collective-permute-start = (bf16[1,640,640]{2,1,0:T(8,128)(2,1)S(1)}, bf16[1,640,640]{2,1,0:T(8,128)(2,1)S(1)}, u32[]{:S(2)}, u32[]{:S(2)}) collective-permute-start(bf16[1,640,640]{2,1,0:T(8,128)(2,1)S(1)} %get-tuple-element.30), channel_id=1, source_target_pairs={{0,1},{1,0},{2,3},{3,2},{4,5},{5,4},{6,7},{7,6},{8,9},{9,8},{10,11... | collective-permute-start | bytes 2457608 | tf_op jit(solution)/shard_map/ppermute | solution.py:329
  14.6 0.0 copy-done.10
  14.6 0.0 copy-done.11
  14.6 0.0 copy-start.8
  14.6 0.0 copy-start.9
  14.6 0.1 fusion
  14.7 0.1 divide_multiply_fusion
  14.8 0.9 fusion.2.temb_ref
  15.7 0.0 copy-start.7
  15.7 3.0 %own_taps.1 = (f32[640,640]{1,0:T(8,128)S(1)}, f32[640,640]{1,0:T(8,128)S(1)}, f32[640,640]{1,0:T(8,128)S(1)}) custom-call(s32[1]{0:T(128)S(6)} %select_n.20.pick_ref, bf16[2,640,640]{2,1,0:T(8,128)(2,1)S(1)} %copy-done.4, f32[1,640]{1,0:T(1,128)S(1)} %reshape.18.gain_ref.gain_pre_ref, f32[1,640]{1,0:T(1,128)S(1)} %fusion.2.temb_ref, ...), custom_call_target="tpu_custom_call" | custom-call | flops 2097152000 | bytes 8000000 | tf_op jit(solution)/shard_map/own_taps/pallas_call | solution.py:341
  18.7 0.0 copy-start.5
  18.7 1.2 copy-done.5
  19.8 0.0 collective-permute-done.1.beyond_ref.beyond_hbm
  19.8 0.0 collective-permute-done.beside_ref.beside_hbm
  19.9 0.0 copy-start.3
  19.9 0.0 copy-done.8
  19.9 0.0 copy-done.9
  19.9 0.0 copy-done.7
  19.9 1.8 %context_rows.1 = bf16[8,4,640]{2,1,0:T(4,128)(2,1)S(1)} custom-call(s32[1]{0:T(128)S(6)} %select_n.20.pick_ref, s32[1]{0:T(128)S(6)} %select_n.22.apart_ref, bf16[1,640,640]{2,1,0:T(8,128)(2,1)S(1)} %collective-permute-done.beside_ref.beside_hbm, bf16[1,640,640]{2,1,0:T(8,128)(2,1)S(1)} %collective-permute-done.1.beyond_ref.beyond_hbm, ...), custom_call_target="tpu_custom_call" | custom-call | flops 524288000 | bytes 8000000 | tf_op jit(solution)/shard_map/context_rows/pallas_call | solution.py:356
  21.7 11.8 %all_to_all.10 = bf16[8,4,640]{2,1,0:T(4,128)(2,1)S(1)} all-to-all(bf16[8,4,640]{2,1,0:T(4,128)(2,1)S(1)} %context_rows.1), channel_id=1, replica_groups={{0,2,4,6,8,10,12,14},{1,3,5,7,9,11,13,15},{16,18,20,22,24,26,28,30},{17..., dimensions={0} | all-to-all | bytes 81920 | tf_op jit(solution)/shard_map/all_to_all | solution.py:47
  33.5 0.9 broadcast_in_dim.15
  34.4 8.1 %all-to-all-start.1 = ((bf16[16,32,640]{2,1,0:T(8,128)(2,1)}), bf16[16,32,640]{2,1,0:T(8,128)(2,1)S(1)}, u32[]{:S(2)}, u32[]{:S(2)}) async-start(bf16[16,32,640]{2,1,0:T(8,128)(2,1)} %broadcast_in_dim.15), calls=%async_computation.1 | async-start | bytes 1310720 | tf_op jit(solution)/shard_map/all_to_all | solution.py:47
  42.6 8.4 %hidden_queries.1 = (bf16[640,640]{1,0:T(8,128)(2,1)}, bf16[640,640]{1,0:T(8,128)(2,1)}, bf16[640,640]{1,0:T(8,128)(2,1)}, bf16[640,640]{1,0:T(8,128)(2,1)}) custom-call(s32[1]{0:T(128)S(6)} %select_n.20.pick_ref, s32[1]{0:T(128)S(6)} %select_n.22.apart_ref, f32[1,640]{1,0:T(1,128)} %copy-done.8, f32[1,640]{1,0:T(1,128)} %copy-done.9, ...), custom_call_target="tpu_custom_call" | custom-call | flops 2097152000 | bytes 12000000 | tf_op jit(solution)/shard_map/hidden_queries/pallas_call | solution.py:366
  51.0 3.1 %all-to-all-done.1 = bf16[16,32,640]{2,1,0:T(8,128)(2,1)S(1)} async-done(((bf16[16,32,640]{2,1,0:T(8,128)(2,1)}), bf16[16,32,640]{2,1,0:T(8,128)(2,1)S(1)}, u32[]{:S(2)}, u32[]{:S(2)}) %all-to-all-start.1) | async-done | bytes 655392 | tf_op jit(solution)/shard_map/all_to_all | solution.py:47
  54.1 1.3 %collective-permute-start.2 = (bf16[512,640]{1,0:T(8,128)(2,1)S(1)}, bf16[512,640]{1,0:T(8,128)(2,1)S(1)}, u32[]{:S(2)}, u32[]{:S(2)}) collective-permute-start(bf16[512,640]{1,0:T(8,128)(2,1)S(1)} %bitcast.5), channel_id=1, source_target_pairs={{0,1},{1,0},{2,3},{3,2},{4,5},{5,4},{6,7},{7,6},{8,9},{9,8},{10,11... | collective-permute-start | bytes 1966088 | tf_op jit(solution)/shard_map/ppermute | solution.py:395
  55.4 1.7 %collective-permute-done.2.far_ref = bf16[512,640]{1,0:T(8,128)(2,1)S(1)} collective-permute-done((bf16[512,640]{1,0:T(8,128)(2,1)S(1)}, bf16[512,640]{1,0:T(8,128)(2,1)S(1)}, u32[]{:S(2)}, u32[]{:S(2)}) %collective-permute-start.2) | collective-permute-done | bytes 655392 | tf_op jit(solution)/shard_map/ppermute | solution.py:395
  57.2 65.7 %attention.1 = bf16[2,640,640]{2,1,0:T(8,128)(2,1)} custom-call(s32[1]{0:T(128)S(6)} %select_n.20.pick_ref, bf16[512,640]{1,0:T(8,128)(2,1)S(1)} %bitcast.6, bf16[512,640]{1,0:T(8,128)(2,1)S(1)} %collective-permute-done.2.far_ref, bf16[640,640]{1,0:T(8,128)(2,1)} %w_key_hbm.1, bf16[640,640]{1,0:T(8,128)(2,1)} %w_value_hbm.1, bf16[640,640]{1,0:T(8,128)(2,1)} %w_out_hbm.1, ...), custom_call_target="tpu_custom_call" | custom-call | flops 20000000000 | bytes 10000000 | tf_op jit(solution)/shard_map/attention/pallas_call | solution.py:287
  (14 shorter events, 0.0 us)
Async XLA Ops:
  0.0 14.8 %copy-start = (f32[640,640]{1,0:T(8,128)S(1)}, f32[640,640]{1,0:T(8,128)}, u32[]{:S(2)}) copy-start(f32[640,640]{1,0:T(8,128)} %param.17) | copy-start | bytes 4915204
  0.0 14.6 %copy-start.10 = (f32[640]{0:T(1024)S(1)}, f32[640]{0:T(1024)}, u32[]{:S(2)}) copy-start(f32[640]{0:T(1024)} %param.15) | copy-start | bytes 7684
  0.0 14.6 %copy-start.11 = (f32[640]{0:T(1024)S(1)}, f32[640]{0:T(1024)}, u32[]{:S(2)}) copy-start(f32[640]{0:T(1024)} %param.18) | copy-start | bytes 7684
  0.0 15.7 %copy-start.1 = (bf16[3,640,640]{2,1,0:T(8,128)(2,1)S(1)}, bf16[3,640,640]{2,1,0:T(8,128)(2,1)}, u32[]{:S(2)}) copy-start(bf16[3,640,640]{2,1,0:T(8,128)(2,1)} %taps_hbm.1) | copy-start | bytes 7372804
  1.7 14.0 %copy-start.4 = (bf16[2,640,640]{2,1,0:T(8,128)(2,1)S(1)}, bf16[2,640,640]{2,1,0:T(8,128)(2,1)}, u32[]{:S(2)}) copy-start(bf16[2,640,640]{2,1,0:T(8,128)(2,1)} %latents_ref.1) | copy-start | bytes 4915204
  1.7 18.1 %collective-permute-start.1 = (bf16[1,640,640]{2,1,0:T(8,128)(2,1)S(1)}, bf16[1,640,640]{2,1,0:T(8,128)(2,1)S(1)}, u32[]{:S(2)}, u32[]{:S(2)}) collective-permute-start(bf16[1,640,640]{2,1,0:T(8,128)(2,1)S(1)} %get-tuple-element.29), channel_id=1, source_target_pairs={{0,255},{1,2},{2,1},{3,4},{4,3},{5,6},{6,5},{7,8},{8,7},{9,10},{10... | collective-permute-start | bytes 2457608 | tf_op jit(solution)/shard_map/ppermute | solution.py:328
  4.8 15.0 %collective-permute-start = (bf16[1,640,640]{2,1,0:T(8,128)(2,1)S(1)}, bf16[1,640,640]{2,1,0:T(8,128)(2,1)S(1)}, u32[]{:S(2)}, u32[]{:S(2)}) collective-permute-start(bf16[1,640,640]{2,1,0:T(8,128)(2,1)S(1)} %get-tuple-element.30), channel_id=1, source_target_pairs={{0,1},{1,0},{2,3},{3,2},{4,5},{5,4},{6,7},{7,6},{8,9},{9,8},{10,11... | collective-permute-start | bytes 2457608 | tf_op jit(solution)/shard_map/ppermute | solution.py:329
  14.6 5.3 %copy-start.8 = (f32[1,640]{1,0:T(1,128)}, f32[1,640]{1,0:T(1,128)S(1)}, u32[]{:S(2)}) copy-start(f32[1,640]{1,0:T(1,128)S(1)} %reshape.18.gain_ref.gain_pre_ref) | copy-start | bytes 7684
  14.6 5.3 %copy-start.9 = (f32[1,640]{1,0:T(1,128)}, f32[1,640]{1,0:T(1,128)S(1)}, u32[]{:S(2)}) copy-start(f32[1,640]{1,0:T(1,128)S(1)} %reshape.19.gain_mid_ref) | copy-start | bytes 7684
  15.7 4.2 %copy-start.7 = (f32[40,1280]{1,0:T(8,128)S(1)}, f32[40,1280]{1,0:T(8,128)}, u32[]{:S(2)}) copy-start(f32[40,1280]{1,0:T(8,128)} %constant.36.clone.side_ref) | copy-start | bytes 614404
  18.7 1.2 copy-start.5
  19.8 1.9 %copy-start.6 = (f32[640,640]{1,0:T(8,128)}, f32[640,640]{1,0:T(8,128)S(1)}, u32[]{:S(2)}) copy-start(f32[640,640]{1,0:T(8,128)S(1)} %get-tuple-element.19.other_part_hbm) | copy-start | bytes 4915204
  19.8 1.9 %copy-start.2 = (bf16[1,640,640]{2,1,0:T(8,128)(2,1)}, bf16[1,640,640]{2,1,0:T(8,128)(2,1)S(1)}, u32[]{:S(2)}) copy-start(bf16[1,640,640]{2,1,0:T(8,128)(2,1)S(1)} %collective-permute-done.1.beyond_ref.beyond_hbm) | copy-start | bytes 2457604
  19.9 1.9 %copy-start.3 = (bf16[1,640,640]{2,1,0:T(8,128)(2,1)}, bf16[1,640,640]{2,1,0:T(8,128)(2,1)S(1)}, u32[]{:S(2)}) copy-start(bf16[1,640,640]{2,1,0:T(8,128)(2,1)S(1)} %collective-permute-done.beside_ref.beside_hbm) | copy-start | bytes 2457604
  34.4 19.7 %all-to-all-start.1 = ((bf16[16,32,640]{2,1,0:T(8,128)(2,1)}), bf16[16,32,640]{2,1,0:T(8,128)(2,1)S(1)}, u32[]{:S(2)}, u32[]{:S(2)}) async-start(bf16[16,32,640]{2,1,0:T(8,128)(2,1)} %broadcast_in_dim.15), calls=%async_computation.1 | async-start | bytes 1310720 | tf_op jit(solution)/shard_map/all_to_all | solution.py:47
  54.1 3.1 %collective-permute-start.2 = (bf16[512,640]{1,0:T(8,128)(2,1)S(1)}, bf16[512,640]{1,0:T(8,128)(2,1)S(1)}, u32[]{:S(2)}, u32[]{:S(2)}) collective-permute-start(bf16[512,640]{1,0:T(8,128)(2,1)S(1)} %bitcast.5), channel_id=1, source_target_pairs={{0,1},{1,0},{2,3},{3,2},{4,5},{5,4},{6,7},{7,6},{8,9},{9,8},{10,11... | collective-permute-start | bytes 1966088 | tf_op jit(solution)/shard_map/ppermute | solution.py:395
